TPU v7x, 32 devices: a whole 2x2x4 slice. The times are simulated.
32 devices in a mesh: expert: 4 (over x, core), dp: 8 (over z, y).
Axes of the slice: x: 2, y: 2, z: 4, core: 2. Of those that a mesh axis runs over, the one named last changes fastest.
Arguments:
- tokens: bfloat16 [4096, 1664], P(('expert', 'dp')), may hold values from -6 to 6
- expert_ids: int32 [4096, 2], P(('expert', 'dp')), may hold values from 0 to 7, as said below
- slot_ids: int32 [4096, 2], P(('expert', 'dp')), may hold values from 0 to 3, as said below
- dropped: int32 [4096, 2], P(('expert', 'dp')), may hold values from 0 to 1, as said below
- gates: float32 [4096, 2], P(('expert', 'dp')), may hold values from 0.1 to 1
- w_in: bfloat16 [8, 1664, 8192], P('expert', None, 'dp'), may hold values from -0.15625 to 0.15625
- w_out: bfloat16 [8, 8192, 1664], P('expert', 'dp'), may hold values from -0.0625 to 0.0625
- out_grad: bfloat16 [4096, 1664], P(('expert', 'dp')), may hold values from -6 to 6
Outputs:
- mixed: bfloat16 [4096, 1664], P(('expert', 'dp'))
- tok_grad: bfloat16 [4096, 1664], P(('expert', 'dp'))
- gate_grad: float32 [4096, 2], P(('expert', 'dp'))
- w_in_grad: float32 [8, 1664, 8192], P('expert', None, 'dp')
- w_out_grad: float32 [8, 8192, 1664], P('expert', 'dp')
Inputs may be any that keep to these rules, and one draw needn't show every extreme that they name: `expert_ids`: the two experts of a token differ. `slot_ids`: choices are ranked in each block of 128 tokens by batch priority, all first choices before all second choices; a choice's slot is the number of higher-ranked choices of the same block to the same expert; it is dropped where that number is 4 or more, and its slot is then 0. Kept choices of one expert in one block have distinct slots. In every draw one expert is the first choice of at least 5 tokens of every block. `dropped`: 1 exactly where the slot count described for slot_ids reaches 4.
All inputs are finite; a program needn't handle non-finite values.
Results may differ from a plain program's by a relative error of at most 0.039.
Values may be sent and summed in bfloat16 or wider, within the bound.
No kernel may reach another device: no remote copies, remote signals or barrier semaphores. Data moves between devices by JAX's collectives and lax.ppermute only.
A program may use at most 128 MiB of HBM per device.

v0:
```python
import jax
import jax.numpy as jnp
from jax import lax
from jax.sharding import PartitionSpec as P

CAP = 4


inv_root_two = 0.7071067811865476
inv_root_two_pi = 0.3989422804014327


def gelu_exact(value):
    return 0.5 * value * (1.0 + lax.erf(value * inv_root_two))


def gelu_slope(value):
    return (
        0.5 * (1.0 + lax.erf(value * inv_root_two))
        + value * jnp.exp(-0.5 * value * value) * inv_root_two_pi
    )


def spread(buffer):
    grouped = lax.all_gather(buffer[None], "dp", axis=0, tiled=True)
    return lax.all_to_all(grouped, "expert", split_axis=1, concat_axis=1, tiled=True)


def collect(term_fn):
    summed = lax.psum_scatter(
        term_fn(jnp.int32(0), 1 * lax.axis_size("dp")).astype(jnp.bfloat16),
        "dp",
        scatter_dimension=0,
        tiled=True,
    ).astype(jnp.float32)
    return lax.all_to_all(
        summed[0].astype(jnp.bfloat16), "expert", split_axis=0, concat_axis=0, tiled=True
    )


def per_device(tokens, expert_ids, slot_ids, dropped, gates, w_in, w_out, out_grad):
    n_expert = lax.axis_size("expert")
    exp_local = w_in.shape[0]
    width = tokens.shape[1]
    experts_all = n_expert * exp_local
    capacity = CAP
    columns = experts_all * capacity
    target = expert_ids * capacity + slot_ids
    keep = dropped == 0
    column_ids = lax.broadcasted_iota(jnp.int32, (1, 1, columns), 2)
    select = ((target[:, :, None] == column_ids) & keep[:, :, None]).astype(jnp.float32)
    select_half = select.astype(jnp.bfloat16)
    shape_slots = (n_expert, exp_local, capacity, width)
    send_rows = jnp.einsum("tkj,td->jd", select_half, tokens, preferred_element_type=jnp.float32)
    rows = spread(send_rows.astype(jnp.bfloat16).reshape(shape_slots))
    pre = jnp.einsum("pqxcd,xdf->pqxcf", rows, w_in, preferred_element_type=jnp.float32)
    hidden = gelu_exact(pre).astype(jnp.bfloat16)

    def output_term(start, count):
        return jnp.einsum("pqxcf,xfd->pqxcd", hidden, w_out, preferred_element_type=jnp.float32)

    returned = collect(output_term).reshape(columns, width)
    picked = jnp.einsum("tkj,jd->tkd", select_half, returned, preferred_element_type=jnp.float32)
    mixed = jnp.sum(gates[:, :, None] * picked, axis=1).astype(jnp.bfloat16)
    grad_wide = out_grad.astype(jnp.float32)
    gate_grad = jnp.sum(picked * grad_wide[:, None, :], axis=-1)
    scaled = gates[:, :, None] * grad_wide[:, None, :]
    send_grads = jnp.einsum("tkj,tkd->jd", select, scaled, precision=lax.Precision.HIGHEST)
    grad_rows = spread(send_grads.astype(jnp.bfloat16).reshape(shape_slots))
    hidden_grad = jnp.einsum(
        "pqxcd,xfd->pqxcf", grad_rows, w_out, preferred_element_type=jnp.float32
    )
    pre_grad = (hidden_grad * gelu_slope(pre)).astype(jnp.bfloat16)
    w_out_grad = jnp.einsum(
        "pqxcf,pqxcd->xfd", hidden, grad_rows, preferred_element_type=jnp.float32
    )
    w_in_grad = jnp.einsum("pqxcd,pqxcf->xdf", rows, pre_grad, preferred_element_type=jnp.float32)

    def input_term(start, count):
        return jnp.einsum("pqxcf,xdf->pqxcd", pre_grad, w_in, preferred_element_type=jnp.float32)

    returned_grad = collect(input_term).reshape(columns, width)
    picked_grad = jnp.einsum(
        "tkj,jd->tkd", select_half, returned_grad, preferred_element_type=jnp.float32
    )
    tok_grad = jnp.sum(picked_grad, axis=1).astype(jnp.bfloat16)
    return (mixed, tok_grad, gate_grad, w_in_grad, w_out_grad)


def solution(mesh):
    placed = (
        P(("expert", "dp"), None),
        P(("expert", "dp"), None),
        P(("expert", "dp"), None),
        P(("expert", "dp"), None),
        P(("expert", "dp"), None),
        P("expert", None, "dp"),
        P("expert", "dp", None),
        P(("expert", "dp"), None),
    )
    return jax.shard_map(
        per_device,
        mesh=mesh,
        in_specs=placed,
        out_specs=(
            P(("expert", "dp"), None),
            P(("expert", "dp"), None),
            P(("expert", "dp"), None),
            P("expert", None, "dp"),
            P("expert", "dp", None),
        ),
        check_vma=False,
    )
```

profile of v0, /device:TPU:0, one launch (start us, length us, event | category | flops | bytes accessed | tf_op | source)
XLA Modules:
  0.0 232.3 jit_solution(17116658502392838650)
XLA Ops:
  7.2 0.0 copy-start
  7.2 0.0 copy-start.8
  7.2 0.7 broadcast_compare_fusion
  7.9 0.7 multiply_add_fusion
  8.6 0.0 copy-done
  8.6 0.2 fusion.53
  8.9 34.0 %all_gather.6 = bf16[8,4,2,4,1664]{4,3,2,1,0:T(4,128)(2,1)S(1)} all-gather(bf16[1,4,2,4,1664]{4,3,2,1,0:T(4,128)(2,1)S(1)} %broadcast_in_dim_reshape.6), channel_id=1, replica_groups=mesh['expert'=4,'dp'=8] {'dp'}, dimensions={0}, use_global_device_ids=true | all-gather | bytes 958464 | tf_op jit(solution)/shard_map/all_gather | solution.py:25
  42.8 1.2 copy.27
  44.0 3.5 %all-to-all-start = ((bf16[8,4,2,4,1664]{4,0,3,2,1:T(8,128)(2,1)}), bf16[8,4,2,4,1664]{4,0,3,2,1:T(8,128)(2,1)S(1)}, u32[]{:S(2)}, u32[]{:S(2)}) async-start(bf16[8,4,2,4,1664]{4,0,3,2,1:T(8,128)(2,1)} %copy.27), calls=%async_computation | async-start | bytes 1703936 | tf_op jit(solution)/shard_map/all_to_all | solution.py:26
  47.5 1.1 convert_element_type.61
  48.6 0.0 copy-start.5
  48.6 0.9 copy-done.5
  49.5 1.5 fusion.20
  51.0 31.9 %all_gather.7 = bf16[8,4,2,4,1664]{4,3,2,1,0:T(4,128)(2,1)S(1)} all-gather(bf16[1,4,2,4,1664]{4,3,2,1,0:T(4,128)(2,1)S(1)} %broadcast_in_dim_reshape.7), channel_id=1, replica_groups=mesh['expert'=4,'dp'=8] {'dp'}, dimensions={0}, use_global_device_ids=true | all-gather | bytes 958464 | tf_op jit(solution)/shard_map/all_gather | solution.py:25
  82.9 1.2 copy.30
  84.1 0.0 copy-done.8
  84.1 0.6 dynamic-slice
  84.7 0.0 all-to-all-done
  84.7 4.2 %all-to-all-start.2 = ((bf16[8,4,2,4,1664]{4,0,3,2,1:T(8,128)(2,1)}), bf16[8,4,2,4,1664]{4,0,3,2,1:T(8,128)(2,1)}, u32[]{:S(2)}, u32[]{:S(2)}) async-start(bf16[8,4,2,4,1664]{4,0,3,2,1:T(8,128)(2,1)} %copy.30), calls=%async_computation.2 | async-start | bytes 1703936 | tf_op jit(solution)/shard_map/all_to_all | solution.py:26
  88.9 0.2 all-reduce.5.cloned.1.call-start
  89.1 0.0 copy-done.1
  89.1 5.4 %multiply_convert_fusion = (bf16[8,4,2,4,1024]{4,0,3,1,2:T(8,128)(2,1)}, f32[8,4,2,4,1024]{4,0,3,1,2:T(8,128)}) fusion(bf16[2,1664,1024]{2,1,0:T(8,128)(2,1)} %param.13, bf16[8,4,2,4,1664]{4,0,3,2,1:T(8,128)(2,1)S(1)} %all-to-all-done), kind=kOutput, calls=%fused_computation.30 | convolution fusion | flops 873725952 | bytes 9240576 | tf_op jit(solution)/shard_map/pqxcd,xdf->pqxcf/dot_general | solution.py:56
  94.5 6.8 %all-to-all-done.2 = bf16[8,4,2,4,1664]{4,0,3,2,1:T(8,128)(2,1)} async-done(((bf16[8,4,2,4,1664]{4,0,3,2,1:T(8,128)(2,1)}), bf16[8,4,2,4,1664]{4,0,3,2,1:T(8,128)(2,1)}, u32[]{:S(2)}, u32[]{:S(2)}) %all-to-all-start.2) | async-done | bytes 852000 | tf_op jit(solution)/shard_map/all_to_all | solution.py:26
  101.3 5.9 %fusion.31 = bf16[8,4,2,4,1024]{4,0,3,1,2:T(8,128)(2,1)S(1)} fusion(bf16[2,1024,1664]{2,1,0:T(8,128)(2,1)} %param.14, f32[8,4,2,4,1024]{4,0,3,1,2:T(8,128)} %get-tuple-element.10, bf16[8,4,2,4,1664]{4,0,3,2,1:T(8,128)(2,1)} %all-to-all-done.2), kind=kOutput, calls=%fused_computation.25 | convolution fusion | flops 875036672 | bytes 9240576 | tf_op jit(solution)/shard_map/pqxcd,xfd->pqxcf/dot_general | solution.py:70
  107.2 0.0 slice-done
  107.3 0.0 copy-start.9
  107.3 0.0 slice-start.3
  107.3 2.3 fusion.14
  109.6 1.3 copy.32
  110.9 1.2 fusion.17
  112.1 1.2 copy.29
  113.3 0.0 all-reduce.5.cloned.1.call-update
  113.4 0.0 copy-done.4
  113.4 0.0 copy-start.2
  113.4 0.0 copy-start.10
  113.4 8.4 %convolution_bitcast_fusion = f32[2,1024,1664]{2,1,0:T(8,128)} fusion(bf16[8,4,2,4,1664]{4,0,3,2,1:T(8,128)(2,1)} %all-to-all-done.2, bf16[8,4,2,4,1024]{4,0,3,1,2:T(8,128)(2,1)S(1)} %copy-done.4), kind=kOutput, calls=%fused_computation.8 | convolution fusion | flops 872415232 | bytes 15007744 | tf_op jit(solution)/shard_map/pqxcf,pqxcd->xfd/dot_general | solution.py:74
  121.8 7.1 %convolution_bitcast_fusion.1 = f32[2,1664,1024]{2,1,0:T(8,128)} fusion(bf16[8,4,2,4,1664]{4,0,3,2,1:T(8,128)(2,1)S(1)} %copy-done.2, bf16[8,4,2,4,1024]{4,0,3,1,2:T(8,128)(2,1)S(1)} %copy-done.10), kind=kOutput, calls=%fused_computation.9 | convolution fusion | flops 872415232 | bytes 15007744 | tf_op jit(solution)/shard_map/pqxcd,pqxcf->xdf/dot_general | solution.py:77
  128.8 77.8 %all-reduce.5.cloned.1.call-done = (bf16[8,4,2,4,1664]{4,3,2,1,0:T(4,128)(2,1)}, bf16[8,4,2,4,1664]{4,3,2,1,0:T(4,128)(2,1)}) async-done(((bf16[8,4,2,4,1664]{4,3,2,1,0:T(4,128)(2,1)}, bf16[8,4,2,4,1664]{4,3,2,1,0:T(4,128)(2,1)}), (bf16[8,4,2,4,1664]{4,3,2,1,0:T(4,128)(2,1)}, bf16[8,4,2,4,1664]{4,3,2,1,0:T(4,128)(2,1)})) %all-reduce.5.cloned.1.call-update) | async-done | bytes 1703952
  206.7 2.2 dynamic-slice_bitcast_fusion.1
  208.9 3.3 %all-to-all-start.1 = ((bf16[4,2,4,1664]{3,2,1,0:T(4,128)(2,1)}), bf16[4,2,4,1664]{3,2,1,0:T(4,128)(2,1)S(1)}, u32[]{:S(2)}, u32[]{:S(2)}) async-start(bf16[4,2,4,1664]{3,2,1,0:T(4,128)(2,1)} %dynamic-slice_bitcast_fusion.1), calls=%async_computation.1 | async-start | bytes 212992 | tf_op jit(solution)/shard_map/all_to_all | solution.py:36
  212.2 2.2 dynamic-slice_bitcast_fusion
  214.4 2.1 all-to-all-done.1
  216.5 3.3 %all-to-all-start.3 = ((bf16[4,2,4,1664]{3,2,1,0:T(4,128)(2,1)}), bf16[4,2,4,1664]{3,2,1,0:T(4,128)(2,1)S(1)}, u32[]{:S(2)}, u32[]{:S(2)}) async-start(bf16[4,2,4,1664]{3,2,1,0:T(4,128)(2,1)} %dynamic-slice_bitcast_fusion), calls=%async_computation.3 | async-start | bytes 212992 | tf_op jit(solution)/shard_map/all_to_all | solution.py:36
  219.9 0.0 copy-done.6
  219.9 0.0 copy-done.7
  219.9 1.3 multiply_reduce_fusion
  221.2 3.0 %all-to-all-done.3 = bf16[4,2,4,1664]{3,2,1,0:T(4,128)(2,1)S(1)} async-done(((bf16[4,2,4,1664]{3,2,1,0:T(4,128)(2,1)}), bf16[4,2,4,1664]{3,2,1,0:T(4,128)(2,1)S(1)}, u32[]{:S(2)}, u32[]{:S(2)}) %all-to-all-start.3) | async-done | bytes 106528 | tf_op jit(solution)/shard_map/all_to_all | solution.py:36
  224.2 1.2 convolution_reduce_fusion
  (22 shorter events, 0.2 us)
Async XLA Ops:
  7.2 1.5 copy-start
  7.2 76.9 %copy-start.8 = (u32[32]{0:T(128)S(1)}, u32[32]{0:T(128)}, u32[]{:S(2)}) copy-start(u32[32]{0:T(128)} %constant.20) | copy-start | bytes 388
  44.0 40.7 %all-to-all-start = ((bf16[8,4,2,4,1664]{4,0,3,2,1:T(8,128)(2,1)}), bf16[8,4,2,4,1664]{4,0,3,2,1:T(8,128)(2,1)S(1)}, u32[]{:S(2)}, u32[]{:S(2)}) async-start(bf16[8,4,2,4,1664]{4,0,3,2,1:T(8,128)(2,1)} %copy.27), calls=%async_computation | async-start | bytes 1703936 | tf_op jit(solution)/shard_map/all_to_all | solution.py:26
  48.6 0.9 copy-start.5
  84.7 4.4 %copy-start.1 = (bf16[8,4,2,4,1664]{4,0,3,2,1:T(8,128)(2,1)}, bf16[8,4,2,4,1664]{4,0,3,2,1:T(8,128)(2,1)S(1)}, u32[]{:S(2)}) copy-start(bf16[8,4,2,4,1664]{4,0,3,2,1:T(8,128)(2,1)S(1)} %all-to-all-done) | copy-start | bytes 2555908
  84.7 16.6 %all-to-all-start.2 = ((bf16[8,4,2,4,1664]{4,0,3,2,1:T(8,128)(2,1)}), bf16[8,4,2,4,1664]{4,0,3,2,1:T(8,128)(2,1)}, u32[]{:S(2)}, u32[]{:S(2)}) async-start(bf16[8,4,2,4,1664]{4,0,3,2,1:T(8,128)(2,1)} %copy.30), calls=%async_computation.2 | async-start | bytes 1703936 | tf_op jit(solution)/shard_map/all_to_all | solution.py:26
  88.9 117.8 %all-reduce.5.cloned.1.call-start = ((), (), s32[]{:S(2)}) async-start(), calls=%async_computation.4 | async-start | bytes 3407872
  94.5 12.7 %slice-start = ((s8[6815744]{0:T(1024)(128)(4,1)}), s8[2621440]{0:T(1024)(128)(4,1)S(1)}, s32[]{:S(2)}) async-start(s8[6815744]{0:T(1024)(128)(4,1)} %bitcast.69), calls=%async_computation.5 | async-start | bytes 5242880
  101.3 5.9 %slice-start.1 = ((s8[6815744]{0:T(1024)(128)(4,1)}), s8[4194304]{0:T(1024)(128)(4,1)S(1)}, s32[]{:S(2)}) async-start(s8[6815744]{0:T(1024)(128)(4,1)} %bitcast.69), calls=%async_computation.6 | async-start | bytes 8388608
  101.3 9.6 %slice-start.2 = ((s8[6815744]{0:T(1024)(128)(4,1)}), s8[2621440]{0:T(1024)(128)(4,1)S(1)}, s32[]{:S(2)}) async-start(s8[6815744]{0:T(1024)(128)(4,1)} %bitcast.71), calls=%async_computation.7 | async-start | bytes 5242880
  107.3 3.6 %copy-start.9 = (bf16[8,4,2,4,1024]{4,0,3,1,2:T(8,128)(2,1)}, bf16[8,4,2,4,1024]{4,0,3,1,2:T(8,128)(2,1)S(1)}, u32[]{:S(2)}) copy-start(bf16[8,4,2,4,1024]{4,0,3,1,2:T(8,128)(2,1)S(1)} %fusion.31) | copy-start | bytes 1572868
  107.3 3.6 %slice-start.3 = ((s8[6815744]{0:T(1024)(128)(4,1)}), s8[4194304]{0:T(1024)(128)(4,1)S(1)}, s32[]{:S(2)}) async-start(s8[6815744]{0:T(1024)(128)(4,1)} %bitcast.71), calls=%async_computation.8 | async-start | bytes 8388608
  107.3 3.6 %copy-start.3 = (bf16[8,4,2,4,1024]{4,0,3,1,2:T(8,128)(2,1)S(1)}, bf16[8,4,2,4,1024]{4,0,3,1,2:T(8,128)(2,1)}, u32[]{:S(2)}) copy-start(bf16[8,4,2,4,1024]{4,0,3,1,2:T(8,128)(2,1)} %get-tuple-element.9) | copy-start | bytes 1572868
  110.9 2.5 %copy-start.4 = (bf16[8,4,2,4,1024]{4,0,3,1,2:T(8,128)(2,1)S(1)}, bf16[8,4,2,4,1024]{4,0,3,1,2:T(8,128)(2,1)}, u32[]{:S(2)}) copy-start(bf16[8,4,2,4,1024]{4,0,3,1,2:T(8,128)(2,1)} %get-tuple-element.9) | copy-start | bytes 1572868
  113.4 8.4 %copy-start.2 = (bf16[8,4,2,4,1664]{4,0,3,2,1:T(8,128)(2,1)S(1)}, bf16[8,4,2,4,1664]{4,0,3,2,1:T(8,128)(2,1)}, u32[]{:S(2)}) copy-start(bf16[8,4,2,4,1664]{4,0,3,2,1:T(8,128)(2,1)} %copy-done.1) | copy-start | bytes 2555908
  113.4 8.4 %copy-start.10 = (bf16[8,4,2,4,1024]{4,0,3,1,2:T(8,128)(2,1)S(1)}, bf16[8,4,2,4,1024]{4,0,3,1,2:T(8,128)(2,1)}, u32[]{:S(2)}) copy-start(bf16[8,4,2,4,1024]{4,0,3,1,2:T(8,128)(2,1)} %copy-done.9) | copy-start | bytes 1572868
  121.7 98.2 %copy-start.6 = (f32[128,1664]{1,0:T(8,128)S(1)}, f32[128,1664]{1,0:T(8,128)}, u32[]{:S(2)}) copy-start(f32[128,1664]{1,0:T(8,128)} %copy-done.5) | copy-start | bytes 2555908
  121.7 98.2 %copy-start.7 = (f32[128,2]{0,1:T(2,128)S(1)}, f32[128,2]{0,1:T(2,128)}, u32[]{:S(2)}) copy-start(f32[128,2]{0,1:T(2,128)} %param.12) | copy-start | bytes 3076
  208.9 7.7 %all-to-all-start.1 = ((bf16[4,2,4,1664]{3,2,1,0:T(4,128)(2,1)}), bf16[4,2,4,1664]{3,2,1,0:T(4,128)(2,1)S(1)}, u32[]{:S(2)}, u32[]{:S(2)}) async-start(bf16[4,2,4,1664]{3,2,1,0:T(4,128)(2,1)} %dynamic-slice_bitcast_fusion.1), calls=%async_computation.1 | async-start | bytes 212992 | tf_op jit(solution)/shard_map/all_to_all | solution.py:36
  216.5 7.7 %all-to-all-start.3 = ((bf16[4,2,4,1664]{3,2,1,0:T(4,128)(2,1)}), bf16[4,2,4,1664]{3,2,1,0:T(4,128)(2,1)S(1)}, u32[]{:S(2)}, u32[]{:S(2)}) async-start(bf16[4,2,4,1664]{3,2,1,0:T(4,128)(2,1)} %dynamic-slice_bitcast_fusion), calls=%async_computation.3 | async-start | bytes 212992 | tf_op jit(solution)/shard_map/all_to_all | solution.py:36
Sparse Core Ops, SparseCore 0:
  113.5 93.1 all-reduce.4
where the time goes:
time: 233 us; the launch traced here: 232 us
  waiting for transfers between devices  89.7 us (38%)
  blocking collectives  65.9 us (28%)
  matrix products  34.4 us (15%)
  starting transfers between devices  14.5 us (6%)
  between operations  14.3 us (6%)
  local copies, waits for them, and re-layouts  11 us (5%)
  other arithmetic  2.51 us (1%)
    unnamed x2, waiting for transfers between devices  77.8 us
    all_gather x2, blocking collectives, spread(): grouped = lax.all_gather(buffer[None], 'dp', axis=0, tiled=True)  65.9 us
    dot_general x1, matrix products, per_device(): jnp.einsum('pqxcf,pqxcd->xfd', hidden, grad_rows, preferred_element_type=...  8.35 us
    all_to_all x2, starting transfers between devices, spread(): lax.all_to_all(grouped, 'expert', split_axis=1, concat_axis=1, tiled=True)  7.71 us
    dot_general x1, matrix products, per_device(): jnp.einsum('pqxcd,pqxcf->xdf', rows, pre_grad, preferred_element_type=jnp...  7.1 us
    all_to_all x2, waiting for transfers between devices, spread(): lax.all_to_all(grouped, 'expert', split_axis=1, concat_axis=1, tiled=True)  6.81 us
    all_to_all x2, starting transfers between devices, collect(): lax.all_to_all(summed[0].astype(jnp.bfloat16), 'expert', split_axis=0, co...  6.62 us
    dot_general x1, matrix products, per_device(): jnp.einsum('pqxcd,xfd->pqxcf', grad_rows, w_out, preferred_element_type=j...  5.91 us
  transfers between devices with their start and end apart: 5, of which 4 were waited for; matrix products, arithmetic and copies ran while one was open for 12% of the time, Pallas kernels for 0%

commit v1 on v0

v1 whole, which is shorter than its diff:
```python
import functools

import jax
import jax.numpy as jnp
from jax import lax
from jax.experimental import pallas as pl
from jax.experimental.pallas import tpu as pltpu
from jax.sharding import Mesh
from jax.sharding import PartitionSpec as P

CAP = 4
CHUNK = 256
DONE = jax.ShapeDtypeStruct((8, 128), jnp.float32)


inv_root_two = 0.7071067811865476
inv_root_two_pi = 0.3989422804014327


def gelu_exact(value):
    return 0.5 * value * (1.0 + lax.erf(value * inv_root_two))


def gelu_slope(value):
    return (
        0.5 * (1.0 + lax.erf(value * inv_root_two))
        + value * jnp.exp(-0.5 * value * value) * inv_root_two_pi
    )


def contract(left, right, left_dim, right_dim):
    return lax.dot_general(
        left,
        right,
        (((left_dim,), (right_dim,)), ((), ())),
        preferred_element_type=jnp.float32,
    )


def order_matrix(expert, exp_local, count):
    shape = (count // exp_local, count)
    pick = lax.broadcasted_iota(jnp.int32, shape, 0)
    row = lax.broadcasted_iota(jnp.int32, shape, 1)
    wanted = (pick // CAP) * (CAP * exp_local) + expert * CAP + pick % CAP
    return (row == wanted).astype(jnp.bfloat16)


def slot_masks(ids_ref, slot_ref, dropped_ref, exp_local, columns):
    ids = ids_ref[...]
    group = jnp.bitwise_xor(ids // exp_local, lax.axis_index("expert"))
    target = (group * exp_local + ids % exp_local) * CAP + slot_ref[...]
    target = jnp.where(dropped_ref[...] == 0, target, -1)
    column = lax.broadcasted_iota(jnp.int32, (columns, target.shape[1]), 0)
    return [column == target[k : k + 1] for k in range(target.shape[0])]


def prepare_kernel(
    ids_ref, slot_ref, dropped_ref, gates_ref, tokens_ref, out_grad_ref, *outs, exp_local
):
    half = exp_local * CAP
    masks = slot_masks(ids_ref, slot_ref, dropped_ref, exp_local, half * len(outs))
    select = sum(mask.astype(jnp.float32) for mask in masks).astype(jnp.bfloat16)
    gate = sum(
        jnp.sum(jnp.where(mask, gates_ref[k : k + 1], 0.0), axis=1, keepdims=True)
        for k, mask in enumerate(masks)
    )
    rows = contract(select, tokens_ref[...], 1, 0)
    grads = contract(select, out_grad_ref[...], 1, 0) * gate
    for group, out_ref in enumerate(outs):
        part = slice(group * half, (group + 1) * half)
        out_ref[...] = jnp.concatenate([rows[part], grads[part]], axis=0).astype(jnp.bfloat16)


def stack_halves(refs):
    half = refs[0].shape[0] // 2
    wide = [ref[...].astype(jnp.float32) for ref in refs]
    return [
        jnp.concatenate([part[at : at + half] for part in wide], axis=0) for at in (0, half)
    ]


def finish_kernel(
    ids_ref, slot_ref, dropped_ref, gates_ref, out_grad_ref, *refs, exp_local
):
    parts, (mixed_ref, tok_grad_ref, gate_grad_ref) = refs[:-3], refs[-3:]
    returned, returned_grad = [rows.astype(jnp.bfloat16) for rows in stack_halves(parts)]
    masks = slot_masks(ids_ref, slot_ref, dropped_ref, exp_local, returned.shape[0])
    select = sum(mask.astype(jnp.float32) for mask in masks).astype(jnp.bfloat16)
    tok_grad_ref[...] = contract(select, returned_grad, 0, 0).astype(jnp.bfloat16)
    tokens = gates_ref.shape[1]
    gates = jnp.concatenate([gates_ref[...], jnp.zeros((6, tokens), jnp.float32)], axis=0).T
    wide = out_grad_ref[...].astype(jnp.float32)
    mixed = jnp.zeros(wide.shape, jnp.float32)
    grads = []
    for k, mask in enumerate(masks):
        picked = contract(mask.astype(jnp.bfloat16), returned, 0, 0)
        mixed = mixed + gates[:, k : k + 1] * picked
        grads.append(jnp.sum(picked * wide, axis=1, keepdims=True))
    mixed_ref[...] = mixed.astype(jnp.bfloat16)
    grads.append(jnp.zeros((tokens, 6), jnp.float32))
    gate_grad_ref[...] = jnp.concatenate(grads, axis=1).T[:2]


def split_kernel(after_ref, *refs):
    for out_ref, rows in zip(refs[-2:], stack_halves(refs[:-2])):
        out_ref[...] = rows.astype(jnp.bfloat16)


def pair_kernel(*refs):
    own_ref, mate_ref, out_ref = refs[-3:]
    half = own_ref.shape[0]
    out_ref[:half] = own_ref[...]
    out_ref[half:] = mate_ref[...]


def pass_kernel(*refs):
    refs[-1][...] = refs[-2][...]


def add(left_ref, right_ref):
    total = left_ref[...].astype(jnp.float32) + right_ref[...].astype(jnp.float32)
    return total.astype(jnp.bfloat16)


def add_kernel(*refs):
    left_ref, right_ref = refs[-3:-1]
    refs[-1][...] = add(left_ref, right_ref)


def add_split_kernel(*refs):
    left_ref, right_ref, mine_ref, other_ref = refs[-4:]
    half = mine_ref.shape[0]
    total = add(left_ref, right_ref)
    mine_ref[...] = total[:half]
    other_ref[...] = total[half:]


def join_kernel(*refs, groups):
    first_a, first_b, second_a, second_b = refs[-groups - 4 : -groups]
    first = add(first_a, first_b).astype(jnp.float32)
    second = add(second_a, second_b).astype(jnp.float32)
    half = first.shape[0] // groups
    for group, out_ref in enumerate(refs[-groups:]):
        part = slice(group * half, (group + 1) * half)
        out_ref[...] = jnp.concatenate([first[part], second[part]], axis=0).astype(jnp.bfloat16)


def hold_kernel(*refs):
    weight_ref, held_ref, done_ref, sems = refs[-4:]
    copies = [
        pltpu.make_async_copy(weight_ref.at[x], held_ref.at[x], sems.at[x])
        for x in range(weight_ref.shape[0])
    ]
    for copy in copies:
        copy.start()
    done_ref[...] = jnp.zeros(done_ref.shape, done_ref.dtype)
    for copy in copies:
        copy.wait()


def w_out_grad_kernel(*refs, skip, expert, at, chunk):
    hidden_ref, rows_ref = refs[skip : skip + 2]
    out_ref, done_ref, made, sems = refs[-4:]
    done_ref[...] = jnp.zeros(done_ref.shape, done_ref.dtype)
    copies = []
    for i, begin in enumerate(range(0, made.shape[0], chunk)):
        here, there = pl.ds(begin, chunk), pl.ds(at + begin, chunk)
        made[here] = contract(hidden_ref[expert, :, there], rows_ref[expert], 0, 0)
        copies.append(
            pltpu.make_async_copy(made.at[here], out_ref.at[expert, there], sems.at[i])
        )
        copies[-1].start()
    for copy in copies:
        copy.wait()


def w_in_grad_kernel(*refs, skip, expert, at, chunk):
    pre_grad_ref, rows_ref = refs[skip : skip + 2]
    out_ref, done_ref, made, sems = refs[-4:]
    done_ref[...] = jnp.zeros(done_ref.shape, done_ref.dtype)
    turned = rows_ref[expert].T
    copies = []
    for i, begin in enumerate(range(0, made.shape[1], chunk)):
        here, there = pl.ds(begin, chunk), pl.ds(at + begin, chunk)
        made[:, here] = contract(turned, pre_grad_ref[expert, :, there], 1, 0)
        copies.append(
            pltpu.make_async_copy(made.at[:, here], out_ref.at[expert, :, there], sems.at[i])
        )
        copies[-1].start()
    for copy in copies:
        copy.wait()


def params(rows):
    return pltpu.CompilerParams(vmem_limit_bytes=(6 << 20) + rows * (24 << 10))


def prepare(choices, gates, tokens, out_grad, groups, exp_local):
    block = (2 * exp_local * CAP, tokens.shape[1])
    whole = pl.BlockSpec(memory_space=pltpu.VMEM)
    return pl.pallas_call(
        functools.partial(prepare_kernel, exp_local=exp_local),
        out_specs=[whole] * groups,
        out_shape=[pltpu.VMEM(block, jnp.bfloat16)]
        + [jax.ShapeDtypeStruct(block, jnp.bfloat16)] * (groups - 1),
        compiler_params=pltpu.CompilerParams(vmem_limit_bytes=60 << 20),
        name="prepare",
    )(*choices, gates, tokens, out_grad)


def finish(choices, gates, out_grad, parts, exp_local):
    return pl.pallas_call(
        functools.partial(finish_kernel, exp_local=exp_local),
        out_shape=[
            jax.ShapeDtypeStruct(out_grad.shape, jnp.bfloat16),
            jax.ShapeDtypeStruct(out_grad.shape, jnp.bfloat16),
            jax.ShapeDtypeStruct(gates.shape, jnp.float32),
        ],
        compiler_params=params(out_grad.shape[0]),
        name="finish",
    )(*choices, gates, out_grad, *parts)


def small_call(kernel, name, after, operands, counts):
    width = operands[0].shape[1]
    results = pl.pallas_call(
        kernel,
        in_specs=[pl.BlockSpec(memory_space=pl.ANY)] * len(after)
        + [pl.BlockSpec(memory_space=pltpu.VMEM)] * len(operands),
        out_shape=[jax.ShapeDtypeStruct((count, width), jnp.bfloat16) for count in counts],
        compiler_params=params(4 * counts[0]),
        cost_estimate=order_cost(counts[0], width),
        name=name,
    )(*after, *operands)
    return list(results)


def hold(after, weight):
    return pl.pallas_call(
        hold_kernel,
        in_specs=[pl.BlockSpec(memory_space=pl.ANY)] * (len(after) + 1),
        out_specs=[pl.BlockSpec(memory_space=pltpu.VMEM)] * 2,
        out_shape=[pltpu.VMEM(weight.shape, weight.dtype), DONE],
        scratch_shapes=[pltpu.SemaphoreType.DMA((weight.shape[0],))],
        compiler_params=pltpu.CompilerParams(vmem_limit_bytes=42 << 20),
        cost_estimate=pl.CostEstimate(
            flops=0, bytes_accessed=4 * weight.size, transcendentals=0
        ),
        name="hold",
    )(*after, weight)


def weight_gradient(kernel, hidden, rows, shape, after, name, expert, part, parts, base=None):
    whole = pl.BlockSpec(memory_space=pltpu.VMEM)
    anywhere = pl.BlockSpec(memory_space=pl.ANY)
    width, units = rows.shape[2], hidden.shape[2] // parts
    chunk = min(CHUNK, units)
    made = (units, width) if kernel is w_out_grad_kernel else (width, units)
    operands = (*after, hidden, rows) + (() if base is None else (base,))
    return pl.pallas_call(
        functools.partial(kernel, skip=len(after), expert=expert, at=part * units, chunk=chunk),
        in_specs=[anywhere] * len(after) + [whole] * 2 + [anywhere] * (base is not None),
        out_specs=[anywhere, whole],
        out_shape=[jax.ShapeDtypeStruct(shape, jnp.float32), DONE],
        input_output_aliases={} if base is None else {len(operands) - 1: 0},
        scratch_shapes=[
            pltpu.VMEM(made, jnp.float32),
            pltpu.SemaphoreType.DMA((units // chunk,)),
        ],
        compiler_params=pltpu.CompilerParams(vmem_limit_bytes=24 << 20),
        cost_estimate=pl.CostEstimate(
            flops=2 * rows.shape[1] * units * width,
            bytes_accessed=4 * units * width,
            transcendentals=0,
        ),
        name=name,
    )(*operands)


def sort_kernel(after_ref, *refs, places):
    blocks, out_ref = refs[:-1], refs[-1]
    experts = out_ref.shape[0]
    count = blocks[0].shape[0]
    part = count // experts // 2
    for expert in range(experts):
        order = order_matrix(expert, experts, count)
        for step, ref in enumerate(blocks):
            rows = contract(order, ref[...], 1, 0).astype(jnp.bfloat16)
            for i in range(2):
                at = places[2 * step + i] * part
                out_ref[expert, at : at + part] = rows[i * part : (i + 1) * part]


def unsort_kernel(in_ref, *blocks, places):
    experts = in_ref.shape[0]
    count = blocks[0].shape[0]
    part = count // experts // 2
    order = jnp.concatenate(
        [order_matrix(expert, experts, count) for expert in range(experts)], axis=0
    )
    for step, ref in enumerate(blocks):
        piece = jnp.concatenate(
            [
                in_ref[expert, at * part : (at + 1) * part]
                for expert in range(experts)
                for at in places[2 * step : 2 * step + 2]
            ],
            axis=0,
        )
        ref[...] = contract(order, piece, 0, 0).astype(jnp.bfloat16)


def order_cost(count, width):
    return pl.CostEstimate(
        flops=2 * count * count * width, bytes_accessed=4 * count * width, transcendentals=0
    )


def sort_rows(blocks, experts, places, after):
    count, width = blocks[0].shape
    rows = len(blocks) * count // experts
    return pl.pallas_call(
        functools.partial(sort_kernel, places=places),
        in_specs=[pl.BlockSpec(memory_space=pl.ANY)]
        + [pl.BlockSpec(memory_space=pltpu.VMEM)] * len(blocks),
        out_shape=jax.ShapeDtypeStruct((experts, rows, width), jnp.bfloat16),
        compiler_params=params(rows),
        cost_estimate=order_cost(experts * rows, width),
        name="sort_rows",
    )(after, *blocks)


def unsort_rows(rows, places):
    experts, count, width = rows.shape
    steps = len(places) // 2
    block = experts * count // steps
    return pl.pallas_call(
        functools.partial(unsort_kernel, places=places),
        out_shape=[jax.ShapeDtypeStruct((block, width), jnp.bfloat16)] * steps,
        compiler_params=params(count),
        cost_estimate=order_cost(experts * count, width),
        name="unsort_rows",
    )(rows)


DP = ("far", "near", "pair")


def ring_mate(position, count, odd):
    if (position % 2 == 1) == odd:
        return (position + 1) % count
    return (position - 1) % count


def odd_edges(count):
    columns = count // 2
    ring = [2 * c for c in range(columns)] + [2 * c + 1 for c in reversed(range(columns))]
    return [(ring[i], ring[ring_mate(i, count, True)]) for i in range(count)]


def ring_order(count, odd):
    held = [[i, ring_mate(i, count, odd)] for i in range(count)]
    blocks = [list(pair) for pair in held]
    for _ in range(count // 2 - 1):
        odd = not odd
        held = [held[ring_mate(i, count, odd)] for i in range(count)]
        for mine, more in zip(blocks, held):
            mine += more
    return blocks


def regroup(count):
    even, odd = ring_order(count, False), ring_order(count, True)
    places = {tuple(e.index(block) for block in o) for e, o in zip(even, odd)}
    (place,) = places
    return place


def swap(block, odd):
    if odd:
        return lax.ppermute(block, DP, odd_edges(lax.axis_size(DP)))
    return lax.ppermute(block, "near", [(0, 1), (1, 0)])


def expert_swap(blocks):
    size = lax.axis_size("expert")
    got = [
        lax.ppermute(blocks[k], "expert", [(i, i ^ k) for i in range(size)])
        for k in reversed(range(1, size))
    ]
    return [blocks[0]] + got[::-1]


def per_device(tokens, expert_ids, slot_ids, dropped, gates, w_in, w_out, out_grad):
    n_expert = lax.axis_size("expert")
    n_dp = lax.axis_size(DP)
    steps = n_dp // 2
    exp_local = w_in.shape[0]
    count = n_expert * exp_local * CAP
    choices = (expert_ids.T, slot_ids.T, dropped.T)
    gates = gates.T
    send = prepare(choices, gates, tokens, out_grad, n_expert, exp_local)
    got = expert_swap(send)
    held_in, done_in = hold([], w_in)
    own_rows, own_grads = small_call(split_kernel, "split", [done_in], got, [count] * 2)

    mate_rows, mate_grads = swap(own_rows, False), swap(own_grads, True)
    pairs = [own_rows, mate_rows]
    row_blocks = small_call(pair_kernel, "pair", [mate_grads], pairs, [2 * count])
    pairs = [own_grads, mate_grads]
    grad_blocks = small_call(pair_kernel, "pair", [], pairs, [2 * count])
    held_out, done_out = hold([row_blocks[0], grad_blocks[0]], w_out)
    for step in range(1, steps):
        arrived = swap(row_blocks[-1], step % 2 == 1)
        if step == 1:
            (arrived,) = small_call(pass_kernel, "pass", [done_out], [arrived], [2 * count])
        row_blocks.append(arrived)
        grad_blocks.append(swap(grad_blocks[-1], step % 2 == 0))
    straight, crossed = range(n_dp), regroup(n_dp)
    rows = sort_rows(row_blocks, exp_local, straight, done_in)
    pre = jnp.einsum("xmd,xdf->xmf", rows, held_in, preferred_element_type=jnp.float32)
    hidden = gelu_exact(pre).astype(jnp.bfloat16)
    grad_rows = sort_rows(grad_blocks, exp_local, crossed, rows)
    hidden_grad = jnp.einsum(
        "xmd,xfd->xmf", grad_rows, held_out, preferred_element_type=jnp.float32
    )
    pre_grad = (hidden_grad * gelu_slope(pre)).astype(jnp.bfloat16)
    row_grad = jnp.einsum(
        "xmf,xdf->xmd", pre_grad, held_in, preferred_element_type=jnp.float32
    )
    back_blocks = unsort_rows(row_grad.astype(jnp.bfloat16), straight)
    output = jnp.einsum("xmf,xfd->xmd", hidden, held_out, preferred_element_type=jnp.float32)
    out_blocks = unsort_rows(output.astype(jnp.bfloat16), crossed)

    parts = 2
    work = [
        (kernel, left, right, shape, expert, part)
        for kernel, left, right, shape in (
            (w_out_grad_kernel, hidden, grad_rows, w_out.shape),
            (w_in_grad_kernel, pre_grad, rows, w_in.shape),
        )
        for expert in range(exp_local)
        for part in range(parts)
    ]
    made = {}

    def next_piece(after):
        if len(work) == 0:
            return after
        kernel, left, right, shape, expert, part = work.pop(0)
        name = kernel.__name__
        made[name], ready = weight_gradient(
            kernel, left, right, shape, [after], name, expert, part, parts, made.get(name)
        )
        return ready

    def add_step(after, block, arrived, step):
        if step > 1:
            return small_call(add_kernel, "add", after, [block, arrived], [2 * count])
        return small_call(add_split_kernel, "add_split", after, [block, arrived], [count] * 2)

    back_sum, out_sum = back_blocks[-1:], out_blocks[-1:]
    back_arrived, out_arrived = swap(back_sum[0], True), swap(out_sum[0], False)
    for step in range(steps - 1, 0, -1):
        ready = next_piece(out_sum[-1])
        back_sum = add_step([ready], back_blocks[step - 1], back_arrived, step)
        back_arrived = swap(back_sum[-1], step % 2 == 0)
        if step > 1:
            ready = next_piece(back_sum[-1])
        out_sum = add_step([ready], out_blocks[step - 1], out_arrived, step)
        out_arrived = swap(out_sum[-1], step % 2 == 1)
    joined = small_call(
        functools.partial(join_kernel, groups=n_expert),
        "join",
        [next_piece(out_sum[-1])],
        [out_sum[0], out_arrived, back_sum[0], back_arrived],
        [2 * exp_local * CAP] * n_expert,
    )
    while work:
        next_piece(joined[0])
    mixed, tok_grad, gate_grad = finish(
        choices, gates, out_grad, expert_swap(joined), exp_local
    )
    return (mixed, tok_grad, gate_grad.T, made["w_in_grad_kernel"], made["w_out_grad_kernel"])


def solution(mesh):
    n_expert, n_dp = mesh.shape["expert"], mesh.shape["dp"]
    split = Mesh(mesh.devices.reshape(n_expert, n_dp // 4, 2, 2), ("expert",) + DP)
    rows = P(("expert",) + DP, None)
    into = P("expert", None, DP)
    out_of = P("expert", DP, None)
    return jax.shard_map(
        per_device,
        mesh=split,
        in_specs=(rows, rows, rows, rows, rows, into, out_of, rows),
        out_specs=(rows, rows, rows, into, out_of),
        check_vma=False,
    )
```

time: 233 us -> 80.6 us (0.35)
  waiting for transfers between devices: 89.7 us -> 12.6 us
  blocking collectives: 65.9 us -> 0 us
  Pallas kernels: 0 us -> 31.2 us
  matrix products: 34.4 us -> 7.26 us
  starting transfers between devices: 14.5 us -> 28.4 us
  between operations: 14.3 us -> 1 us
  local copies, waits for them, and re-layouts: 11 us -> 0.03 us
  other arithmetic: 2.51 us -> 0 us
    unnamed x2 -> x0, waiting for transfers between devices: 77.8 us -> none
    all_gather x2 -> x0, blocking collectives: 65.9 us -> none  [spread(): grouped = lax.all_gather(buffer[None], 'dp', axis=0, tiled=True)]
    pallas_call x0 -> x27, Pallas kernels: none -> 31.2 us  [the longest x8 19.5 us: weight_gradient(): pl.pallas_call(functools.partial(kernel, skip=len(after), expert=expert,...]
    ppermute x0 -> x22, starting transfers between devices: none -> 28.4 us  [the longest x8 12.3 us: swap(): return lax.ppermute(block, 'near', [(0, 1), (1, 0)])]
    dot_general x10 -> x4, matrix products: 34.4 us -> 7.26 us  [the longest x1 2.37 us: per_device(): jnp.einsum('xmd,xfd->xmf', grad_rows, held_out, preferred_element_type=jn...]
    all_to_all x4 -> x0, starting transfers between devices: 14.3 us -> none  [the longest x2 7.71 us: spread(): lax.all_to_all(grouped, 'expert', split_axis=1, concat_axis=1, tiled=True)]
    ppermute x0 -> x22, waiting for transfers between devices: none -> 12.6 us  [the longest x8 6.8 us: swap(): return lax.ppermute(block, 'near', [(0, 1), (1, 0)])]
    all_to_all x4 -> x0, waiting for transfers between devices: 11.9 us -> none  [the longest x2 6.81 us: spread(): lax.all_to_all(grouped, 'expert', split_axis=1, concat_axis=1, tiled=True)]
  transfers between devices with their start and end apart: 5 -> 22, of which waited for: 4 -> 11; matrix products, arithmetic and copies ran while one was open for 12% -> 3% of each run, Pallas kernels for 0% -> 33%
where the time goes in v1:
time: 80.6 us; the launch traced here: 80.5 us
  Pallas kernels  31.2 us (39%)
  starting transfers between devices  28.4 us (35%)
  waiting for transfers between devices  12.6 us (16%)
  matrix products  7.26 us (9%)
  between operations  1 us (1%)
    pallas_call x8, Pallas kernels, weight_gradient(): pl.pallas_call(functools.partial(kernel, skip=len(after), expert=expert,...  19.5 us
    ppermute x8, starting transfers between devices, swap(): return lax.ppermute(block, 'near', [(0, 1), (1, 0)])  12.3 us
    ppermute x8, starting transfers between devices, swap(): return lax.ppermute(block, DP, odd_edges(lax.axis_size(DP)))  11.1 us
    ppermute x8, waiting for transfers between devices, swap(): return lax.ppermute(block, 'near', [(0, 1), (1, 0)])  6.8 us
    pallas_call x2, Pallas kernels, hold(): pl.pallas_call(hold_kernel, in_specs=[pl.BlockSpec(memory_space=pl.ANY)]...  6.04 us
    ppermute x6, starting transfers between devices, expert_swap(): lax.ppermute(blocks[k], 'expert', [(i, i ^ k) for i in range(size)])  5.02 us
    ppermute x8, waiting for transfers between devices, swap(): return lax.ppermute(block, DP, odd_edges(lax.axis_size(DP)))  4.99 us
    dot_general x1, matrix products, per_device(): jnp.einsum('xmd,xfd->xmf', grad_rows, held_out, preferred_element_type=jn...  2.37 us
  transfers between devices with their start and end apart: 22, of which 11 were waited for; matrix products, arithmetic and copies ran while one was open for 3% of the time, Pallas kernels for 33%

profile of v1, /device:TPU:0, one launch (start us, length us, event | category | flops | bytes accessed | tf_op | source)
XLA Modules:
  0.0 80.5 jit_solution(5846074130984284137)
XLA Ops:
  0.6 2.1 %prepare.1 = (bf16[16,1664]{1,0:T(8,128)(2,1)S(1)}, bf16[16,1664]{1,0:T(8,128)(2,1)}, bf16[16,1664]{1,0:T(8,128)(2,1)}, bf16[16,1664]{1,0:T(8,128)(2,1)}) custom-call(s32[2,128]{1,0:T(2,128)} %bitcast.13, s32[2,128]{1,0:T(2,128)} %bitcast.15, s32[2,128]{1,0:T(2,128)} %bitcast.17, f32[2,128]{1,0:T(2,128)} %bitcast.19, bf16[128,1664]{1,0:T(8,128)(2,1)} %tokens_ref.1, ...), custom_call_target="tpu_custom_call" | custom-call | tf_op jit(solution)/shard_map/prepare/pallas_call | solution.py:201
  2.8 0.4 collective-permute-start
  3.2 2.5 %collective-permute-start.1 = (bf16[16,1664]{1,0:T(8,128)(2,1)}, bf16[16,1664]{1,0:T(8,128)(2,1)S(1)}, u32[]{:S(2)}, u32[]{:S(2)}) collective-permute-start(bf16[16,1664]{1,0:T(8,128)(2,1)} %get-tuple-element.51), channel_id=1, source_target_pairs={{0,16},{8,24},{16,0},{24,8},{1,17},{9,25},{17,1},{25,9},{2,18},{10... | collective-permute-start | bytes 159752 | tf_op jit(solution)/shard_map/ppermute | solution.py:388
  5.8 3.0 %hold.2 = (bf16[2,1664,1024]{2,1,0:T(8,128)(2,1)S(1)}, f32[8,128]{1,0:T(8,128)S(1)}) custom-call(bf16[2,1664,1024]{2,1,0:T(8,128)(2,1)} %refs_0_.1), custom_call_target="tpu_custom_call" | custom-call | bytes 13631488 | tf_op jit(solution)/shard_map/hold/pallas_call | solution.py:239
  8.9 0.8 %collective-permute-done.2.refs_3_ = bf16[16,1664]{1,0:T(8,128)(2,1)S(1)} collective-permute-done((bf16[16,1664]{1,0:T(8,128)(2,1)}, bf16[16,1664]{1,0:T(8,128)(2,1)S(1)}, u32[]{:S(2)}, u32[]{:S(2)}) %collective-permute-start.2) | collective-permute-done | bytes 53280 | tf_op jit(solution)/shard_map/ppermute | solution.py:388
  9.7 1.6 %collective-permute-start.3 = (bf16[32,1664]{1,0:T(8,128)(2,1)S(1)}, bf16[32,1664]{1,0:T(8,128)(2,1)S(1)}, u32[]{:S(2)}, u32[]{:S(2)}) collective-permute-start(bf16[32,1664]{1,0:T(8,128)(2,1)S(1)} %get-tuple-element.53.refs_0_), channel_id=1, source_target_pairs={{0,1},{2,4},{4,2},{6,7},{7,6},{5,3},{3,5},{1,0},{8,9},{10,12},{12,... | collective-permute-start | bytes 319496 | tf_op jit(solution)/shard_map/ppermute | solution.py:381
  11.3 1.6 %collective-permute-start.4 = (bf16[32,1664]{1,0:T(8,128)(2,1)S(1)}, bf16[32,1664]{1,0:T(8,128)(2,1)S(1)}, u32[]{:S(2)}, u32[]{:S(2)}) collective-permute-start(bf16[32,1664]{1,0:T(8,128)(2,1)S(1)} %get-tuple-element.54.refs_1_), channel_id=1, source_target_pairs={{0,2},{2,0},{1,3},{3,1},{4,6},{6,4},{5,7},{7,5},{8,10},{10,8},{9,1... | collective-permute-start | bytes 319496 | tf_op jit(solution)/shard_map/ppermute | solution.py:382
  13.0 1.9 %collective-permute-done.3.refs_0_.refs_1_ = bf16[32,1664]{1,0:T(8,128)(2,1)S(1)} collective-permute-done((bf16[32,1664]{1,0:T(8,128)(2,1)S(1)}, bf16[32,1664]{1,0:T(8,128)(2,1)S(1)}, u32[]{:S(2)}, u32[]{:S(2)}) %collective-permute-start.3) | collective-permute-done | bytes 106528 | tf_op jit(solution)/shard_map/ppermute | solution.py:381
  14.8 1.2 %collective-permute-done.4.refs_2_ = bf16[32,1664]{1,0:T(8,128)(2,1)S(1)} collective-permute-done((bf16[32,1664]{1,0:T(8,128)(2,1)S(1)}, bf16[32,1664]{1,0:T(8,128)(2,1)S(1)}, u32[]{:S(2)}, u32[]{:S(2)}) %collective-permute-start.4) | collective-permute-done | bytes 106528 | tf_op jit(solution)/shard_map/ppermute | solution.py:382
  16.1 1.5 %collective-permute-start.5 = (bf16[64,1664]{1,0:T(8,128)(2,1)S(1)}, bf16[64,1664]{1,0:T(8,128)(2,1)S(1)}, u32[]{:S(2)}, u32[]{:S(2)}) collective-permute-start(bf16[64,1664]{1,0:T(8,128)(2,1)S(1)} %pair.2.refs_0_), channel_id=1, source_target_pairs={{0,1},{2,4},{4,2},{6,7},{7,6},{5,3},{3,5},{1,0},{8,9},{10,12},{12,... | collective-permute-start | bytes 638984 | tf_op jit(solution)/shard_map/ppermute | solution.py:381
  17.6 1.6 %collective-permute-start.8 = (bf16[64,1664]{1,0:T(8,128)(2,1)S(1)}, bf16[64,1664]{1,0:T(8,128)(2,1)S(1)}, u32[]{:S(2)}, u32[]{:S(2)}) collective-permute-start(bf16[64,1664]{1,0:T(8,128)(2,1)S(1)} %pair.3.refs_1_.refs_0_), channel_id=1, source_target_pairs={{0,2},{2,0},{1,3},{3,1},{4,6},{6,4},{5,7},{7,5},{8,10},{10,8},{9,1... | collective-permute-start | bytes 638984 | tf_op jit(solution)/shard_map/ppermute | solution.py:382
  19.2 3.0 %hold.3 = (bf16[2,1024,1664]{2,1,0:T(8,128)(2,1)S(1)}, f32[8,128]{1,0:T(8,128)S(1)}) custom-call(bf16[64,1664]{1,0:T(8,128)(2,1)S(1)} %pair.2.refs_0_, bf16[64,1664]{1,0:T(8,128)(2,1)S(1)} %pair.3.refs_1_.refs_0_, bf16[2,1024,1664]{2,1,0:T(8,128)(2,1)} %refs_2_.1), custom_call_target="tpu_custom_call" | custom-call | bytes 13631488 | tf_op jit(solution)/shard_map/hold/pallas_call | solution.py:239
  22.3 1.7 %collective-permute-start.6 = (bf16[64,1664]{1,0:T(8,128)(2,1)S(1)}, bf16[64,1664]{1,0:T(8,128)(2,1)S(1)}, u32[]{:S(2)}, u32[]{:S(2)}) collective-permute-start(bf16[64,1664]{1,0:T(8,128)(2,1)S(1)} %pass.1.refs_1_), channel_id=1, source_target_pairs={{0,2},{2,0},{1,3},{3,1},{4,6},{6,4},{5,7},{7,5},{8,10},{10,8},{9,1... | collective-permute-start | bytes 638984 | tf_op jit(solution)/shard_map/ppermute | solution.py:382
  24.0 1.5 %collective-permute-start.9 = (bf16[64,1664]{1,0:T(8,128)(2,1)S(1)}, bf16[64,1664]{1,0:T(8,128)(2,1)S(1)}, u32[]{:S(2)}, u32[]{:S(2)}) collective-permute-start(bf16[64,1664]{1,0:T(8,128)(2,1)S(1)} %collective-permute-done.8.refs_1_), channel_id=1, source_target_pairs={{0,1},{2,4},{4,2},{6,7},{7,6},{5,3},{3,5},{1,0},{8,9},{10,12},{12,... | collective-permute-start | bytes 638984 | tf_op jit(solution)/shard_map/ppermute | solution.py:381
  25.5 2.9 %collective-permute-done.6.refs_2_ = bf16[64,1664]{1,0:T(8,128)(2,1)S(1)} collective-permute-done((bf16[64,1664]{1,0:T(8,128)(2,1)S(1)}, bf16[64,1664]{1,0:T(8,128)(2,1)S(1)}, u32[]{:S(2)}, u32[]{:S(2)}) %collective-permute-start.6) | collective-permute-done | bytes 213024 | tf_op jit(solution)/shard_map/ppermute | solution.py:382
  28.4 1.6 %collective-permute-start.7 = (bf16[64,1664]{1,0:T(8,128)(2,1)S(1)}, bf16[64,1664]{1,0:T(8,128)(2,1)S(1)}, u32[]{:S(2)}, u32[]{:S(2)}) collective-permute-start(bf16[64,1664]{1,0:T(8,128)(2,1)S(1)} %collective-permute-done.6.refs_2_), channel_id=1, source_target_pairs={{0,1},{2,4},{4,2},{6,7},{7,6},{5,3},{3,5},{1,0},{8,9},{10,12},{12,... | collective-permute-start | bytes 638984 | tf_op jit(solution)/shard_map/ppermute | solution.py:381
  30.0 0.8 %collective-permute-done.9.refs_2_ = bf16[64,1664]{1,0:T(8,128)(2,1)S(1)} collective-permute-done((bf16[64,1664]{1,0:T(8,128)(2,1)S(1)}, bf16[64,1664]{1,0:T(8,128)(2,1)S(1)}, u32[]{:S(2)}, u32[]{:S(2)}) %collective-permute-start.9) | collective-permute-done | bytes 213024 | tf_op jit(solution)/shard_map/ppermute | solution.py:381
  30.8 2.6 %collective-permute-start.10 = (bf16[64,1664]{1,0:T(8,128)(2,1)S(1)}, bf16[64,1664]{1,0:T(8,128)(2,1)S(1)}, u32[]{:S(2)}, u32[]{:S(2)}) collective-permute-start(bf16[64,1664]{1,0:T(8,128)(2,1)S(1)} %collective-permute-done.9.refs_2_), channel_id=1, source_target_pairs={{0,2},{2,0},{1,3},{3,1},{4,6},{6,4},{5,7},{7,5},{8,10},{10,8},{9,1... | collective-permute-start | bytes 638984 | tf_op jit(solution)/shard_map/ppermute | solution.py:382
  33.4 1.0 %collective-permute-done.7.refs_3_ = bf16[64,1664]{1,0:T(8,128)(2,1)S(1)} collective-permute-done((bf16[64,1664]{1,0:T(8,128)(2,1)S(1)}, bf16[64,1664]{1,0:T(8,128)(2,1)S(1)}, u32[]{:S(2)}, u32[]{:S(2)}) %collective-permute-start.7) | collective-permute-done | bytes 213024 | tf_op jit(solution)/shard_map/ppermute | solution.py:381
  34.8 1.4 %multiply_convert_fusion = (bf16[2,128,1024]{2,1,0:T(8,128)(2,1)S(1)}, f32[2,128,1024]{2,1,0:T(8,128)S(1)}) fusion(bf16[2,128,1664]{2,1,0:T(8,128)(2,1)S(1)} %sort_rows.2.after_ref.refs_2_, bf16[2,1664,1024]{2,1,0:T(8,128)(2,1)S(1)} %get-tuple-element.56), kind=kOutput, calls=%fused_computation.9 | convolution fusion | flops 873725952 | bytes 9240576 | tf_op jit(solution)/shard_map/xmd,xdf->xmf/dot_general | solution.py:421
  36.2 1.0 %collective-permute-done.10.refs_3_ = bf16[64,1664]{1,0:T(8,128)(2,1)S(1)} collective-permute-done((bf16[64,1664]{1,0:T(8,128)(2,1)S(1)}, bf16[64,1664]{1,0:T(8,128)(2,1)S(1)}, u32[]{:S(2)}, u32[]{:S(2)}) %collective-permute-start.10) | collective-permute-done | bytes 213024 | tf_op jit(solution)/shard_map/ppermute | solution.py:382
  37.6 2.4 %fusion.refs_1_ = bf16[2,128,1024]{2,1,0:T(8,128)(2,1)S(1)} fusion(bf16[2,128,1664]{2,1,0:T(8,128)(2,1)S(1)} %sort_rows.3.refs_2_, bf16[2,1024,1664]{2,1,0:T(8,128)(2,1)S(1)} %get-tuple-element.57, f32[2,128,1024]{2,1,0:T(8,128)S(1)} %get-tuple-element.92), kind=kOutput, calls=%fused_computation.4 | convolution fusion | flops 875036672 | bytes 9240576 | tf_op jit(solution)/shard_map/xmd,xfd->xmf/dot_general | solution.py:424
  40.0 2.3 %convolution_convert_fusion.in_ref = bf16[2,128,1664]{2,1,0:T(8,128)(2,1)S(1)} fusion(bf16[2,128,1024]{2,1,0:T(8,128)(2,1)S(1)} %fusion.refs_1_, bf16[2,1664,1024]{2,1,0:T(8,128)(2,1)S(1)} %get-tuple-element.56), kind=kOutput, calls=%fused_computation | convolution fusion | flops 872841216 | bytes 8192000 | tf_op jit(solution)/shard_map/xmf,xdf->xmd/dot_general | solution.py:428
  42.3 0.4 unsort_rows.3
  42.7 1.7 %collective-permute-start.11 = (bf16[64,1664]{1,0:T(8,128)(2,1)S(1)}, bf16[64,1664]{1,0:T(8,128)(2,1)S(1)}, u32[]{:S(2)}, u32[]{:S(2)}) collective-permute-start(bf16[64,1664]{1,0:T(8,128)(2,1)S(1)} %get-tuple-element.61), channel_id=1, source_target_pairs={{0,1},{2,4},{4,2},{6,7},{7,6},{5,3},{3,5},{1,0},{8,9},{10,12},{12,... | collective-permute-start | bytes 638984 | tf_op jit(solution)/shard_map/ppermute | solution.py:381
  44.5 1.2 %convolution_convert_fusion.1.in_ref = bf16[2,128,1664]{2,1,0:T(8,128)(2,1)S(1)} fusion(bf16[2,128,1024]{2,1,0:T(8,128)(2,1)S(1)} %get-tuple-element.91.refs_1_, bf16[2,1024,1664]{2,1,0:T(8,128)(2,1)S(1)} %get-tuple-element.57), kind=kOutput, calls=%fused_computation.1 | convolution fusion | flops 872841216 | bytes 8192000 | tf_op jit(solution)/shard_map/xmf,xfd->xmd/dot_general | solution.py:432
  45.6 0.4 unsort_rows.2
  46.0 1.6 %collective-permute-start.12 = (bf16[64,1664]{1,0:T(8,128)(2,1)S(1)}, bf16[64,1664]{1,0:T(8,128)(2,1)S(1)}, u32[]{:S(2)}, u32[]{:S(2)}) collective-permute-start(bf16[64,1664]{1,0:T(8,128)(2,1)S(1)} %get-tuple-element.58.refs_0_), channel_id=1, source_target_pairs={{0,2},{2,0},{1,3},{3,1},{4,6},{6,4},{5,7},{7,5},{8,10},{10,8},{9,1... | collective-permute-start | bytes 638984 | tf_op jit(solution)/shard_map/ppermute | solution.py:382
  47.7 2.2 %w_out_grad_kernel.4 = (f32[2,1024,1664]{2,1,0:T(8,128)}, f32[8,128]{1,0:T(8,128)S(1)}) custom-call(bf16[64,1664]{1,0:T(8,128)(2,1)S(1)} %get-tuple-element.58.refs_0_, bf16[2,128,1024]{2,1,0:T(8,128)(2,1)S(1)} %get-tuple-element.91.refs_1_, bf16[2,128,1664]{2,1,0:T(8,128)(2,1)S(1)} %sort_rows.3.refs_2_), custom_call_target="tpu_custom_call" | custom-call | flops 218103808 | bytes 3407872 | tf_op jit(solution)/shard_map/w_out_grad_kernel/pallas_call | solution.py:260
  49.9 0.9 %collective-permute-start.13 = (bf16[64,1664]{1,0:T(8,128)(2,1)S(1)}, bf16[64,1664]{1,0:T(8,128)(2,1)S(1)}, u32[]{:S(2)}, u32[]{:S(2)}) collective-permute-start(bf16[64,1664]{1,0:T(8,128)(2,1)S(1)} %add.21.refs_0_), channel_id=1, source_target_pairs={{0,2},{2,0},{1,3},{3,1},{4,6},{6,4},{5,7},{7,5},{8,10},{10,8},{9,1... | collective-permute-start | bytes 638984 | tf_op jit(solution)/shard_map/ppermute | solution.py:382
  50.8 2.2 %w_out_grad_kernel.5 = (f32[2,1024,1664]{2,1,0:T(8,128)}, f32[8,128]{1,0:T(8,128)S(1)}) custom-call(bf16[64,1664]{1,0:T(8,128)(2,1)S(1)} %add.21.refs_0_, bf16[2,128,1024]{2,1,0:T(8,128)(2,1)S(1)} %get-tuple-element.91.refs_1_, bf16[2,128,1664]{2,1,0:T(8,128)(2,1)S(1)} %sort_rows.3.refs_2_, ...), custom_call_target="tpu_custom_call", output_to_operand_aliasing={{0}: (3, {})} | custom-call | flops 218103808 | bytes 3407872 | tf_op jit(solution)/shard_map/w_out_grad_kernel/pallas_call | solution.py:260
  53.0 0.4 collective-permute-done.12.refs_2_
  53.5 0.8 %collective-permute-start.14 = (bf16[64,1664]{1,0:T(8,128)(2,1)S(1)}, bf16[64,1664]{1,0:T(8,128)(2,1)S(1)}, u32[]{:S(2)}, u32[]{:S(2)}) collective-permute-start(bf16[64,1664]{1,0:T(8,128)(2,1)S(1)} %add.22.refs_0_), channel_id=1, source_target_pairs={{0,1},{2,4},{4,2},{6,7},{7,6},{5,3},{3,5},{1,0},{8,9},{10,12},{12,... | collective-permute-start | bytes 638984 | tf_op jit(solution)/shard_map/ppermute | solution.py:381
  54.3 2.2 %w_out_grad_kernel.6 = (f32[2,1024,1664]{2,1,0:T(8,128)}, f32[8,128]{1,0:T(8,128)S(1)}) custom-call(bf16[64,1664]{1,0:T(8,128)(2,1)S(1)} %add.22.refs_0_, bf16[2,128,1024]{2,1,0:T(8,128)(2,1)S(1)} %get-tuple-element.91.refs_1_, bf16[2,128,1664]{2,1,0:T(8,128)(2,1)S(1)} %sort_rows.3.refs_2_, ...), custom_call_target="tpu_custom_call", output_to_operand_aliasing={{0}: (3, {})} | custom-call | flops 218103808 | bytes 3407872 | tf_op jit(solution)/shard_map/w_out_grad_kernel/pallas_call | solution.py:260
  56.6 1.3 %collective-permute-start.17 = (bf16[64,1664]{1,0:T(8,128)(2,1)S(1)}, bf16[64,1664]{1,0:T(8,128)(2,1)S(1)}, u32[]{:S(2)}, u32[]{:S(2)}) collective-permute-start(bf16[64,1664]{1,0:T(8,128)(2,1)S(1)} %add.23.refs_0_), channel_id=1, source_target_pairs={{0,1},{2,4},{4,2},{6,7},{7,6},{5,3},{3,5},{1,0},{8,9},{10,12},{12,... | collective-permute-start | bytes 638984 | tf_op jit(solution)/shard_map/ppermute | solution.py:381
  57.9 2.2 %w_out_grad_kernel.7 = (f32[2,1024,1664]{2,1,0:T(8,128)}, f32[8,128]{1,0:T(8,128)S(1)}) custom-call(bf16[64,1664]{1,0:T(8,128)(2,1)S(1)} %add.23.refs_0_, bf16[2,128,1024]{2,1,0:T(8,128)(2,1)S(1)} %get-tuple-element.91.refs_1_, bf16[2,128,1664]{2,1,0:T(8,128)(2,1)S(1)} %sort_rows.3.refs_2_, ...), custom_call_target="tpu_custom_call", output_to_operand_aliasing={{0}: (3, {})} | custom-call | flops 218103808 | bytes 3407872 | tf_op jit(solution)/shard_map/w_out_grad_kernel/pallas_call | solution.py:260
  60.2 1.0 %collective-permute-start.15 = (bf16[64,1664]{1,0:T(8,128)(2,1)S(1)}, bf16[64,1664]{1,0:T(8,128)(2,1)S(1)}, u32[]{:S(2)}, u32[]{:S(2)}) collective-permute-start(bf16[64,1664]{1,0:T(8,128)(2,1)S(1)} %add.24.refs_0_), channel_id=1, source_target_pairs={{0,2},{2,0},{1,3},{3,1},{4,6},{6,4},{5,7},{7,5},{8,10},{10,8},{9,1... | collective-permute-start | bytes 638984 | tf_op jit(solution)/shard_map/ppermute | solution.py:382
  61.1 2.4 %w_in_grad_kernel.4 = (f32[2,1664,1024]{2,1,0:T(8,128)}, f32[8,128]{1,0:T(8,128)S(1)}) custom-call(bf16[64,1664]{1,0:T(8,128)(2,1)S(1)} %add.24.refs_0_, bf16[2,128,1024]{2,1,0:T(8,128)(2,1)S(1)} %fusion.refs_1_, bf16[2,128,1664]{2,1,0:T(8,128)(2,1)S(1)} %sort_rows.2.after_ref.refs_2_), custom_call_target="tpu_custom_call" | custom-call | flops 218103808 | bytes 3407872 | tf_op jit(solution)/shard_map/w_in_grad_kernel/pallas_call | solution.py:260
  63.6 1.2 %collective-permute-start.18 = (bf16[32,1664]{1,0:T(8,128)(2,1)S(1)}, bf16[32,1664]{1,0:T(8,128)(2,1)S(1)}, u32[]{:S(2)}, u32[]{:S(2)}) collective-permute-start(bf16[32,1664]{1,0:T(8,128)(2,1)S(1)} %get-tuple-element.79), channel_id=1, source_target_pairs={{0,2},{2,0},{1,3},{3,1},{4,6},{6,4},{5,7},{7,5},{8,10},{10,8},{9,1... | collective-permute-start | bytes 319496 | tf_op jit(solution)/shard_map/ppermute | solution.py:382
  64.8 1.3 %collective-permute-done.15.refs_2_ = bf16[64,1664]{1,0:T(8,128)(2,1)S(1)} collective-permute-done((bf16[64,1664]{1,0:T(8,128)(2,1)S(1)}, bf16[64,1664]{1,0:T(8,128)(2,1)S(1)}, u32[]{:S(2)}, u32[]{:S(2)}) %collective-permute-start.15) | collective-permute-done | bytes 213024 | tf_op jit(solution)/shard_map/ppermute | solution.py:382
  66.1 1.1 %collective-permute-start.16 = (bf16[32,1664]{1,0:T(8,128)(2,1)S(1)}, bf16[32,1664]{1,0:T(8,128)(2,1)S(1)}, u32[]{:S(2)}, u32[]{:S(2)}) collective-permute-start(bf16[32,1664]{1,0:T(8,128)(2,1)S(1)} %get-tuple-element.73.refs_0_), channel_id=1, source_target_pairs={{0,1},{2,4},{4,2},{6,7},{7,6},{5,3},{3,5},{1,0},{8,9},{10,12},{12,... | collective-permute-start | bytes 319496 | tf_op jit(solution)/shard_map/ppermute | solution.py:381
  67.3 2.4 %w_in_grad_kernel.5 = (f32[2,1664,1024]{2,1,0:T(8,128)}, f32[8,128]{1,0:T(8,128)S(1)}) custom-call(bf16[32,1664]{1,0:T(8,128)(2,1)S(1)} %get-tuple-element.73.refs_0_, bf16[2,128,1024]{2,1,0:T(8,128)(2,1)S(1)} %fusion.refs_1_, bf16[2,128,1664]{2,1,0:T(8,128)(2,1)S(1)} %sort_rows.2.after_ref.refs_2_, ...), custom_call_target="tpu_custom_call", output_to_operand_aliasing={{0}: (3, {})} | custom-call | flops 218103808 | bytes 3407872 | tf_op jit(solution)/shard_map/w_in_grad_kernel/pallas_call | solution.py:260
  69.7 1.2 %collective-permute-done.16.refs_2_ = bf16[32,1664]{1,0:T(8,128)(2,1)S(1)} collective-permute-done((bf16[32,1664]{1,0:T(8,128)(2,1)S(1)}, bf16[32,1664]{1,0:T(8,128)(2,1)S(1)}, u32[]{:S(2)}, u32[]{:S(2)}) %collective-permute-start.16) | collective-permute-done | bytes 106528 | tf_op jit(solution)/shard_map/ppermute | solution.py:381
  71.0 1.4 %collective-permute-start.20 = (bf16[16,1664]{1,0:T(8,128)(2,1)S(1)}, bf16[16,1664]{1,0:T(8,128)(2,1)S(1)}, u32[]{:S(2)}, u32[]{:S(2)}) collective-permute-start(bf16[16,1664]{1,0:T(8,128)(2,1)S(1)} %get-tuple-element.82), channel_id=1, source_target_pairs={{0,16},{8,24},{16,0},{24,8},{1,17},{9,25},{17,1},{25,9},{2,18},{10... | collective-permute-start | bytes 159752 | tf_op jit(solution)/shard_map/ppermute | solution.py:388
  72.4 0.5 collective-permute-start.21
  72.9 3.0 %w_in_grad_kernel.6 = (f32[2,1664,1024]{2,1,0:T(8,128)}, f32[8,128]{1,0:T(8,128)}) custom-call(bf16[16,1664]{1,0:T(8,128)(2,1)S(1)} %get-tuple-element.80.refs_0_, bf16[2,128,1024]{2,1,0:T(8,128)(2,1)S(1)} %fusion.refs_1_, bf16[2,128,1664]{2,1,0:T(8,128)(2,1)S(1)} %sort_rows.2.after_ref.refs_2_, ...), custom_call_target="tpu_custom_call", output_to_operand_aliasing={{0}: (3, {})} | custom-call | flops 218103808 | bytes 3407872 | tf_op jit(solution)/shard_map/w_in_grad_kernel/pallas_call | solution.py:260
  75.9 3.0 %w_in_grad_kernel.7 = (f32[2,1664,1024]{2,1,0:T(8,128)}, f32[8,128]{1,0:T(8,128)}) custom-call(bf16[16,1664]{1,0:T(8,128)(2,1)S(1)} %get-tuple-element.80.refs_0_, bf16[2,128,1024]{2,1,0:T(8,128)(2,1)S(1)} %fusion.refs_1_, bf16[2,128,1664]{2,1,0:T(8,128)(2,1)S(1)} %sort_rows.2.after_ref.refs_2_, ...), custom_call_target="tpu_custom_call", output_to_operand_aliasing={{0}: (3, {})} | custom-call | flops 218103808 | bytes 3407872 | tf_op jit(solution)/shard_map/w_in_grad_kernel/pallas_call | solution.py:260
  79.0 1.5 %finish.1 = (bf16[128,1664]{1,0:T(8,128)(2,1)}, bf16[128,1664]{1,0:T(8,128)(2,1)}, f32[2,128]{1,0:T(2,128)}) custom-call(s32[2,128]{1,0:T(2,128)S(1)} %bitcast.14, s32[2,128]{1,0:T(2,128)S(1)} %bitcast.16, s32[2,128]{1,0:T(2,128)S(1)} %bitcast.18, f32[2,128]{1,0:T(2,128)S(1)} %bitcast.20, bf16[128,1664]{1,0:T(8,128)(2,1)S(1)} %copy-done, ...), custom_call_target="tpu_custom_call" | custom-call | tf_op jit(solution)/shard_map/finish/pallas_call | solution.py:212
  (37 shorter events, 1.5 us)
Async XLA Ops:
  2.8 6.1 %collective-permute-start = (bf16[16,1664]{1,0:T(8,128)(2,1)}, bf16[16,1664]{1,0:T(8,128)(2,1)S(1)}, u32[]{:S(2)}, u32[]{:S(2)}) collective-permute-start(bf16[16,1664]{1,0:T(8,128)(2,1)} %get-tuple-element.50), channel_id=1, source_target_pairs={{0,8},{8,0},{16,24},{24,16},{1,9},{9,1},{17,25},{25,17},{2,10},{10... | collective-permute-start | bytes 159752 | tf_op jit(solution)/shard_map/ppermute | solution.py:388
  3.2 5.7 %collective-permute-start.1 = (bf16[16,1664]{1,0:T(8,128)(2,1)}, bf16[16,1664]{1,0:T(8,128)(2,1)S(1)}, u32[]{:S(2)}, u32[]{:S(2)}) collective-permute-start(bf16[16,1664]{1,0:T(8,128)(2,1)} %get-tuple-element.51), channel_id=1, source_target_pairs={{0,16},{8,24},{16,0},{24,8},{1,17},{9,25},{17,1},{25,9},{2,18},{10... | collective-permute-start | bytes 159752 | tf_op jit(solution)/shard_map/ppermute | solution.py:388
  5.7 4.0 %collective-permute-start.2 = (bf16[16,1664]{1,0:T(8,128)(2,1)}, bf16[16,1664]{1,0:T(8,128)(2,1)S(1)}, u32[]{:S(2)}, u32[]{:S(2)}) collective-permute-start(bf16[16,1664]{1,0:T(8,128)(2,1)} %get-tuple-element.52), channel_id=1, source_target_pairs={{0,24},{8,16},{16,8},{24,0},{1,25},{9,17},{17,9},{25,1},{2,26},{10... | collective-permute-start | bytes 159752 | tf_op jit(solution)/shard_map/ppermute | solution.py:388
  9.7 5.1 %collective-permute-start.3 = (bf16[32,1664]{1,0:T(8,128)(2,1)S(1)}, bf16[32,1664]{1,0:T(8,128)(2,1)S(1)}, u32[]{:S(2)}, u32[]{:S(2)}) collective-permute-start(bf16[32,1664]{1,0:T(8,128)(2,1)S(1)} %get-tuple-element.53.refs_0_), channel_id=1, source_target_pairs={{0,1},{2,4},{4,2},{6,7},{7,6},{5,3},{3,5},{1,0},{8,9},{10,12},{12,... | collective-permute-start | bytes 319496 | tf_op jit(solution)/shard_map/ppermute | solution.py:381
  11.3 4.7 %collective-permute-start.4 = (bf16[32,1664]{1,0:T(8,128)(2,1)S(1)}, bf16[32,1664]{1,0:T(8,128)(2,1)S(1)}, u32[]{:S(2)}, u32[]{:S(2)}) collective-permute-start(bf16[32,1664]{1,0:T(8,128)(2,1)S(1)} %get-tuple-element.54.refs_1_), channel_id=1, source_target_pairs={{0,2},{2,0},{1,3},{3,1},{4,6},{6,4},{5,7},{7,5},{8,10},{10,8},{9,1... | collective-permute-start | bytes 319496 | tf_op jit(solution)/shard_map/ppermute | solution.py:382
  16.1 6.2 %collective-permute-start.5 = (bf16[64,1664]{1,0:T(8,128)(2,1)S(1)}, bf16[64,1664]{1,0:T(8,128)(2,1)S(1)}, u32[]{:S(2)}, u32[]{:S(2)}) collective-permute-start(bf16[64,1664]{1,0:T(8,128)(2,1)S(1)} %pair.2.refs_0_), channel_id=1, source_target_pairs={{0,1},{2,4},{4,2},{6,7},{7,6},{5,3},{3,5},{1,0},{8,9},{10,12},{12,... | collective-permute-start | bytes 638984 | tf_op jit(solution)/shard_map/ppermute | solution.py:381
  17.6 6.4 %collective-permute-start.8 = (bf16[64,1664]{1,0:T(8,128)(2,1)S(1)}, bf16[64,1664]{1,0:T(8,128)(2,1)S(1)}, u32[]{:S(2)}, u32[]{:S(2)}) collective-permute-start(bf16[64,1664]{1,0:T(8,128)(2,1)S(1)} %pair.3.refs_1_.refs_0_), channel_id=1, source_target_pairs={{0,2},{2,0},{1,3},{3,1},{4,6},{6,4},{5,7},{7,5},{8,10},{10,8},{9,1... | collective-permute-start | bytes 638984 | tf_op jit(solution)/shard_map/ppermute | solution.py:382
  22.3 6.1 %collective-permute-start.6 = (bf16[64,1664]{1,0:T(8,128)(2,1)S(1)}, bf16[64,1664]{1,0:T(8,128)(2,1)S(1)}, u32[]{:S(2)}, u32[]{:S(2)}) collective-permute-start(bf16[64,1664]{1,0:T(8,128)(2,1)S(1)} %pass.1.refs_1_), channel_id=1, source_target_pairs={{0,2},{2,0},{1,3},{3,1},{4,6},{6,4},{5,7},{7,5},{8,10},{10,8},{9,1... | collective-permute-start | bytes 638984 | tf_op jit(solution)/shard_map/ppermute | solution.py:382
  24.0 6.7 %collective-permute-start.9 = (bf16[64,1664]{1,0:T(8,128)(2,1)S(1)}, bf16[64,1664]{1,0:T(8,128)(2,1)S(1)}, u32[]{:S(2)}, u32[]{:S(2)}) collective-permute-start(bf16[64,1664]{1,0:T(8,128)(2,1)S(1)} %collective-permute-done.8.refs_1_), channel_id=1, source_target_pairs={{0,1},{2,4},{4,2},{6,7},{7,6},{5,3},{3,5},{1,0},{8,9},{10,12},{12,... | collective-permute-start | bytes 638984 | tf_op jit(solution)/shard_map/ppermute | solution.py:381
  28.4 6.0 %collective-permute-start.7 = (bf16[64,1664]{1,0:T(8,128)(2,1)S(1)}, bf16[64,1664]{1,0:T(8,128)(2,1)S(1)}, u32[]{:S(2)}, u32[]{:S(2)}) collective-permute-start(bf16[64,1664]{1,0:T(8,128)(2,1)S(1)} %collective-permute-done.6.refs_2_), channel_id=1, source_target_pairs={{0,1},{2,4},{4,2},{6,7},{7,6},{5,3},{3,5},{1,0},{8,9},{10,12},{12,... | collective-permute-start | bytes 638984 | tf_op jit(solution)/shard_map/ppermute | solution.py:381
  30.8 6.5 %collective-permute-start.10 = (bf16[64,1664]{1,0:T(8,128)(2,1)S(1)}, bf16[64,1664]{1,0:T(8,128)(2,1)S(1)}, u32[]{:S(2)}, u32[]{:S(2)}) collective-permute-start(bf16[64,1664]{1,0:T(8,128)(2,1)S(1)} %collective-permute-done.9.refs_2_), channel_id=1, source_target_pairs={{0,2},{2,0},{1,3},{3,1},{4,6},{6,4},{5,7},{7,5},{8,10},{10,8},{9,1... | collective-permute-start | bytes 638984 | tf_op jit(solution)/shard_map/ppermute | solution.py:382
  42.7 7.1 %collective-permute-start.11 = (bf16[64,1664]{1,0:T(8,128)(2,1)S(1)}, bf16[64,1664]{1,0:T(8,128)(2,1)S(1)}, u32[]{:S(2)}, u32[]{:S(2)}) collective-permute-start(bf16[64,1664]{1,0:T(8,128)(2,1)S(1)} %get-tuple-element.61), channel_id=1, source_target_pairs={{0,1},{2,4},{4,2},{6,7},{7,6},{5,3},{3,5},{1,0},{8,9},{10,12},{12,... | collective-permute-start | bytes 638984 | tf_op jit(solution)/shard_map/ppermute | solution.py:381
  46.0 7.4 %collective-permute-start.12 = (bf16[64,1664]{1,0:T(8,128)(2,1)S(1)}, bf16[64,1664]{1,0:T(8,128)(2,1)S(1)}, u32[]{:S(2)}, u32[]{:S(2)}) collective-permute-start(bf16[64,1664]{1,0:T(8,128)(2,1)S(1)} %get-tuple-element.58.refs_0_), channel_id=1, source_target_pairs={{0,2},{2,0},{1,3},{3,1},{4,6},{6,4},{5,7},{7,5},{8,10},{10,8},{9,1... | collective-permute-start | bytes 638984 | tf_op jit(solution)/shard_map/ppermute | solution.py:382
  49.9 6.5 %collective-permute-start.13 = (bf16[64,1664]{1,0:T(8,128)(2,1)S(1)}, bf16[64,1664]{1,0:T(8,128)(2,1)S(1)}, u32[]{:S(2)}, u32[]{:S(2)}) collective-permute-start(bf16[64,1664]{1,0:T(8,128)(2,1)S(1)} %add.21.refs_0_), channel_id=1, source_target_pairs={{0,2},{2,0},{1,3},{3,1},{4,6},{6,4},{5,7},{7,5},{8,10},{10,8},{9,1... | collective-permute-start | bytes 638984 | tf_op jit(solution)/shard_map/ppermute | solution.py:382
  53.5 6.6 %collective-permute-start.14 = (bf16[64,1664]{1,0:T(8,128)(2,1)S(1)}, bf16[64,1664]{1,0:T(8,128)(2,1)S(1)}, u32[]{:S(2)}, u32[]{:S(2)}) collective-permute-start(bf16[64,1664]{1,0:T(8,128)(2,1)S(1)} %add.22.refs_0_), channel_id=1, source_target_pairs={{0,1},{2,4},{4,2},{6,7},{7,6},{5,3},{3,5},{1,0},{8,9},{10,12},{12,... | collective-permute-start | bytes 638984 | tf_op jit(solution)/shard_map/ppermute | solution.py:381
  56.6 7.0 %collective-permute-start.17 = (bf16[64,1664]{1,0:T(8,128)(2,1)S(1)}, bf16[64,1664]{1,0:T(8,128)(2,1)S(1)}, u32[]{:S(2)}, u32[]{:S(2)}) collective-permute-start(bf16[64,1664]{1,0:T(8,128)(2,1)S(1)} %add.23.refs_0_), channel_id=1, source_target_pairs={{0,1},{2,4},{4,2},{6,7},{7,6},{5,3},{3,5},{1,0},{8,9},{10,12},{12,... | collective-permute-start | bytes 638984 | tf_op jit(solution)/shard_map/ppermute | solution.py:381
  60.2 5.9 %collective-permute-start.15 = (bf16[64,1664]{1,0:T(8,128)(2,1)S(1)}, bf16[64,1664]{1,0:T(8,128)(2,1)S(1)}, u32[]{:S(2)}, u32[]{:S(2)}) collective-permute-start(bf16[64,1664]{1,0:T(8,128)(2,1)S(1)} %add.24.refs_0_), channel_id=1, source_target_pairs={{0,2},{2,0},{1,3},{3,1},{4,6},{6,4},{5,7},{7,5},{8,10},{10,8},{9,1... | collective-permute-start | bytes 638984 | tf_op jit(solution)/shard_map/ppermute | solution.py:382
  63.6 6.1 %collective-permute-start.18 = (bf16[32,1664]{1,0:T(8,128)(2,1)S(1)}, bf16[32,1664]{1,0:T(8,128)(2,1)S(1)}, u32[]{:S(2)}, u32[]{:S(2)}) collective-permute-start(bf16[32,1664]{1,0:T(8,128)(2,1)S(1)} %get-tuple-element.79), channel_id=1, source_target_pairs={{0,2},{2,0},{1,3},{3,1},{4,6},{6,4},{5,7},{7,5},{8,10},{10,8},{9,1... | collective-permute-start | bytes 319496 | tf_op jit(solution)/shard_map/ppermute | solution.py:382
  66.1 4.8 %collective-permute-start.16 = (bf16[32,1664]{1,0:T(8,128)(2,1)S(1)}, bf16[32,1664]{1,0:T(8,128)(2,1)S(1)}, u32[]{:S(2)}, u32[]{:S(2)}) collective-permute-start(bf16[32,1664]{1,0:T(8,128)(2,1)S(1)} %get-tuple-element.73.refs_0_), channel_id=1, source_target_pairs={{0,1},{2,4},{4,2},{6,7},{7,6},{5,3},{3,5},{1,0},{8,9},{10,12},{12,... | collective-permute-start | bytes 319496 | tf_op jit(solution)/shard_map/ppermute | solution.py:381
  71.0 8.0 %collective-permute-start.19 = (bf16[16,1664]{1,0:T(8,128)(2,1)S(1)}, bf16[16,1664]{1,0:T(8,128)(2,1)S(1)}, u32[]{:S(2)}, u32[]{:S(2)}) collective-permute-start(bf16[16,1664]{1,0:T(8,128)(2,1)S(1)} %get-tuple-element.81), channel_id=1, source_target_pairs={{0,8},{8,0},{16,24},{24,16},{1,9},{9,1},{17,25},{25,17},{2,10},{10... | collective-permute-start | bytes 159752 | tf_op jit(solution)/shard_map/ppermute | solution.py:388
  71.0 7.9 %collective-permute-start.20 = (bf16[16,1664]{1,0:T(8,128)(2,1)S(1)}, bf16[16,1664]{1,0:T(8,128)(2,1)S(1)}, u32[]{:S(2)}, u32[]{:S(2)}) collective-permute-start(bf16[16,1664]{1,0:T(8,128)(2,1)S(1)} %get-tuple-element.82), channel_id=1, source_target_pairs={{0,16},{8,24},{16,0},{24,8},{1,17},{9,25},{17,1},{25,9},{2,18},{10... | collective-permute-start | bytes 159752 | tf_op jit(solution)/shard_map/ppermute | solution.py:388
  72.4 6.5 %collective-permute-start.21 = (bf16[16,1664]{1,0:T(8,128)(2,1)S(1)}, bf16[16,1664]{1,0:T(8,128)(2,1)S(1)}, u32[]{:S(2)}, u32[]{:S(2)}) collective-permute-start(bf16[16,1664]{1,0:T(8,128)(2,1)S(1)} %get-tuple-element.83), channel_id=1, source_target_pairs={{0,24},{8,16},{16,8},{24,0},{1,25},{9,17},{17,9},{25,1},{2,26},{10... | collective-permute-start | bytes 159752 | tf_op jit(solution)/shard_map/ppermute | solution.py:388
  75.9 3.1 %copy-start = (bf16[128,1664]{1,0:T(8,128)(2,1)S(1)}, bf16[128,1664]{1,0:T(8,128)(2,1)}, u32[]{:S(2)}) copy-start(bf16[128,1664]{1,0:T(8,128)(2,1)} %out_grad_ref.3) | copy-start | bytes 1277956
  75.9 3.1 %copy-start.1 = (s32[128,2]{0,1:T(2,128)S(1)}, s32[128,2]{0,1:T(2,128)}, u32[]{:S(2)}) copy-start(s32[128,2]{0,1:T(2,128)} %param.9) | copy-start | bytes 3076
  75.9 3.1 %copy-start.2 = (s32[128,2]{0,1:T(2,128)S(1)}, s32[128,2]{0,1:T(2,128)}, u32[]{:S(2)}) copy-start(s32[128,2]{0,1:T(2,128)} %param.10) | copy-start | bytes 3076
  75.9 3.1 %copy-start.3 = (s32[128,2]{0,1:T(2,128)S(1)}, s32[128,2]{0,1:T(2,128)}, u32[]{:S(2)}) copy-start(s32[128,2]{0,1:T(2,128)} %param.11) | copy-start | bytes 3076
  75.9 3.1 %copy-start.4 = (f32[128,2]{0,1:T(2,128)S(1)}, f32[128,2]{0,1:T(2,128)}, u32[]{:S(2)}) copy-start(f32[128,2]{0,1:T(2,128)} %param.12) | copy-start | bytes 3076

commit v2 on v1

--- a/solution.py
+++ b/solution.py
@@ -37,11 +37,13 @@
     )
 
 
-def order_matrix(expert, exp_local, count):
-    shape = (count // exp_local, count)
-    pick = lax.broadcasted_iota(jnp.int32, shape, 0)
-    row = lax.broadcasted_iota(jnp.int32, shape, 1)
-    wanted = (pick // CAP) * (CAP * exp_local) + expert * CAP + pick % CAP
+def order_matrix(count, exp_local):
+    pick = lax.broadcasted_iota(jnp.int32, (count, count), 0)
+    row = lax.broadcasted_iota(jnp.int32, (count, count), 1)
+    kinds = 2 * exp_local
+    each = count // kinds
+    kind, rest = pick // each, pick % each
+    wanted = (rest // CAP) * (CAP * kinds) + kind * CAP + rest % CAP
     return (row == wanted).astype(jnp.bfloat16)
 
 
@@ -101,16 +103,11 @@
     gate_grad_ref[...] = jnp.concatenate(grads, axis=1).T[:2]
 
 
-def split_kernel(after_ref, *refs):
-    for out_ref, rows in zip(refs[-2:], stack_halves(refs[:-2])):
-        out_ref[...] = rows.astype(jnp.bfloat16)
-
-
-def pair_kernel(*refs):
-    own_ref, mate_ref, out_ref = refs[-3:]
-    half = own_ref.shape[0]
-    out_ref[:half] = own_ref[...]
-    out_ref[half:] = mate_ref[...]
+def stack_kernel(*refs, skip):
+    out_ref = refs[-1]
+    for i, ref in enumerate(refs[skip:-1]):
+        count = ref.shape[0]
+        out_ref[i * count : (i + 1) * count] = ref[...]
 
 
 def pass_kernel(*refs):
@@ -135,14 +132,11 @@
     other_ref[...] = total[half:]
 
 
-def join_kernel(*refs, groups):
-    first_a, first_b, second_a, second_b = refs[-groups - 4 : -groups]
-    first = add(first_a, first_b).astype(jnp.float32)
-    second = add(second_a, second_b).astype(jnp.float32)
-    half = first.shape[0] // groups
-    for group, out_ref in enumerate(refs[-groups:]):
-        part = slice(group * half, (group + 1) * half)
-        out_ref[...] = jnp.concatenate([first[part], second[part]], axis=0).astype(jnp.bfloat16)
+def join_kernel(left_ref, right_ref, *outs):
+    total = add(left_ref, right_ref)
+    for i, out_ref in enumerate(outs):
+        count = out_ref.shape[0]
+        out_ref[...] = total[i * count : (i + 1) * count]
 
 
 def hold_kernel(*refs):
@@ -277,37 +271,32 @@
     )(*operands)
 
 
-def sort_kernel(after_ref, *refs, places):
-    blocks, out_ref = refs[:-1], refs[-1]
-    experts = out_ref.shape[0]
-    count = blocks[0].shape[0]
-    part = count // experts // 2
-    for expert in range(experts):
-        order = order_matrix(expert, experts, count)
-        for step, ref in enumerate(blocks):
-            rows = contract(order, ref[...], 1, 0).astype(jnp.bfloat16)
-            for i in range(2):
-                at = places[2 * step + i] * part
-                out_ref[expert, at : at + part] = rows[i * part : (i + 1) * part]
-
-
-def unsort_kernel(in_ref, *blocks, places):
-    experts = in_ref.shape[0]
-    count = blocks[0].shape[0]
-    part = count // experts // 2
-    order = jnp.concatenate(
-        [order_matrix(expert, experts, count) for expert in range(experts)], axis=0
-    )
-    for step, ref in enumerate(blocks):
-        piece = jnp.concatenate(
-            [
-                in_ref[expert, at * part : (at + 1) * part]
-                for expert in range(experts)
-                for at in places[2 * step : 2 * step + 2]
-            ],
-            axis=0,
-        )
-        ref[...] = contract(order, piece, 0, 0).astype(jnp.bfloat16)
+def sort_kernel(after_ref, *refs):
+    blocks, outs = refs[:-2], refs[-2:]
+    experts = outs[0].shape[0]
+    count = blocks[0].shape[0] // 2
+    part = count // (2 * experts)
+    order = order_matrix(count, experts)
+    for i in range(2 * len(blocks)):
+        half = slice((i % 2) * count, (i % 2 + 1) * count)
+        rows = contract(order, blocks[i // 2][half], 1, 0).astype(jnp.bfloat16)
+        for kind in range(2 * experts):
+            outs[kind // experts][kind % experts, i * part : (i + 1) * part] = rows[
+                kind * part : (kind + 1) * part
+            ]
+
+
+def unsort_kernel(*refs):
+    ins, blocks = refs[:2], refs[2:]
+    experts = ins[0].shape[0]
+    count = blocks[0].shape[0] // 2
+    part = count // (2 * experts)
+    order = order_matrix(count, experts)
+    for i in range(2 * len(blocks)):
+        at = slice(i * part, (i + 1) * part)
+        piece = jnp.concatenate([ref[x, at] for ref in ins for x in range(experts)], axis=0)
+        half = slice((i % 2) * count, (i % 2 + 1) * count)
+        blocks[i // 2][half] = contract(order, piece, 0, 0).astype(jnp.bfloat16)
 
 
 def order_cost(count, width):
@@ -316,31 +305,30 @@
     )
 
 
-def sort_rows(blocks, experts, places, after):
+def sort_rows(blocks, experts, after):
     count, width = blocks[0].shape
-    rows = len(blocks) * count // experts
-    return pl.pallas_call(
-        functools.partial(sort_kernel, places=places),
+    rows = len(blocks) * count // (2 * experts)
+    return pl.pallas_call(
+        sort_kernel,
         in_specs=[pl.BlockSpec(memory_space=pl.ANY)]
         + [pl.BlockSpec(memory_space=pltpu.VMEM)] * len(blocks),
-        out_shape=jax.ShapeDtypeStruct((experts, rows, width), jnp.bfloat16),
-        compiler_params=params(rows),
-        cost_estimate=order_cost(experts * rows, width),
+        out_shape=[jax.ShapeDtypeStruct((experts, rows, width), jnp.bfloat16)] * 2,
+        compiler_params=params(2 * rows),
+        cost_estimate=order_cost(2 * experts * rows, width),
         name="sort_rows",
     )(after, *blocks)
 
 
-def unsort_rows(rows, places):
-    experts, count, width = rows.shape
-    steps = len(places) // 2
-    block = experts * count // steps
-    return pl.pallas_call(
-        functools.partial(unsort_kernel, places=places),
+def unsort_rows(first, second, steps):
+    experts, count, width = first.shape
+    block = 2 * experts * count // steps
+    return pl.pallas_call(
+        unsort_kernel,
         out_shape=[jax.ShapeDtypeStruct((block, width), jnp.bfloat16)] * steps,
-        compiler_params=params(count),
-        cost_estimate=order_cost(experts * count, width),
+        compiler_params=params(2 * count),
+        cost_estimate=order_cost(2 * experts * count, width),
         name="unsort_rows",
-    )(rows)
+    )(first, second)
 
 
 DP = ("far", "near", "pair")
@@ -352,34 +340,20 @@
     return (position - 1) % count
 
 
-def odd_edges(count):
+def ring_edges(count, odd):
     columns = count // 2
     ring = [2 * c for c in range(columns)] + [2 * c + 1 for c in reversed(range(columns))]
-    return [(ring[i], ring[ring_mate(i, count, True)]) for i in range(count)]
-
-
-def ring_order(count, odd):
-    held = [[i, ring_mate(i, count, odd)] for i in range(count)]
-    blocks = [list(pair) for pair in held]
-    for _ in range(count // 2 - 1):
-        odd = not odd
-        held = [held[ring_mate(i, count, odd)] for i in range(count)]
-        for mine, more in zip(blocks, held):
-            mine += more
-    return blocks
-
-
-def regroup(count):
-    even, odd = ring_order(count, False), ring_order(count, True)
-    places = {tuple(e.index(block) for block in o) for e, o in zip(even, odd)}
-    (place,) = places
-    return place
-
-
-def swap(block, odd):
-    if odd:
-        return lax.ppermute(block, DP, odd_edges(lax.axis_size(DP)))
-    return lax.ppermute(block, "near", [(0, 1), (1, 0)])
+    return [(ring[i], ring[ring_mate(i, count, odd)]) for i in range(count)]
+
+
+def swap(block, phase):
+    n_expert, n_dp = lax.axis_size("expert"), lax.axis_size(DP)
+    pairs = [
+        (e * n_dp + i, e * n_dp + j)
+        for e in range(n_expert)
+        for i, j in ring_edges(n_dp, (phase + e) % 2 == 1)
+    ]
+    return lax.ppermute(block, ("expert",) + DP, pairs)
 
 
 def expert_swap(blocks):
@@ -396,31 +370,27 @@
     n_dp = lax.axis_size(DP)
     steps = n_dp // 2
     exp_local = w_in.shape[0]
-    count = n_expert * exp_local * CAP
+    count = 2 * n_expert * exp_local * CAP
     choices = (expert_ids.T, slot_ids.T, dropped.T)
     gates = gates.T
     send = prepare(choices, gates, tokens, out_grad, n_expert, exp_local)
     got = expert_swap(send)
     held_in, done_in = hold([], w_in)
-    own_rows, own_grads = small_call(split_kernel, "split", [done_in], got, [count] * 2)
-
-    mate_rows, mate_grads = swap(own_rows, False), swap(own_grads, True)
-    pairs = [own_rows, mate_rows]
-    row_blocks = small_call(pair_kernel, "pair", [mate_grads], pairs, [2 * count])
-    pairs = [own_grads, mate_grads]
-    grad_blocks = small_call(pair_kernel, "pair", [], pairs, [2 * count])
-    held_out, done_out = hold([row_blocks[0], grad_blocks[0]], w_out)
+    stack = functools.partial(stack_kernel, skip=1)
+    (own,) = small_call(stack, "stack", [done_in], got, [count])
+
+    stack = functools.partial(stack_kernel, skip=0)
+    blocks = small_call(stack, "pair", [], [own, swap(own, 0)], [2 * count])
+    held_out, done_out = hold(blocks, w_out)
     for step in range(1, steps):
-        arrived = swap(row_blocks[-1], step % 2 == 1)
+        arrived = swap(blocks[-1], step)
         if step == 1:
             (arrived,) = small_call(pass_kernel, "pass", [done_out], [arrived], [2 * count])
-        row_blocks.append(arrived)
-        grad_blocks.append(swap(grad_blocks[-1], step % 2 == 0))
-    straight, crossed = range(n_dp), regroup(n_dp)
-    rows = sort_rows(row_blocks, exp_local, straight, done_in)
+        blocks.append(arrived)
+    rows, grad_rows = sort_rows(blocks, exp_local, done_in)
     pre = jnp.einsum("xmd,xdf->xmf", rows, held_in, preferred_element_type=jnp.float32)
     hidden = gelu_exact(pre).astype(jnp.bfloat16)
-    grad_rows = sort_rows(grad_blocks, exp_local, crossed, rows)
+    output = jnp.einsum("xmf,xfd->xmd", hidden, held_out, preferred_element_type=jnp.float32)
     hidden_grad = jnp.einsum(
         "xmd,xfd->xmf", grad_rows, held_out, preferred_element_type=jnp.float32
     )
@@ -428,11 +398,9 @@
     row_grad = jnp.einsum(
         "xmf,xdf->xmd", pre_grad, held_in, preferred_element_type=jnp.float32
     )
-    back_blocks = unsort_rows(row_grad.astype(jnp.bfloat16), straight)
-    output = jnp.einsum("xmf,xfd->xmd", hidden, held_out, preferred_element_type=jnp.float32)
-    out_blocks = unsort_rows(output.astype(jnp.bfloat16), crossed)
-
-    parts = 2
+    blocks = unsort_rows(output.astype(jnp.bfloat16), row_grad.astype(jnp.bfloat16), steps)
+
+    parts = 1
     work = [
         (kernel, left, right, shape, expert, part)
         for kernel, left, right, shape in (
@@ -459,22 +427,14 @@
             return small_call(add_kernel, "add", after, [block, arrived], [2 * count])
         return small_call(add_split_kernel, "add_split", after, [block, arrived], [count] * 2)
 
-    back_sum, out_sum = back_blocks[-1:], out_blocks[-1:]
-    back_arrived, out_arrived = swap(back_sum[0], True), swap(out_sum[0], False)
+    total = blocks[-1:]
     for step in range(steps - 1, 0, -1):
-        ready = next_piece(out_sum[-1])
-        back_sum = add_step([ready], back_blocks[step - 1], back_arrived, step)
-        back_arrived = swap(back_sum[-1], step % 2 == 0)
-        if step > 1:
-            ready = next_piece(back_sum[-1])
-        out_sum = add_step([ready], out_blocks[step - 1], out_arrived, step)
-        out_arrived = swap(out_sum[-1], step % 2 == 1)
+        arrived = swap(total[-1], step)
+        ready = next_piece(total[-1]) if len(work) > 1 else total[-1]
+        total = add_step([ready], blocks[step - 1], arrived, step)
+    arrived = swap(total[-1], 0)
     joined = small_call(
-        functools.partial(join_kernel, groups=n_expert),
-        "join",
-        [next_piece(out_sum[-1])],
-        [out_sum[0], out_arrived, back_sum[0], back_arrived],
-        [2 * exp_local * CAP] * n_expert,
+        join_kernel, "join", [], [total[0], arrived], [2 * exp_local * CAP] * n_expert
     )
     while work:
         next_piece(joined[0])

time: 80.6 us -> 93.3 us (1.16)
  waiting for transfers between devices: 12.6 us -> 41.6 us
  starting transfers between devices: 28.4 us -> 17.9 us
  Pallas kernels: 31.2 us -> 25.6 us
    ppermute x16 -> x8, waiting for transfers between devices: 11.8 us -> 40.7 us  [swap(): return lax.ppermute(block, ('expert',) + DP, pairs)]
    ppermute x16 -> x8, starting transfers between devices: 23.4 us -> 12.9 us  [swap(): return lax.ppermute(block, ('expert',) + DP, pairs)]
    pallas_call x8 -> x4, Pallas kernels: 19.5 us -> 14.3 us  [weight_gradient(): pl.pallas_call(functools.partial(kernel, skip=len(after), expert=expert,...]
  transfers between devices with their start and end apart: 22 -> 14, of which waited for: 11 -> 9; matrix products, arithmetic and copies ran while one was open for 3% -> 0% of each run, Pallas kernels for 33% -> 22%
where the time goes in v2:
time: 93.3 us; the launch traced here: 93.2 us
  waiting for transfers between devices  41.6 us (45%)
  Pallas kernels  25.6 us (27%)
  starting transfers between devices  17.9 us (19%)
  matrix products  7.26 us (8%)
    ppermute x8, waiting for transfers between devices, swap(): return lax.ppermute(block, ('expert',) + DP, pairs)  40.7 us
    pallas_call x4, Pallas kernels, weight_gradient(): pl.pallas_call(functools.partial(kernel, skip=len(after), expert=expert,...  14.3 us
    ppermute x8, starting transfers between devices, swap(): return lax.ppermute(block, ('expert',) + DP, pairs)  12.9 us
    pallas_call x2, Pallas kernels, hold(): pl.pallas_call(hold_kernel, in_specs=[pl.BlockSpec(memory_space=pl.ANY)]...  6.04 us
    ppermute x6, starting transfers between devices, expert_swap(): lax.ppermute(blocks[k], 'expert', [(i, i ^ k) for i in range(size)])  5.02 us
    dot_general x1, matrix products, per_device(): jnp.einsum('xmd,xfd->xmf', grad_rows, held_out, preferred_element_type=jn...  2.36 us
    dot_general x1, matrix products, per_device(): jnp.einsum('xmf,xdf->xmd', pre_grad, held_in, preferred_element_type=jnp....  2.33 us
    pallas_call x1, Pallas kernels, prepare(): pl.pallas_call(functools.partial(prepare_kernel, exp_local=exp_local), ou...  2.12 us
  transfers between devices with their start and end apart: 14, of which 9 were waited for; matrix products, arithmetic and copies ran while one was open for 0% of the time, Pallas kernels for 22%

profile of v2, /device:TPU:0, one launch (start us, length us, event | category | flops | bytes accessed | tf_op | source)
XLA Modules:
  0.0 93.2 jit_solution(15058680195213070767)
XLA Ops:
  0.6 2.1 %prepare.1 = (bf16[16,1664]{1,0:T(8,128)(2,1)S(1)}, bf16[16,1664]{1,0:T(8,128)(2,1)}, bf16[16,1664]{1,0:T(8,128)(2,1)}, bf16[16,1664]{1,0:T(8,128)(2,1)}) custom-call(s32[2,128]{1,0:T(2,128)} %bitcast.13, s32[2,128]{1,0:T(2,128)} %bitcast.15, s32[2,128]{1,0:T(2,128)} %bitcast.17, f32[2,128]{1,0:T(2,128)} %bitcast.19, bf16[128,1664]{1,0:T(8,128)(2,1)} %tokens_ref.1, ...), custom_call_target="tpu_custom_call" | custom-call | tf_op jit(solution)/shard_map/prepare/pallas_call | solution.py:195
  2.8 0.4 collective-permute-start
  3.2 2.5 %collective-permute-start.1 = (bf16[16,1664]{1,0:T(8,128)(2,1)}, bf16[16,1664]{1,0:T(8,128)(2,1)S(1)}, u32[]{:S(2)}, u32[]{:S(2)}) collective-permute-start(bf16[16,1664]{1,0:T(8,128)(2,1)} %get-tuple-element.38), channel_id=1, source_target_pairs={{0,16},{8,24},{16,0},{24,8},{1,17},{9,25},{17,1},{25,9},{2,18},{10... | collective-permute-start | bytes 159752 | tf_op jit(solution)/shard_map/ppermute | solution.py:362
  5.7 0.1 collective-permute-start.2
  5.8 3.0 %hold.2 = (bf16[2,1664,1024]{2,1,0:T(8,128)(2,1)S(1)}, f32[8,128]{1,0:T(8,128)S(1)}) custom-call(bf16[2,1664,1024]{2,1,0:T(8,128)(2,1)} %refs_0_.1), custom_call_target="tpu_custom_call" | custom-call | bytes 13631488 | tf_op jit(solution)/shard_map/hold/pallas_call | solution.py:233
  8.9 0.0 collective-permute-done.refs_2_
  8.9 0.0 collective-permute-done.1.refs_3_
  8.9 0.8 collective-permute-done.2.refs_4_
  9.7 1.6 %collective-permute-start.3 = (bf16[64,1664]{1,0:T(8,128)(2,1)S(1)}, bf16[64,1664]{1,0:T(8,128)(2,1)S(1)}, u32[]{:S(2)}, u32[]{:S(2)}) collective-permute-start(bf16[64,1664]{1,0:T(8,128)(2,1)S(1)} %stack.1.refs_0_), channel_id=1, source_target_pairs={{0,2},{2,0},{4,6},{6,4},{7,5},{5,7},{3,1},{1,3},{8,9},{10,12},{12,... | collective-permute-start | bytes 638984 | tf_op jit(solution)/shard_map/ppermute | solution.py:356
  11.4 4.3 %collective-permute-done.3.refs_1_ = bf16[64,1664]{1,0:T(8,128)(2,1)S(1)} collective-permute-done((bf16[64,1664]{1,0:T(8,128)(2,1)S(1)}, bf16[64,1664]{1,0:T(8,128)(2,1)S(1)}, u32[]{:S(2)}, u32[]{:S(2)}) %collective-permute-start.3) | collective-permute-done | bytes 213024 | tf_op jit(solution)/shard_map/ppermute | solution.py:356
  15.7 1.6 %collective-permute-start.4 = (bf16[128,1664]{1,0:T(8,128)(2,1)S(1)}, bf16[128,1664]{1,0:T(8,128)(2,1)S(1)}, u32[]{:S(2)}, u32[]{:S(2)}) collective-permute-start(bf16[128,1664]{1,0:T(8,128)(2,1)S(1)} %pair.1.refs_0_), channel_id=1, source_target_pairs={{0,1},{2,4},{4,2},{6,7},{7,6},{5,3},{3,5},{1,0},{8,10},{10,8},{12,... | collective-permute-start | bytes 1277960 | tf_op jit(solution)/shard_map/ppermute | solution.py:356
  17.3 3.0 %hold.3 = (bf16[2,1024,1664]{2,1,0:T(8,128)(2,1)S(1)}, f32[8,128]{1,0:T(8,128)S(1)}) custom-call(bf16[128,1664]{1,0:T(8,128)(2,1)S(1)} %pair.1.refs_0_, bf16[2,1024,1664]{2,1,0:T(8,128)(2,1)} %refs_1_.1), custom_call_target="tpu_custom_call" | custom-call | bytes 13631488 | tf_op jit(solution)/shard_map/hold/pallas_call | solution.py:233
  20.3 3.6 %collective-permute-done.4.refs_1_ = bf16[128,1664]{1,0:T(8,128)(2,1)S(1)} collective-permute-done((bf16[128,1664]{1,0:T(8,128)(2,1)S(1)}, bf16[128,1664]{1,0:T(8,128)(2,1)S(1)}, u32[]{:S(2)}, u32[]{:S(2)}) %collective-permute-start.4) | collective-permute-done | bytes 426016 | tf_op jit(solution)/shard_map/ppermute | solution.py:356
  23.9 1.6 %collective-permute-start.5 = (bf16[128,1664]{1,0:T(8,128)(2,1)S(1)}, bf16[128,1664]{1,0:T(8,128)(2,1)S(1)}, u32[]{:S(2)}, u32[]{:S(2)}) collective-permute-start(bf16[128,1664]{1,0:T(8,128)(2,1)S(1)} %pass.1.refs_1_), channel_id=1, source_target_pairs={{0,2},{2,0},{4,6},{6,4},{7,5},{5,7},{3,1},{1,3},{8,9},{10,12},{12,... | collective-permute-start | bytes 1277960 | tf_op jit(solution)/shard_map/ppermute | solution.py:356
  25.5 6.5 %collective-permute-done.5.refs_2_ = bf16[128,1664]{1,0:T(8,128)(2,1)S(1)} collective-permute-done((bf16[128,1664]{1,0:T(8,128)(2,1)S(1)}, bf16[128,1664]{1,0:T(8,128)(2,1)S(1)}, u32[]{:S(2)}, u32[]{:S(2)}) %collective-permute-start.5) | collective-permute-done | bytes 426016 | tf_op jit(solution)/shard_map/ppermute | solution.py:356
  32.1 1.5 %collective-permute-start.6 = (bf16[128,1664]{1,0:T(8,128)(2,1)S(1)}, bf16[128,1664]{1,0:T(8,128)(2,1)S(1)}, u32[]{:S(2)}, u32[]{:S(2)}) collective-permute-start(bf16[128,1664]{1,0:T(8,128)(2,1)S(1)} %collective-permute-done.5.refs_2_), channel_id=1, source_target_pairs={{0,1},{2,4},{4,2},{6,7},{7,6},{5,3},{3,5},{1,0},{8,10},{10,8},{12,... | collective-permute-start | bytes 1277960 | tf_op jit(solution)/shard_map/ppermute | solution.py:356
  33.6 6.6 %collective-permute-done.6.refs_3_ = bf16[128,1664]{1,0:T(8,128)(2,1)S(1)} collective-permute-done((bf16[128,1664]{1,0:T(8,128)(2,1)S(1)}, bf16[128,1664]{1,0:T(8,128)(2,1)S(1)}, u32[]{:S(2)}, u32[]{:S(2)}) %collective-permute-start.6) | collective-permute-done | bytes 426016 | tf_op jit(solution)/shard_map/ppermute | solution.py:356
  40.2 0.6 sort_rows.1
  40.8 1.4 %multiply_convert_fusion = (bf16[2,128,1024]{2,1,0:T(8,128)(2,1)S(1)}, f32[2,128,1024]{2,1,0:T(8,128)S(1)}) fusion(bf16[2,128,1664]{2,1,0:T(8,128)(2,1)S(1)} %get-tuple-element.41.refs_2_, bf16[2,1664,1024]{2,1,0:T(8,128)(2,1)S(1)} %get-tuple-element.42), kind=kOutput, calls=%fused_computation.9 | convolution fusion | flops 873725952 | bytes 9240576 | tf_op jit(solution)/shard_map/xmd,xdf->xmf/dot_general | solution.py:391
  42.2 1.2 %convolution_convert_fusion.1.refs_0_ = bf16[2,128,1664]{2,1,0:T(8,128)(2,1)S(1)} fusion(bf16[2,128,1024]{2,1,0:T(8,128)(2,1)S(1)} %get-tuple-element.65.refs_1_, bf16[2,1024,1664]{2,1,0:T(8,128)(2,1)S(1)} %get-tuple-element.43), kind=kOutput, calls=%fused_computation.1 | convolution fusion | flops 872841216 | bytes 8192000 | tf_op jit(solution)/shard_map/xmf,xfd->xmd/dot_general | solution.py:393
  43.4 2.4 %fusion.refs_1_ = bf16[2,128,1024]{2,1,0:T(8,128)(2,1)S(1)} fusion(bf16[2,128,1664]{2,1,0:T(8,128)(2,1)S(1)} %get-tuple-element.44.refs_2_, bf16[2,1024,1664]{2,1,0:T(8,128)(2,1)S(1)} %get-tuple-element.43, f32[2,128,1024]{2,1,0:T(8,128)S(1)} %get-tuple-element.66), kind=kOutput, calls=%fused_computation.4 | convolution fusion | flops 875036672 | bytes 9240576 | tf_op jit(solution)/shard_map/xmd,xfd->xmf/dot_general | solution.py:394
  45.8 2.3 %convolution_convert_fusion.refs_1_ = bf16[2,128,1664]{2,1,0:T(8,128)(2,1)S(1)} fusion(bf16[2,128,1024]{2,1,0:T(8,128)(2,1)S(1)} %fusion.refs_1_, bf16[2,1664,1024]{2,1,0:T(8,128)(2,1)S(1)} %get-tuple-element.42), kind=kOutput, calls=%fused_computation | convolution fusion | flops 872841216 | bytes 8192000 | tf_op jit(solution)/shard_map/xmf,xdf->xmd/dot_general | solution.py:398
  48.1 0.6 unsort_rows.1
  48.7 1.6 %collective-permute-start.7 = (bf16[128,1664]{1,0:T(8,128)(2,1)S(1)}, bf16[128,1664]{1,0:T(8,128)(2,1)S(1)}, u32[]{:S(2)}, u32[]{:S(2)}) collective-permute-start(bf16[128,1664]{1,0:T(8,128)(2,1)S(1)} %get-tuple-element.45.refs_0_), channel_id=1, source_target_pairs={{0,1},{2,4},{4,2},{6,7},{7,6},{5,3},{3,5},{1,0},{8,10},{10,8},{12,... | collective-permute-start | bytes 1277960 | tf_op jit(solution)/shard_map/ppermute | solution.py:356
  50.3 3.3 %w_out_grad_kernel.2 = (f32[2,1024,1664]{2,1,0:T(8,128)}, f32[8,128]{1,0:T(8,128)S(1)}) custom-call(bf16[128,1664]{1,0:T(8,128)(2,1)S(1)} %get-tuple-element.45.refs_0_, bf16[2,128,1024]{2,1,0:T(8,128)(2,1)S(1)} %get-tuple-element.65.refs_1_, bf16[2,128,1664]{2,1,0:T(8,128)(2,1)S(1)} %get-tuple-element.44.refs_2_), custom_call_target="tpu_custom_call" | custom-call | flops 436207616 | bytes 6815744 | tf_op jit(solution)/shard_map/w_out_grad_kernel/pallas_call | solution.py:254
  53.6 4.6 %collective-permute-done.7.refs_2_ = bf16[128,1664]{1,0:T(8,128)(2,1)S(1)} collective-permute-done((bf16[128,1664]{1,0:T(8,128)(2,1)S(1)}, bf16[128,1664]{1,0:T(8,128)(2,1)S(1)}, u32[]{:S(2)}, u32[]{:S(2)}) %collective-permute-start.7) | collective-permute-done | bytes 426016 | tf_op jit(solution)/shard_map/ppermute | solution.py:356
  58.2 0.1 add.19.refs_0_
  58.3 1.7 %collective-permute-start.8 = (bf16[128,1664]{1,0:T(8,128)(2,1)S(1)}, bf16[128,1664]{1,0:T(8,128)(2,1)S(1)}, u32[]{:S(2)}, u32[]{:S(2)}) collective-permute-start(bf16[128,1664]{1,0:T(8,128)(2,1)S(1)} %add.19.refs_0_), channel_id=1, source_target_pairs={{0,2},{2,0},{4,6},{6,4},{7,5},{5,7},{3,1},{1,3},{8,9},{10,12},{12,... | collective-permute-start | bytes 1277960 | tf_op jit(solution)/shard_map/ppermute | solution.py:356
  60.0 3.3 %w_out_grad_kernel.3 = (f32[2,1024,1664]{2,1,0:T(8,128)}, f32[8,128]{1,0:T(8,128)S(1)}) custom-call(bf16[128,1664]{1,0:T(8,128)(2,1)S(1)} %add.19.refs_0_, bf16[2,128,1024]{2,1,0:T(8,128)(2,1)S(1)} %get-tuple-element.65.refs_1_, bf16[2,128,1664]{2,1,0:T(8,128)(2,1)S(1)} %get-tuple-element.44.refs_2_, ...), custom_call_target="tpu_custom_call", output_to_operand_aliasing={{0}: (3, {})} | custom-call | flops 436207616 | bytes 6815744 | tf_op jit(solution)/shard_map/w_out_grad_kernel/pallas_call | solution.py:254
  63.3 5.6 %collective-permute-done.8.refs_2_ = bf16[128,1664]{1,0:T(8,128)(2,1)S(1)} collective-permute-done((bf16[128,1664]{1,0:T(8,128)(2,1)S(1)}, bf16[128,1664]{1,0:T(8,128)(2,1)S(1)}, u32[]{:S(2)}, u32[]{:S(2)}) %collective-permute-start.8) | collective-permute-done | bytes 426016 | tf_op jit(solution)/shard_map/ppermute | solution.py:356
  68.9 0.1 add.20.refs_0_
  69.0 1.6 %collective-permute-start.9 = (bf16[128,1664]{1,0:T(8,128)(2,1)S(1)}, bf16[128,1664]{1,0:T(8,128)(2,1)S(1)}, u32[]{:S(2)}, u32[]{:S(2)}) collective-permute-start(bf16[128,1664]{1,0:T(8,128)(2,1)S(1)} %add.20.refs_0_), channel_id=1, source_target_pairs={{0,1},{2,4},{4,2},{6,7},{7,6},{5,3},{3,5},{1,0},{8,10},{10,8},{12,... | collective-permute-start | bytes 1277960 | tf_op jit(solution)/shard_map/ppermute | solution.py:356
  70.5 3.5 %w_in_grad_kernel.2 = (f32[2,1664,1024]{2,1,0:T(8,128)}, f32[8,128]{1,0:T(8,128)S(1)}) custom-call(bf16[128,1664]{1,0:T(8,128)(2,1)S(1)} %add.20.refs_0_, bf16[2,128,1024]{2,1,0:T(8,128)(2,1)S(1)} %fusion.refs_1_, bf16[2,128,1664]{2,1,0:T(8,128)(2,1)S(1)} %get-tuple-element.41.refs_2_), custom_call_target="tpu_custom_call" | custom-call | flops 436207616 | bytes 6815744 | tf_op jit(solution)/shard_map/w_in_grad_kernel/pallas_call | solution.py:254
  74.1 5.4 %collective-permute-done.9.refs_2_ = bf16[128,1664]{1,0:T(8,128)(2,1)S(1)} collective-permute-done((bf16[128,1664]{1,0:T(8,128)(2,1)S(1)}, bf16[128,1664]{1,0:T(8,128)(2,1)S(1)}, u32[]{:S(2)}, u32[]{:S(2)}) %collective-permute-start.9) | collective-permute-done | bytes 426016 | tf_op jit(solution)/shard_map/ppermute | solution.py:356
  79.4 0.1 add_split.1
  79.5 1.7 %collective-permute-start.10 = (bf16[64,1664]{1,0:T(8,128)(2,1)S(1)}, bf16[64,1664]{1,0:T(8,128)(2,1)S(1)}, u32[]{:S(2)}, u32[]{:S(2)}) collective-permute-start(bf16[64,1664]{1,0:T(8,128)(2,1)S(1)} %get-tuple-element.54), channel_id=1, source_target_pairs={{0,2},{2,0},{4,6},{6,4},{7,5},{5,7},{3,1},{1,3},{8,9},{10,12},{12,... | collective-permute-start | bytes 638984 | tf_op jit(solution)/shard_map/ppermute | solution.py:356
  81.2 4.2 %collective-permute-done.10.right_ref = bf16[64,1664]{1,0:T(8,128)(2,1)S(1)} collective-permute-done((bf16[64,1664]{1,0:T(8,128)(2,1)S(1)}, bf16[64,1664]{1,0:T(8,128)(2,1)S(1)}, u32[]{:S(2)}, u32[]{:S(2)}) %collective-permute-start.10) | collective-permute-done | bytes 213024 | tf_op jit(solution)/shard_map/ppermute | solution.py:356
  85.5 0.1 join.1
  85.5 0.1 collective-permute-start.11
  85.6 1.2 %collective-permute-start.12 = (bf16[16,1664]{1,0:T(8,128)(2,1)S(1)}, bf16[16,1664]{1,0:T(8,128)(2,1)S(1)}, u32[]{:S(2)}, u32[]{:S(2)}) collective-permute-start(bf16[16,1664]{1,0:T(8,128)(2,1)S(1)} %get-tuple-element.57), channel_id=1, source_target_pairs={{0,16},{8,24},{16,0},{24,8},{1,17},{9,25},{17,1},{25,9},{2,18},{10... | collective-permute-start | bytes 159752 | tf_op jit(solution)/shard_map/ppermute | solution.py:362
  86.7 0.7 collective-permute-start.13
  87.5 0.0 copy-start.4
  87.5 4.1 %w_in_grad_kernel.3 = (f32[2,1664,1024]{2,1,0:T(8,128)}, f32[8,128]{1,0:T(8,128)}) custom-call(bf16[16,1664]{1,0:T(8,128)(2,1)S(1)} %get-tuple-element.55.refs_0_, bf16[2,128,1024]{2,1,0:T(8,128)(2,1)S(1)} %fusion.refs_1_, bf16[2,128,1664]{2,1,0:T(8,128)(2,1)S(1)} %get-tuple-element.41.refs_2_, ...), custom_call_target="tpu_custom_call", output_to_operand_aliasing={{0}: (3, {})} | custom-call | flops 436207616 | bytes 6815744 | tf_op jit(solution)/shard_map/w_in_grad_kernel/pallas_call | solution.py:254
  91.6 0.0 collective-permute-done.11.refs_1_
  91.6 0.0 collective-permute-done.12.refs_2_
  91.6 0.0 collective-permute-done.13.refs_3_
  91.6 0.0 copy-done
  91.7 1.5 %finish.1 = (bf16[128,1664]{1,0:T(8,128)(2,1)}, bf16[128,1664]{1,0:T(8,128)(2,1)}, f32[2,128]{1,0:T(2,128)}) custom-call(s32[2,128]{1,0:T(2,128)S(1)} %bitcast.14, s32[2,128]{1,0:T(2,128)S(1)} %bitcast.16, s32[2,128]{1,0:T(2,128)S(1)} %bitcast.18, f32[2,128]{1,0:T(2,128)S(1)} %bitcast.20, bf16[128,1664]{1,0:T(8,128)(2,1)S(1)} %copy-done, ...), custom_call_target="tpu_custom_call" | custom-call | tf_op jit(solution)/shard_map/finish/pallas_call | solution.py:206
  (11 shorter events, 0.1 us)
Async XLA Ops:
  2.8 6.1 %collective-permute-start = (bf16[16,1664]{1,0:T(8,128)(2,1)}, bf16[16,1664]{1,0:T(8,128)(2,1)S(1)}, u32[]{:S(2)}, u32[]{:S(2)}) collective-permute-start(bf16[16,1664]{1,0:T(8,128)(2,1)} %get-tuple-element.37), channel_id=1, source_target_pairs={{0,8},{8,0},{16,24},{24,16},{1,9},{9,1},{17,25},{25,17},{2,10},{10... | collective-permute-start | bytes 159752 | tf_op jit(solution)/shard_map/ppermute | solution.py:362
  3.2 5.7 %collective-permute-start.1 = (bf16[16,1664]{1,0:T(8,128)(2,1)}, bf16[16,1664]{1,0:T(8,128)(2,1)S(1)}, u32[]{:S(2)}, u32[]{:S(2)}) collective-permute-start(bf16[16,1664]{1,0:T(8,128)(2,1)} %get-tuple-element.38), channel_id=1, source_target_pairs={{0,16},{8,24},{16,0},{24,8},{1,17},{9,25},{17,1},{25,9},{2,18},{10... | collective-permute-start | bytes 159752 | tf_op jit(solution)/shard_map/ppermute | solution.py:362
  5.7 4.0 %collective-permute-start.2 = (bf16[16,1664]{1,0:T(8,128)(2,1)}, bf16[16,1664]{1,0:T(8,128)(2,1)S(1)}, u32[]{:S(2)}, u32[]{:S(2)}) collective-permute-start(bf16[16,1664]{1,0:T(8,128)(2,1)} %get-tuple-element.39), channel_id=1, source_target_pairs={{0,24},{8,16},{16,8},{24,0},{1,25},{9,17},{17,9},{25,1},{2,26},{10... | collective-permute-start | bytes 159752 | tf_op jit(solution)/shard_map/ppermute | solution.py:362
  9.7 5.9 %collective-permute-start.3 = (bf16[64,1664]{1,0:T(8,128)(2,1)S(1)}, bf16[64,1664]{1,0:T(8,128)(2,1)S(1)}, u32[]{:S(2)}, u32[]{:S(2)}) collective-permute-start(bf16[64,1664]{1,0:T(8,128)(2,1)S(1)} %stack.1.refs_0_), channel_id=1, source_target_pairs={{0,2},{2,0},{4,6},{6,4},{7,5},{5,7},{3,1},{1,3},{8,9},{10,12},{12,... | collective-permute-start | bytes 638984 | tf_op jit(solution)/shard_map/ppermute | solution.py:356
  15.7 8.2 %collective-permute-start.4 = (bf16[128,1664]{1,0:T(8,128)(2,1)S(1)}, bf16[128,1664]{1,0:T(8,128)(2,1)S(1)}, u32[]{:S(2)}, u32[]{:S(2)}) collective-permute-start(bf16[128,1664]{1,0:T(8,128)(2,1)S(1)} %pair.1.refs_0_), channel_id=1, source_target_pairs={{0,1},{2,4},{4,2},{6,7},{7,6},{5,3},{3,5},{1,0},{8,10},{10,8},{12,... | collective-permute-start | bytes 1277960 | tf_op jit(solution)/shard_map/ppermute | solution.py:356
  23.9 8.2 %collective-permute-start.5 = (bf16[128,1664]{1,0:T(8,128)(2,1)S(1)}, bf16[128,1664]{1,0:T(8,128)(2,1)S(1)}, u32[]{:S(2)}, u32[]{:S(2)}) collective-permute-start(bf16[128,1664]{1,0:T(8,128)(2,1)S(1)} %pass.1.refs_1_), channel_id=1, source_target_pairs={{0,2},{2,0},{4,6},{6,4},{7,5},{5,7},{3,1},{1,3},{8,9},{10,12},{12,... | collective-permute-start | bytes 1277960 | tf_op jit(solution)/shard_map/ppermute | solution.py:356
  32.1 8.1 %collective-permute-start.6 = (bf16[128,1664]{1,0:T(8,128)(2,1)S(1)}, bf16[128,1664]{1,0:T(8,128)(2,1)S(1)}, u32[]{:S(2)}, u32[]{:S(2)}) collective-permute-start(bf16[128,1664]{1,0:T(8,128)(2,1)S(1)} %collective-permute-done.5.refs_2_), channel_id=1, source_target_pairs={{0,1},{2,4},{4,2},{6,7},{7,6},{5,3},{3,5},{1,0},{8,10},{10,8},{12,... | collective-permute-start | bytes 1277960 | tf_op jit(solution)/shard_map/ppermute | solution.py:356
  48.7 9.5 %collective-permute-start.7 = (bf16[128,1664]{1,0:T(8,128)(2,1)S(1)}, bf16[128,1664]{1,0:T(8,128)(2,1)S(1)}, u32[]{:S(2)}, u32[]{:S(2)}) collective-permute-start(bf16[128,1664]{1,0:T(8,128)(2,1)S(1)} %get-tuple-element.45.refs_0_), channel_id=1, source_target_pairs={{0,1},{2,4},{4,2},{6,7},{7,6},{5,3},{3,5},{1,0},{8,10},{10,8},{12,... | collective-permute-start | bytes 1277960 | tf_op jit(solution)/shard_map/ppermute | solution.py:356
  58.3 10.5 %collective-permute-start.8 = (bf16[128,1664]{1,0:T(8,128)(2,1)S(1)}, bf16[128,1664]{1,0:T(8,128)(2,1)S(1)}, u32[]{:S(2)}, u32[]{:S(2)}) collective-permute-start(bf16[128,1664]{1,0:T(8,128)(2,1)S(1)} %add.19.refs_0_), channel_id=1, source_target_pairs={{0,2},{2,0},{4,6},{6,4},{7,5},{5,7},{3,1},{1,3},{8,9},{10,12},{12,... | collective-permute-start | bytes 1277960 | tf_op jit(solution)/shard_map/ppermute | solution.py:356
  69.0 10.5 %collective-permute-start.9 = (bf16[128,1664]{1,0:T(8,128)(2,1)S(1)}, bf16[128,1664]{1,0:T(8,128)(2,1)S(1)}, u32[]{:S(2)}, u32[]{:S(2)}) collective-permute-start(bf16[128,1664]{1,0:T(8,128)(2,1)S(1)} %add.20.refs_0_), channel_id=1, source_target_pairs={{0,1},{2,4},{4,2},{6,7},{7,6},{5,3},{3,5},{1,0},{8,10},{10,8},{12,... | collective-permute-start | bytes 1277960 | tf_op jit(solution)/shard_map/ppermute | solution.py:356
  79.5 5.9 %collective-permute-start.10 = (bf16[64,1664]{1,0:T(8,128)(2,1)S(1)}, bf16[64,1664]{1,0:T(8,128)(2,1)S(1)}, u32[]{:S(2)}, u32[]{:S(2)}) collective-permute-start(bf16[64,1664]{1,0:T(8,128)(2,1)S(1)} %get-tuple-element.54), channel_id=1, source_target_pairs={{0,2},{2,0},{4,6},{6,4},{7,5},{5,7},{3,1},{1,3},{8,9},{10,12},{12,... | collective-permute-start | bytes 638984 | tf_op jit(solution)/shard_map/ppermute | solution.py:356
  85.5 6.1 %collective-permute-start.11 = (bf16[16,1664]{1,0:T(8,128)(2,1)S(1)}, bf16[16,1664]{1,0:T(8,128)(2,1)S(1)}, u32[]{:S(2)}, u32[]{:S(2)}) collective-permute-start(bf16[16,1664]{1,0:T(8,128)(2,1)S(1)} %get-tuple-element.56), channel_id=1, source_target_pairs={{0,8},{8,0},{16,24},{24,16},{1,9},{9,1},{17,25},{25,17},{2,10},{10... | collective-permute-start | bytes 159752 | tf_op jit(solution)/shard_map/ppermute | solution.py:362
  85.6 6.0 %collective-permute-start.12 = (bf16[16,1664]{1,0:T(8,128)(2,1)S(1)}, bf16[16,1664]{1,0:T(8,128)(2,1)S(1)}, u32[]{:S(2)}, u32[]{:S(2)}) collective-permute-start(bf16[16,1664]{1,0:T(8,128)(2,1)S(1)} %get-tuple-element.57), channel_id=1, source_target_pairs={{0,16},{8,24},{16,0},{24,8},{1,17},{9,25},{17,1},{25,9},{2,18},{10... | collective-permute-start | bytes 159752 | tf_op jit(solution)/shard_map/ppermute | solution.py:362
  86.7 4.9 %collective-permute-start.13 = (bf16[16,1664]{1,0:T(8,128)(2,1)S(1)}, bf16[16,1664]{1,0:T(8,128)(2,1)S(1)}, u32[]{:S(2)}, u32[]{:S(2)}) collective-permute-start(bf16[16,1664]{1,0:T(8,128)(2,1)S(1)} %get-tuple-element.58), channel_id=1, source_target_pairs={{0,24},{8,16},{16,8},{24,0},{1,25},{9,17},{17,9},{25,1},{2,26},{10... | collective-permute-start | bytes 159752 | tf_op jit(solution)/shard_map/ppermute | solution.py:362
  87.5 4.2 %copy-start = (bf16[128,1664]{1,0:T(8,128)(2,1)S(1)}, bf16[128,1664]{1,0:T(8,128)(2,1)}, u32[]{:S(2)}) copy-start(bf16[128,1664]{1,0:T(8,128)(2,1)} %out_grad_ref.3) | copy-start | bytes 1277956
  87.5 4.2 %copy-start.1 = (s32[128,2]{0,1:T(2,128)S(1)}, s32[128,2]{0,1:T(2,128)}, u32[]{:S(2)}) copy-start(s32[128,2]{0,1:T(2,128)} %param.9) | copy-start | bytes 3076
  87.5 4.2 %copy-start.2 = (s32[128,2]{0,1:T(2,128)S(1)}, s32[128,2]{0,1:T(2,128)}, u32[]{:S(2)}) copy-start(s32[128,2]{0,1:T(2,128)} %param.10) | copy-start | bytes 3076
  87.5 4.2 %copy-start.3 = (s32[128,2]{0,1:T(2,128)S(1)}, s32[128,2]{0,1:T(2,128)}, u32[]{:S(2)}) copy-start(s32[128,2]{0,1:T(2,128)} %param.11) | copy-start | bytes 3076
  87.5 4.2 %copy-start.4 = (f32[128,2]{0,1:T(2,128)S(1)}, f32[128,2]{0,1:T(2,128)}, u32[]{:S(2)}) copy-start(f32[128,2]{0,1:T(2,128)} %param.12) | copy-start | bytes 3076

commit v3 on v1

--- a/solution.py
+++ b/solution.py
@@ -254,7 +254,7 @@
     whole = pl.BlockSpec(memory_space=pltpu.VMEM)
     anywhere = pl.BlockSpec(memory_space=pl.ANY)
     width, units = rows.shape[2], hidden.shape[2] // parts
-    chunk = min(CHUNK, units)
+    chunk = min(CHUNK // 2 if kernel is w_out_grad_kernel else CHUNK, units)
     made = (units, width) if kernel is w_out_grad_kernel else (width, units)
     operands = (*after, hidden, rows) + (() if base is None else (base,))
     return pl.pallas_call(
@@ -291,21 +291,16 @@
                 out_ref[expert, at : at + part] = rows[i * part : (i + 1) * part]
 
 
-def unsort_kernel(in_ref, *blocks, places):
+def unsort_kernel(after_ref, in_ref, *blocks):
     experts = in_ref.shape[0]
     count = blocks[0].shape[0]
-    part = count // experts // 2
+    part = count // experts
     order = jnp.concatenate(
         [order_matrix(expert, experts, count) for expert in range(experts)], axis=0
     )
     for step, ref in enumerate(blocks):
         piece = jnp.concatenate(
-            [
-                in_ref[expert, at * part : (at + 1) * part]
-                for expert in range(experts)
-                for at in places[2 * step : 2 * step + 2]
-            ],
-            axis=0,
+            [in_ref[expert, step * part : (step + 1) * part] for expert in range(experts)], axis=0
         )
         ref[...] = contract(order, piece, 0, 0).astype(jnp.bfloat16)
 
@@ -330,17 +325,17 @@
     )(after, *blocks)
 
 
-def unsort_rows(rows, places):
+def unsort_rows(rows, steps, after):
     experts, count, width = rows.shape
-    steps = len(places) // 2
     block = experts * count // steps
     return pl.pallas_call(
-        functools.partial(unsort_kernel, places=places),
+        unsort_kernel,
+        in_specs=[pl.BlockSpec(memory_space=pl.ANY), pl.BlockSpec(memory_space=pltpu.VMEM)],
         out_shape=[jax.ShapeDtypeStruct((block, width), jnp.bfloat16)] * steps,
         compiler_params=params(count),
         cost_estimate=order_cost(experts * count, width),
         name="unsort_rows",
-    )(rows)
+    )(after, rows)
 
 
 DP = ("far", "near", "pair")
@@ -416,11 +411,12 @@
             (arrived,) = small_call(pass_kernel, "pass", [done_out], [arrived], [2 * count])
         row_blocks.append(arrived)
         grad_blocks.append(swap(grad_blocks[-1], step % 2 == 0))
-    straight, crossed = range(n_dp), regroup(n_dp)
-    rows = sort_rows(row_blocks, exp_local, straight, done_in)
+    rows = sort_rows(row_blocks, exp_local, range(n_dp), done_in)
     pre = jnp.einsum("xmd,xdf->xmf", rows, held_in, preferred_element_type=jnp.float32)
     hidden = gelu_exact(pre).astype(jnp.bfloat16)
-    grad_rows = sort_rows(grad_blocks, exp_local, crossed, rows)
+    output = jnp.einsum("xmf,xfd->xmd", hidden, held_out, preferred_element_type=jnp.float32)
+    out_blocks = unsort_rows(output.astype(jnp.bfloat16), steps, done_out)
+    grad_rows = sort_rows(grad_blocks, exp_local, regroup(n_dp), out_blocks[-1])
     hidden_grad = jnp.einsum(
         "xmd,xfd->xmf", grad_rows, held_out, preferred_element_type=jnp.float32
     )
@@ -428,11 +424,8 @@
     row_grad = jnp.einsum(
         "xmf,xdf->xmd", pre_grad, held_in, preferred_element_type=jnp.float32
     )
-    back_blocks = unsort_rows(row_grad.astype(jnp.bfloat16), straight)
-    output = jnp.einsum("xmf,xfd->xmd", hidden, held_out, preferred_element_type=jnp.float32)
-    out_blocks = unsort_rows(output.astype(jnp.bfloat16), crossed)
-
-    parts = 2
+
+    parts = 1
     work = [
         (kernel, left, right, shape, expert, part)
         for kernel, left, right, shape in (
@@ -459,20 +452,26 @@
             return small_call(add_kernel, "add", after, [block, arrived], [2 * count])
         return small_call(add_split_kernel, "add_split", after, [block, arrived], [count] * 2)
 
-    back_sum, out_sum = back_blocks[-1:], out_blocks[-1:]
-    back_arrived, out_arrived = swap(back_sum[0], True), swap(out_sum[0], False)
-    for step in range(steps - 1, 0, -1):
-        ready = next_piece(out_sum[-1])
-        back_sum = add_step([ready], back_blocks[step - 1], back_arrived, step)
-        back_arrived = swap(back_sum[-1], step % 2 == 0)
-        if step > 1:
-            ready = next_piece(back_sum[-1])
-        out_sum = add_step([ready], out_blocks[step - 1], out_arrived, step)
-        out_arrived = swap(out_sum[-1], step % 2 == 1)
+    last = steps - 1
+    out_sum = out_blocks[last:]
+    out_arrived = swap(out_sum[0], last % 2 == 1)
+    for step in range(last, 0, -1):
+        if step < last:
+            back_arrived = swap(back_sum[-1], step % 2 == 1)
+        ready = [next_piece(back_sum[-1])] if step == 1 < last else []
+        out_sum = add_step(ready, out_blocks[step - 1], out_arrived, step)
+        out_arrived = swap(out_sum[-1], step % 2 == 0)
+        if step == last:
+            back_blocks = unsort_rows(row_grad.astype(jnp.bfloat16), steps, out_sum[0])
+            back_sum = back_blocks[last:]
+            back_arrived = swap(back_sum[-1], step % 2 == 1)
+            ready = [next_piece(back_sum[-1])]
+        back_sum = add_step(ready, back_blocks[step - 1], back_arrived, step)
+    back_arrived = swap(back_sum[-1], False)
     joined = small_call(
         functools.partial(join_kernel, groups=n_expert),
         "join",
-        [next_piece(out_sum[-1])],
+        [next_piece(back_sum[-1])],
         [out_sum[0], out_arrived, back_sum[0], back_arrived],
         [2 * exp_local * CAP] * n_expert,
     )

time: 80.6 us -> 76.7 us (0.952)
  Pallas kernels: 31.2 us -> 25.7 us
  starting transfers between devices: 28.4 us -> 31.5 us
  waiting for transfers between devices: 12.6 us -> 11.1 us
    pallas_call x8 -> x4, Pallas kernels: 19.5 us -> 14 us  [weight_gradient(): pl.pallas_call(functools.partial(kernel, skip=len(after), expert=expert,...]
    ppermute x8, starting transfers between devices: 12.3 us -> 14.9 us  [swap(): return lax.ppermute(block, 'near', [(0, 1), (1, 0)])]
    ppermute x8, waiting for transfers between devices: 6.8 us -> 5.94 us  [swap(): return lax.ppermute(block, 'near', [(0, 1), (1, 0)])]
  transfers between devices with their start and end apart: 22 -> 22, of which waited for: 11 -> 12; matrix products, arithmetic and copies ran while one was open for 3% -> 9% of each run, Pallas kernels for 33% -> 28%
where the time goes in v3:
time: 76.7 us; the launch traced here: 76.5 us
  starting transfers between devices  31.5 us (41%)
  Pallas kernels  25.7 us (34%)
  waiting for transfers between devices  11.1 us (14%)
  matrix products  7.26 us (9%)
  between operations  0.92 us (1%)
    ppermute x8, starting transfers between devices, swap(): return lax.ppermute(block, 'near', [(0, 1), (1, 0)])  14.9 us
    pallas_call x4, Pallas kernels, weight_gradient(): pl.pallas_call(functools.partial(kernel, skip=len(after), expert=expert,...  14 us
    ppermute x8, starting transfers between devices, swap(): return lax.ppermute(block, DP, odd_edges(lax.axis_size(DP)))  11.7 us
    pallas_call x2, Pallas kernels, hold(): pl.pallas_call(hold_kernel, in_specs=[pl.BlockSpec(memory_space=pl.ANY)]...  6.04 us
    ppermute x8, waiting for transfers between devices, swap(): return lax.ppermute(block, 'near', [(0, 1), (1, 0)])  5.94 us
    ppermute x6, starting transfers between devices, expert_swap(): lax.ppermute(blocks[k], 'expert', [(i, i ^ k) for i in range(size)])  5.02 us
    ppermute x8, waiting for transfers between devices, swap(): return lax.ppermute(block, DP, odd_edges(lax.axis_size(DP)))  4.29 us
    dot_general x1, matrix products, per_device(): jnp.einsum('xmd,xfd->xmf', grad_rows, held_out, preferred_element_type=jn...  2.37 us
  transfers between devices with their start and end apart: 22, of which 12 were waited for; matrix products, arithmetic and copies ran while one was open for 9% of the time, Pallas kernels for 28%

profile of v3, /device:TPU:0, one launch (start us, length us, event | category | flops | bytes accessed | tf_op | source)
XLA Modules:
  0.0 76.5 jit_solution(15667912306051226676)
XLA Ops:
  0.6 2.1 %prepare.1 = (bf16[16,1664]{1,0:T(8,128)(2,1)S(1)}, bf16[16,1664]{1,0:T(8,128)(2,1)}, bf16[16,1664]{1,0:T(8,128)(2,1)}, bf16[16,1664]{1,0:T(8,128)(2,1)}) custom-call(s32[2,128]{1,0:T(2,128)} %bitcast.13, s32[2,128]{1,0:T(2,128)} %bitcast.15, s32[2,128]{1,0:T(2,128)} %bitcast.17, f32[2,128]{1,0:T(2,128)} %bitcast.19, bf16[128,1664]{1,0:T(8,128)(2,1)} %tokens_ref.1, ...), custom_call_target="tpu_custom_call" | custom-call | tf_op jit(solution)/shard_map/prepare/pallas_call | solution.py:201
  2.8 0.4 collective-permute-start
  3.2 2.5 %collective-permute-start.1 = (bf16[16,1664]{1,0:T(8,128)(2,1)}, bf16[16,1664]{1,0:T(8,128)(2,1)S(1)}, u32[]{:S(2)}, u32[]{:S(2)}) collective-permute-start(bf16[16,1664]{1,0:T(8,128)(2,1)} %get-tuple-element.44), channel_id=1, source_target_pairs={{0,16},{8,24},{16,0},{24,8},{1,17},{9,25},{17,1},{25,9},{2,18},{10... | collective-permute-start | bytes 159752 | tf_op jit(solution)/shard_map/ppermute | solution.py:383
  5.7 0.1 collective-permute-start.2
  5.8 3.0 %hold.2 = (bf16[2,1664,1024]{2,1,0:T(8,128)(2,1)S(1)}, f32[8,128]{1,0:T(8,128)S(1)}) custom-call(bf16[2,1664,1024]{2,1,0:T(8,128)(2,1)} %refs_0_.1), custom_call_target="tpu_custom_call" | custom-call | bytes 13631488 | tf_op jit(solution)/shard_map/hold/pallas_call | solution.py:239
  8.9 0.8 %collective-permute-done.2.refs_3_ = bf16[16,1664]{1,0:T(8,128)(2,1)S(1)} collective-permute-done((bf16[16,1664]{1,0:T(8,128)(2,1)}, bf16[16,1664]{1,0:T(8,128)(2,1)S(1)}, u32[]{:S(2)}, u32[]{:S(2)}) %collective-permute-start.2) | collective-permute-done | bytes 53280 | tf_op jit(solution)/shard_map/ppermute | solution.py:383
  9.7 1.6 %collective-permute-start.3 = (bf16[32,1664]{1,0:T(8,128)(2,1)S(1)}, bf16[32,1664]{1,0:T(8,128)(2,1)S(1)}, u32[]{:S(2)}, u32[]{:S(2)}) collective-permute-start(bf16[32,1664]{1,0:T(8,128)(2,1)S(1)} %get-tuple-element.46.refs_0_), channel_id=1, source_target_pairs={{0,1},{2,4},{4,2},{6,7},{7,6},{5,3},{3,5},{1,0},{8,9},{10,12},{12,... | collective-permute-start | bytes 319496 | tf_op jit(solution)/shard_map/ppermute | solution.py:376
  11.3 1.6 %collective-permute-start.4 = (bf16[32,1664]{1,0:T(8,128)(2,1)S(1)}, bf16[32,1664]{1,0:T(8,128)(2,1)S(1)}, u32[]{:S(2)}, u32[]{:S(2)}) collective-permute-start(bf16[32,1664]{1,0:T(8,128)(2,1)S(1)} %get-tuple-element.47.refs_1_), channel_id=1, source_target_pairs={{0,2},{2,0},{1,3},{3,1},{4,6},{6,4},{5,7},{7,5},{8,10},{10,8},{9,1... | collective-permute-start | bytes 319496 | tf_op jit(solution)/shard_map/ppermute | solution.py:377
  13.0 1.9 %collective-permute-done.3.refs_0_.refs_1_ = bf16[32,1664]{1,0:T(8,128)(2,1)S(1)} collective-permute-done((bf16[32,1664]{1,0:T(8,128)(2,1)S(1)}, bf16[32,1664]{1,0:T(8,128)(2,1)S(1)}, u32[]{:S(2)}, u32[]{:S(2)}) %collective-permute-start.3) | collective-permute-done | bytes 106528 | tf_op jit(solution)/shard_map/ppermute | solution.py:376
  14.8 1.2 %collective-permute-done.4.refs_2_ = bf16[32,1664]{1,0:T(8,128)(2,1)S(1)} collective-permute-done((bf16[32,1664]{1,0:T(8,128)(2,1)S(1)}, bf16[32,1664]{1,0:T(8,128)(2,1)S(1)}, u32[]{:S(2)}, u32[]{:S(2)}) %collective-permute-start.4) | collective-permute-done | bytes 106528 | tf_op jit(solution)/shard_map/ppermute | solution.py:377
  16.1 1.5 %collective-permute-start.5 = (bf16[64,1664]{1,0:T(8,128)(2,1)S(1)}, bf16[64,1664]{1,0:T(8,128)(2,1)S(1)}, u32[]{:S(2)}, u32[]{:S(2)}) collective-permute-start(bf16[64,1664]{1,0:T(8,128)(2,1)S(1)} %pair.2.refs_0_), channel_id=1, source_target_pairs={{0,1},{2,4},{4,2},{6,7},{7,6},{5,3},{3,5},{1,0},{8,9},{10,12},{12,... | collective-permute-start | bytes 638984 | tf_op jit(solution)/shard_map/ppermute | solution.py:376
  17.6 1.6 %collective-permute-start.9 = (bf16[64,1664]{1,0:T(8,128)(2,1)S(1)}, bf16[64,1664]{1,0:T(8,128)(2,1)S(1)}, u32[]{:S(2)}, u32[]{:S(2)}) collective-permute-start(bf16[64,1664]{1,0:T(8,128)(2,1)S(1)} %pair.3.refs_1_.refs_0_), channel_id=1, source_target_pairs={{0,2},{2,0},{1,3},{3,1},{4,6},{6,4},{5,7},{7,5},{8,10},{10,8},{9,1... | collective-permute-start | bytes 638984 | tf_op jit(solution)/shard_map/ppermute | solution.py:377
  19.2 3.0 %hold.3 = (bf16[2,1024,1664]{2,1,0:T(8,128)(2,1)S(1)}, f32[8,128]{1,0:T(8,128)S(1)}) custom-call(bf16[64,1664]{1,0:T(8,128)(2,1)S(1)} %pair.2.refs_0_, bf16[64,1664]{1,0:T(8,128)(2,1)S(1)} %pair.3.refs_1_.refs_0_, bf16[2,1024,1664]{2,1,0:T(8,128)(2,1)} %refs_2_.1), custom_call_target="tpu_custom_call" | custom-call | bytes 13631488 | tf_op jit(solution)/shard_map/hold/pallas_call | solution.py:239
  22.3 1.7 %collective-permute-start.6 = (bf16[64,1664]{1,0:T(8,128)(2,1)S(1)}, bf16[64,1664]{1,0:T(8,128)(2,1)S(1)}, u32[]{:S(2)}, u32[]{:S(2)}) collective-permute-start(bf16[64,1664]{1,0:T(8,128)(2,1)S(1)} %pass.1.refs_1_), channel_id=1, source_target_pairs={{0,2},{2,0},{1,3},{3,1},{4,6},{6,4},{5,7},{7,5},{8,10},{10,8},{9,1... | collective-permute-start | bytes 638984 | tf_op jit(solution)/shard_map/ppermute | solution.py:377
  24.0 1.5 %collective-permute-start.10 = (bf16[64,1664]{1,0:T(8,128)(2,1)S(1)}, bf16[64,1664]{1,0:T(8,128)(2,1)S(1)}, u32[]{:S(2)}, u32[]{:S(2)}) collective-permute-start(bf16[64,1664]{1,0:T(8,128)(2,1)S(1)} %collective-permute-done.9.refs_1_), channel_id=1, source_target_pairs={{0,1},{2,4},{4,2},{6,7},{7,6},{5,3},{3,5},{1,0},{8,9},{10,12},{12,... | collective-permute-start | bytes 638984 | tf_op jit(solution)/shard_map/ppermute | solution.py:376
  25.5 2.9 %collective-permute-done.6.refs_2_ = bf16[64,1664]{1,0:T(8,128)(2,1)S(1)} collective-permute-done((bf16[64,1664]{1,0:T(8,128)(2,1)S(1)}, bf16[64,1664]{1,0:T(8,128)(2,1)S(1)}, u32[]{:S(2)}, u32[]{:S(2)}) %collective-permute-start.6) | collective-permute-done | bytes 213024 | tf_op jit(solution)/shard_map/ppermute | solution.py:377
  28.4 1.6 %collective-permute-start.7 = (bf16[64,1664]{1,0:T(8,128)(2,1)S(1)}, bf16[64,1664]{1,0:T(8,128)(2,1)S(1)}, u32[]{:S(2)}, u32[]{:S(2)}) collective-permute-start(bf16[64,1664]{1,0:T(8,128)(2,1)S(1)} %collective-permute-done.6.refs_2_), channel_id=1, source_target_pairs={{0,1},{2,4},{4,2},{6,7},{7,6},{5,3},{3,5},{1,0},{8,9},{10,12},{12,... | collective-permute-start | bytes 638984 | tf_op jit(solution)/shard_map/ppermute | solution.py:376
  30.0 0.8 %collective-permute-done.10.refs_2_ = bf16[64,1664]{1,0:T(8,128)(2,1)S(1)} collective-permute-done((bf16[64,1664]{1,0:T(8,128)(2,1)S(1)}, bf16[64,1664]{1,0:T(8,128)(2,1)S(1)}, u32[]{:S(2)}, u32[]{:S(2)}) %collective-permute-start.10) | collective-permute-done | bytes 213024 | tf_op jit(solution)/shard_map/ppermute | solution.py:376
  30.8 2.6 %collective-permute-start.11 = (bf16[64,1664]{1,0:T(8,128)(2,1)S(1)}, bf16[64,1664]{1,0:T(8,128)(2,1)S(1)}, u32[]{:S(2)}, u32[]{:S(2)}) collective-permute-start(bf16[64,1664]{1,0:T(8,128)(2,1)S(1)} %collective-permute-done.10.refs_2_), channel_id=1, source_target_pairs={{0,2},{2,0},{1,3},{3,1},{4,6},{6,4},{5,7},{7,5},{8,10},{10,8},{9,1... | collective-permute-start | bytes 638984 | tf_op jit(solution)/shard_map/ppermute | solution.py:377
  33.4 1.0 %collective-permute-done.7.refs_3_ = bf16[64,1664]{1,0:T(8,128)(2,1)S(1)} collective-permute-done((bf16[64,1664]{1,0:T(8,128)(2,1)S(1)}, bf16[64,1664]{1,0:T(8,128)(2,1)S(1)}, u32[]{:S(2)}, u32[]{:S(2)}) %collective-permute-start.7) | collective-permute-done | bytes 213024 | tf_op jit(solution)/shard_map/ppermute | solution.py:376
  34.4 0.4 sort_rows.2.refs_2_
  34.8 1.4 %multiply_convert_fusion = (bf16[2,128,1024]{2,1,0:T(8,128)(2,1)S(1)}, f32[2,128,1024]{2,1,0:T(8,128)S(1)}) fusion(bf16[2,128,1664]{2,1,0:T(8,128)(2,1)S(1)} %sort_rows.2.refs_2_, bf16[2,1664,1024]{2,1,0:T(8,128)(2,1)S(1)} %get-tuple-element.49), kind=kOutput, calls=%fused_computation.9 | convolution fusion | flops 873725952 | bytes 9240576 | tf_op jit(solution)/shard_map/xmd,xdf->xmf/dot_general | solution.py:415
  36.2 1.2 %convolution_convert_fusion.1.in_ref = bf16[2,128,1664]{2,1,0:T(8,128)(2,1)S(1)} fusion(bf16[2,128,1024]{2,1,0:T(8,128)(2,1)S(1)} %get-tuple-element.77.refs_1_, bf16[2,1024,1664]{2,1,0:T(8,128)(2,1)S(1)} %get-tuple-element.50), kind=kOutput, calls=%fused_computation.1 | convolution fusion | flops 872841216 | bytes 8192000 | tf_op jit(solution)/shard_map/xmf,xfd->xmd/dot_general | solution.py:417
  37.4 0.4 unsort_rows.2
  37.8 1.6 %collective-permute-start.8 = (bf16[64,1664]{1,0:T(8,128)(2,1)S(1)}, bf16[64,1664]{1,0:T(8,128)(2,1)S(1)}, u32[]{:S(2)}, u32[]{:S(2)}) collective-permute-start(bf16[64,1664]{1,0:T(8,128)(2,1)S(1)} %get-tuple-element.52.after_ref), channel_id=1, source_target_pairs={{0,1},{2,4},{4,2},{6,7},{7,6},{5,3},{3,5},{1,0},{8,9},{10,12},{12,... | collective-permute-start | bytes 638984 | tf_op jit(solution)/shard_map/ppermute | solution.py:376
  39.4 0.4 sort_rows.3.refs_2_
  39.8 2.4 %fusion.refs_1_ = bf16[2,128,1024]{2,1,0:T(8,128)(2,1)S(1)} fusion(bf16[2,128,1664]{2,1,0:T(8,128)(2,1)S(1)} %sort_rows.3.refs_2_, bf16[2,1024,1664]{2,1,0:T(8,128)(2,1)S(1)} %get-tuple-element.50, f32[2,128,1024]{2,1,0:T(8,128)S(1)} %get-tuple-element.78), kind=kOutput, calls=%fused_computation.4 | convolution fusion | flops 875036672 | bytes 9240576 | tf_op jit(solution)/shard_map/xmd,xfd->xmf/dot_general | solution.py:420
  42.2 2.3 %convolution_convert_fusion.in_ref = bf16[2,128,1664]{2,1,0:T(8,128)(2,1)S(1)} fusion(bf16[2,128,1024]{2,1,0:T(8,128)(2,1)S(1)} %fusion.refs_1_, bf16[2,1664,1024]{2,1,0:T(8,128)(2,1)S(1)} %get-tuple-element.49), kind=kOutput, calls=%fused_computation | convolution fusion | flops 872841216 | bytes 8192000 | tf_op jit(solution)/shard_map/xmf,xdf->xmd/dot_general | solution.py:424
  44.6 0.4 unsort_rows.3
  45.0 0.8 %collective-permute-start.12 = (bf16[64,1664]{1,0:T(8,128)(2,1)S(1)}, bf16[64,1664]{1,0:T(8,128)(2,1)S(1)}, u32[]{:S(2)}, u32[]{:S(2)}) collective-permute-start(bf16[64,1664]{1,0:T(8,128)(2,1)S(1)} %get-tuple-element.54.refs_0_), channel_id=1, source_target_pairs={{0,1},{2,4},{4,2},{6,7},{7,6},{5,3},{3,5},{1,0},{8,9},{10,12},{12,... | collective-permute-start | bytes 638984 | tf_op jit(solution)/shard_map/ppermute | solution.py:376
  45.8 1.8 %collective-permute-start.15 = (bf16[64,1664]{1,0:T(8,128)(2,1)S(1)}, bf16[64,1664]{1,0:T(8,128)(2,1)S(1)}, u32[]{:S(2)}, u32[]{:S(2)}) collective-permute-start(bf16[64,1664]{1,0:T(8,128)(2,1)S(1)} %add.21.after_ref), channel_id=1, source_target_pairs={{0,2},{2,0},{1,3},{3,1},{4,6},{6,4},{5,7},{7,5},{8,10},{10,8},{9,1... | collective-permute-start | bytes 638984 | tf_op jit(solution)/shard_map/ppermute | solution.py:377
  47.6 3.2 %w_out_grad_kernel.2 = (f32[2,1024,1664]{2,1,0:T(8,128)}, f32[8,128]{1,0:T(8,128)S(1)}) custom-call(bf16[64,1664]{1,0:T(8,128)(2,1)S(1)} %get-tuple-element.54.refs_0_, bf16[2,128,1024]{2,1,0:T(8,128)(2,1)S(1)} %get-tuple-element.77.refs_1_, bf16[2,128,1664]{2,1,0:T(8,128)(2,1)S(1)} %sort_rows.3.refs_2_), custom_call_target="tpu_custom_call" | custom-call | flops 436207616 | bytes 6815744 | tf_op jit(solution)/shard_map/w_out_grad_kernel/pallas_call | solution.py:260
  50.8 0.1 collective-permute-done.12.refs_2_
  51.0 1.6 %collective-permute-start.13 = (bf16[64,1664]{1,0:T(8,128)(2,1)S(1)}, bf16[64,1664]{1,0:T(8,128)(2,1)S(1)}, u32[]{:S(2)}, u32[]{:S(2)}) collective-permute-start(bf16[64,1664]{1,0:T(8,128)(2,1)S(1)} %add.22), channel_id=1, source_target_pairs={{0,2},{2,0},{1,3},{3,1},{4,6},{6,4},{5,7},{7,5},{8,10},{10,8},{9,1... | collective-permute-start | bytes 638984 | tf_op jit(solution)/shard_map/ppermute | solution.py:377
  52.6 0.2 collective-permute-done.15.refs_1_
  52.9 2.4 %collective-permute-start.16 = (bf16[64,1664]{1,0:T(8,128)(2,1)S(1)}, bf16[64,1664]{1,0:T(8,128)(2,1)S(1)}, u32[]{:S(2)}, u32[]{:S(2)}) collective-permute-start(bf16[64,1664]{1,0:T(8,128)(2,1)S(1)} %add.24), channel_id=1, source_target_pairs={{0,1},{2,4},{4,2},{6,7},{7,6},{5,3},{3,5},{1,0},{8,9},{10,12},{12,... | collective-permute-start | bytes 638984 | tf_op jit(solution)/shard_map/ppermute | solution.py:376
  55.3 1.6 %collective-permute-done.13.refs_1_ = bf16[64,1664]{1,0:T(8,128)(2,1)S(1)} collective-permute-done((bf16[64,1664]{1,0:T(8,128)(2,1)S(1)}, bf16[64,1664]{1,0:T(8,128)(2,1)S(1)}, u32[]{:S(2)}, u32[]{:S(2)}) %collective-permute-start.13) | collective-permute-done | bytes 213024 | tf_op jit(solution)/shard_map/ppermute | solution.py:377
  57.0 0.8 %collective-permute-start.14 = (bf16[64,1664]{1,0:T(8,128)(2,1)S(1)}, bf16[64,1664]{1,0:T(8,128)(2,1)S(1)}, u32[]{:S(2)}, u32[]{:S(2)}) collective-permute-start(bf16[64,1664]{1,0:T(8,128)(2,1)S(1)} %add.23.refs_0_), channel_id=1, source_target_pairs={{0,1},{2,4},{4,2},{6,7},{7,6},{5,3},{3,5},{1,0},{8,9},{10,12},{12,... | collective-permute-start | bytes 638984 | tf_op jit(solution)/shard_map/ppermute | solution.py:376
  57.7 3.2 %w_out_grad_kernel.3 = (f32[2,1024,1664]{2,1,0:T(8,128)}, f32[8,128]{1,0:T(8,128)S(1)}) custom-call(bf16[64,1664]{1,0:T(8,128)(2,1)S(1)} %add.23.refs_0_, bf16[2,128,1024]{2,1,0:T(8,128)(2,1)S(1)} %get-tuple-element.77.refs_1_, bf16[2,128,1664]{2,1,0:T(8,128)(2,1)S(1)} %sort_rows.3.refs_2_, ...), custom_call_target="tpu_custom_call", output_to_operand_aliasing={{0}: (3, {})} | custom-call | flops 436207616 | bytes 6815744 | tf_op jit(solution)/shard_map/w_out_grad_kernel/pallas_call | solution.py:260
  60.9 0.1 collective-permute-done.16.refs_2_
  61.1 1.9 %collective-permute-start.17 = (bf16[32,1664]{1,0:T(8,128)(2,1)S(1)}, bf16[32,1664]{1,0:T(8,128)(2,1)S(1)}, u32[]{:S(2)}, u32[]{:S(2)}) collective-permute-start(bf16[32,1664]{1,0:T(8,128)(2,1)S(1)} %get-tuple-element.65), channel_id=1, source_target_pairs={{0,2},{2,0},{1,3},{3,1},{4,6},{6,4},{5,7},{7,5},{8,10},{10,8},{9,1... | collective-permute-start | bytes 319496 | tf_op jit(solution)/shard_map/ppermute | solution.py:377
  63.0 0.3 collective-permute-done.14.refs_2_
  63.4 1.9 %collective-permute-start.18 = (bf16[32,1664]{1,0:T(8,128)(2,1)S(1)}, bf16[32,1664]{1,0:T(8,128)(2,1)S(1)}, u32[]{:S(2)}, u32[]{:S(2)}) collective-permute-start(bf16[32,1664]{1,0:T(8,128)(2,1)S(1)} %get-tuple-element.60.refs_0_), channel_id=1, source_target_pairs={{0,2},{2,0},{1,3},{3,1},{4,6},{6,4},{5,7},{7,5},{8,10},{10,8},{9,1... | collective-permute-start | bytes 319496 | tf_op jit(solution)/shard_map/ppermute | solution.py:377
  65.3 3.5 %w_in_grad_kernel.2 = (f32[2,1664,1024]{2,1,0:T(8,128)}, f32[8,128]{1,0:T(8,128)S(1)}) custom-call(bf16[32,1664]{1,0:T(8,128)(2,1)S(1)} %get-tuple-element.60.refs_0_, bf16[2,128,1024]{2,1,0:T(8,128)(2,1)S(1)} %fusion.refs_1_, bf16[2,128,1664]{2,1,0:T(8,128)(2,1)S(1)} %sort_rows.2.refs_2_), custom_call_target="tpu_custom_call" | custom-call | flops 436207616 | bytes 6815744 | tf_op jit(solution)/shard_map/w_in_grad_kernel/pallas_call | solution.py:260
  69.0 1.3 %collective-permute-start.20 = (bf16[16,1664]{1,0:T(8,128)(2,1)S(1)}, bf16[16,1664]{1,0:T(8,128)(2,1)S(1)}, u32[]{:S(2)}, u32[]{:S(2)}) collective-permute-start(bf16[16,1664]{1,0:T(8,128)(2,1)S(1)} %get-tuple-element.69), channel_id=1, source_target_pairs={{0,16},{8,24},{16,0},{24,8},{1,17},{9,25},{17,1},{25,9},{2,18},{10... | collective-permute-start | bytes 159752 | tf_op jit(solution)/shard_map/ppermute | solution.py:383
  70.3 0.5 collective-permute-start.21
  70.8 4.1 %w_in_grad_kernel.3 = (f32[2,1664,1024]{2,1,0:T(8,128)}, f32[8,128]{1,0:T(8,128)}) custom-call(bf16[16,1664]{1,0:T(8,128)(2,1)S(1)} %get-tuple-element.67.refs_0_, bf16[2,128,1024]{2,1,0:T(8,128)(2,1)S(1)} %fusion.refs_1_, bf16[2,128,1664]{2,1,0:T(8,128)(2,1)S(1)} %sort_rows.2.refs_2_, ...), custom_call_target="tpu_custom_call", output_to_operand_aliasing={{0}: (3, {})} | custom-call | flops 436207616 | bytes 6815744 | tf_op jit(solution)/shard_map/w_in_grad_kernel/pallas_call | solution.py:260
  75.0 1.5 %finish.1 = (bf16[128,1664]{1,0:T(8,128)(2,1)}, bf16[128,1664]{1,0:T(8,128)(2,1)}, f32[2,128]{1,0:T(2,128)}) custom-call(s32[2,128]{1,0:T(2,128)S(1)} %bitcast.14, s32[2,128]{1,0:T(2,128)S(1)} %bitcast.16, s32[2,128]{1,0:T(2,128)S(1)} %bitcast.18, f32[2,128]{1,0:T(2,128)S(1)} %bitcast.20, bf16[128,1664]{1,0:T(8,128)(2,1)S(1)} %copy-done, ...), custom_call_target="tpu_custom_call" | custom-call | tf_op jit(solution)/shard_map/finish/pallas_call | solution.py:212
  (33 shorter events, 0.6 us)
Async XLA Ops:
  2.8 6.1 %collective-permute-start = (bf16[16,1664]{1,0:T(8,128)(2,1)}, bf16[16,1664]{1,0:T(8,128)(2,1)S(1)}, u32[]{:S(2)}, u32[]{:S(2)}) collective-permute-start(bf16[16,1664]{1,0:T(8,128)(2,1)} %get-tuple-element.43), channel_id=1, source_target_pairs={{0,8},{8,0},{16,24},{24,16},{1,9},{9,1},{17,25},{25,17},{2,10},{10... | collective-permute-start | bytes 159752 | tf_op jit(solution)/shard_map/ppermute | solution.py:383
  3.2 5.7 %collective-permute-start.1 = (bf16[16,1664]{1,0:T(8,128)(2,1)}, bf16[16,1664]{1,0:T(8,128)(2,1)S(1)}, u32[]{:S(2)}, u32[]{:S(2)}) collective-permute-start(bf16[16,1664]{1,0:T(8,128)(2,1)} %get-tuple-element.44), channel_id=1, source_target_pairs={{0,16},{8,24},{16,0},{24,8},{1,17},{9,25},{17,1},{25,9},{2,18},{10... | collective-permute-start | bytes 159752 | tf_op jit(solution)/shard_map/ppermute | solution.py:383
  5.7 4.0 %collective-permute-start.2 = (bf16[16,1664]{1,0:T(8,128)(2,1)}, bf16[16,1664]{1,0:T(8,128)(2,1)S(1)}, u32[]{:S(2)}, u32[]{:S(2)}) collective-permute-start(bf16[16,1664]{1,0:T(8,128)(2,1)} %get-tuple-element.45), channel_id=1, source_target_pairs={{0,24},{8,16},{16,8},{24,0},{1,25},{9,17},{17,9},{25,1},{2,26},{10... | collective-permute-start | bytes 159752 | tf_op jit(solution)/shard_map/ppermute | solution.py:383
  9.7 5.1 %collective-permute-start.3 = (bf16[32,1664]{1,0:T(8,128)(2,1)S(1)}, bf16[32,1664]{1,0:T(8,128)(2,1)S(1)}, u32[]{:S(2)}, u32[]{:S(2)}) collective-permute-start(bf16[32,1664]{1,0:T(8,128)(2,1)S(1)} %get-tuple-element.46.refs_0_), channel_id=1, source_target_pairs={{0,1},{2,4},{4,2},{6,7},{7,6},{5,3},{3,5},{1,0},{8,9},{10,12},{12,... | collective-permute-start | bytes 319496 | tf_op jit(solution)/shard_map/ppermute | solution.py:376
  11.3 4.7 %collective-permute-start.4 = (bf16[32,1664]{1,0:T(8,128)(2,1)S(1)}, bf16[32,1664]{1,0:T(8,128)(2,1)S(1)}, u32[]{:S(2)}, u32[]{:S(2)}) collective-permute-start(bf16[32,1664]{1,0:T(8,128)(2,1)S(1)} %get-tuple-element.47.refs_1_), channel_id=1, source_target_pairs={{0,2},{2,0},{1,3},{3,1},{4,6},{6,4},{5,7},{7,5},{8,10},{10,8},{9,1... | collective-permute-start | bytes 319496 | tf_op jit(solution)/shard_map/ppermute | solution.py:377
  16.1 6.2 %collective-permute-start.5 = (bf16[64,1664]{1,0:T(8,128)(2,1)S(1)}, bf16[64,1664]{1,0:T(8,128)(2,1)S(1)}, u32[]{:S(2)}, u32[]{:S(2)}) collective-permute-start(bf16[64,1664]{1,0:T(8,128)(2,1)S(1)} %pair.2.refs_0_), channel_id=1, source_target_pairs={{0,1},{2,4},{4,2},{6,7},{7,6},{5,3},{3,5},{1,0},{8,9},{10,12},{12,... | collective-permute-start | bytes 638984 | tf_op jit(solution)/shard_map/ppermute | solution.py:376
  17.6 6.4 %collective-permute-start.9 = (bf16[64,1664]{1,0:T(8,128)(2,1)S(1)}, bf16[64,1664]{1,0:T(8,128)(2,1)S(1)}, u32[]{:S(2)}, u32[]{:S(2)}) collective-permute-start(bf16[64,1664]{1,0:T(8,128)(2,1)S(1)} %pair.3.refs_1_.refs_0_), channel_id=1, source_target_pairs={{0,2},{2,0},{1,3},{3,1},{4,6},{6,4},{5,7},{7,5},{8,10},{10,8},{9,1... | collective-permute-start | bytes 638984 | tf_op jit(solution)/shard_map/ppermute | solution.py:377
  22.3 6.1 %collective-permute-start.6 = (bf16[64,1664]{1,0:T(8,128)(2,1)S(1)}, bf16[64,1664]{1,0:T(8,128)(2,1)S(1)}, u32[]{:S(2)}, u32[]{:S(2)}) collective-permute-start(bf16[64,1664]{1,0:T(8,128)(2,1)S(1)} %pass.1.refs_1_), channel_id=1, source_target_pairs={{0,2},{2,0},{1,3},{3,1},{4,6},{6,4},{5,7},{7,5},{8,10},{10,8},{9,1... | collective-permute-start | bytes 638984 | tf_op jit(solution)/shard_map/ppermute | solution.py:377
  24.0 6.7 %collective-permute-start.10 = (bf16[64,1664]{1,0:T(8,128)(2,1)S(1)}, bf16[64,1664]{1,0:T(8,128)(2,1)S(1)}, u32[]{:S(2)}, u32[]{:S(2)}) collective-permute-start(bf16[64,1664]{1,0:T(8,128)(2,1)S(1)} %collective-permute-done.9.refs_1_), channel_id=1, source_target_pairs={{0,1},{2,4},{4,2},{6,7},{7,6},{5,3},{3,5},{1,0},{8,9},{10,12},{12,... | collective-permute-start | bytes 638984 | tf_op jit(solution)/shard_map/ppermute | solution.py:376
  28.4 6.0 %collective-permute-start.7 = (bf16[64,1664]{1,0:T(8,128)(2,1)S(1)}, bf16[64,1664]{1,0:T(8,128)(2,1)S(1)}, u32[]{:S(2)}, u32[]{:S(2)}) collective-permute-start(bf16[64,1664]{1,0:T(8,128)(2,1)S(1)} %collective-permute-done.6.refs_2_), channel_id=1, source_target_pairs={{0,1},{2,4},{4,2},{6,7},{7,6},{5,3},{3,5},{1,0},{8,9},{10,12},{12,... | collective-permute-start | bytes 638984 | tf_op jit(solution)/shard_map/ppermute | solution.py:376
  30.8 8.6 %collective-permute-start.11 = (bf16[64,1664]{1,0:T(8,128)(2,1)S(1)}, bf16[64,1664]{1,0:T(8,128)(2,1)S(1)}, u32[]{:S(2)}, u32[]{:S(2)}) collective-permute-start(bf16[64,1664]{1,0:T(8,128)(2,1)S(1)} %collective-permute-done.10.refs_2_), channel_id=1, source_target_pairs={{0,2},{2,0},{1,3},{3,1},{4,6},{6,4},{5,7},{7,5},{8,10},{10,8},{9,1... | collective-permute-start | bytes 638984 | tf_op jit(solution)/shard_map/ppermute | solution.py:377
  37.8 6.7 %collective-permute-start.8 = (bf16[64,1664]{1,0:T(8,128)(2,1)S(1)}, bf16[64,1664]{1,0:T(8,128)(2,1)S(1)}, u32[]{:S(2)}, u32[]{:S(2)}) collective-permute-start(bf16[64,1664]{1,0:T(8,128)(2,1)S(1)} %get-tuple-element.52.after_ref), channel_id=1, source_target_pairs={{0,1},{2,4},{4,2},{6,7},{7,6},{5,3},{3,5},{1,0},{8,9},{10,12},{12,... | collective-permute-start | bytes 638984 | tf_op jit(solution)/shard_map/ppermute | solution.py:376
  45.0 5.9 %collective-permute-start.12 = (bf16[64,1664]{1,0:T(8,128)(2,1)S(1)}, bf16[64,1664]{1,0:T(8,128)(2,1)S(1)}, u32[]{:S(2)}, u32[]{:S(2)}) collective-permute-start(bf16[64,1664]{1,0:T(8,128)(2,1)S(1)} %get-tuple-element.54.refs_0_), channel_id=1, source_target_pairs={{0,1},{2,4},{4,2},{6,7},{7,6},{5,3},{3,5},{1,0},{8,9},{10,12},{12,... | collective-permute-start | bytes 638984 | tf_op jit(solution)/shard_map/ppermute | solution.py:376
  45.8 7.0 %collective-permute-start.15 = (bf16[64,1664]{1,0:T(8,128)(2,1)S(1)}, bf16[64,1664]{1,0:T(8,128)(2,1)S(1)}, u32[]{:S(2)}, u32[]{:S(2)}) collective-permute-start(bf16[64,1664]{1,0:T(8,128)(2,1)S(1)} %add.21.after_ref), channel_id=1, source_target_pairs={{0,2},{2,0},{1,3},{3,1},{4,6},{6,4},{5,7},{7,5},{8,10},{10,8},{9,1... | collective-permute-start | bytes 638984 | tf_op jit(solution)/shard_map/ppermute | solution.py:377
  51.0 5.9 %collective-permute-start.13 = (bf16[64,1664]{1,0:T(8,128)(2,1)S(1)}, bf16[64,1664]{1,0:T(8,128)(2,1)S(1)}, u32[]{:S(2)}, u32[]{:S(2)}) collective-permute-start(bf16[64,1664]{1,0:T(8,128)(2,1)S(1)} %add.22), channel_id=1, source_target_pairs={{0,2},{2,0},{1,3},{3,1},{4,6},{6,4},{5,7},{7,5},{8,10},{10,8},{9,1... | collective-permute-start | bytes 638984 | tf_op jit(solution)/shard_map/ppermute | solution.py:377
  52.9 8.1 %collective-permute-start.16 = (bf16[64,1664]{1,0:T(8,128)(2,1)S(1)}, bf16[64,1664]{1,0:T(8,128)(2,1)S(1)}, u32[]{:S(2)}, u32[]{:S(2)}) collective-permute-start(bf16[64,1664]{1,0:T(8,128)(2,1)S(1)} %add.24), channel_id=1, source_target_pairs={{0,1},{2,4},{4,2},{6,7},{7,6},{5,3},{3,5},{1,0},{8,9},{10,12},{12,... | collective-permute-start | bytes 638984 | tf_op jit(solution)/shard_map/ppermute | solution.py:376
  57.0 6.4 %collective-permute-start.14 = (bf16[64,1664]{1,0:T(8,128)(2,1)S(1)}, bf16[64,1664]{1,0:T(8,128)(2,1)S(1)}, u32[]{:S(2)}, u32[]{:S(2)}) collective-permute-start(bf16[64,1664]{1,0:T(8,128)(2,1)S(1)} %add.23.refs_0_), channel_id=1, source_target_pairs={{0,1},{2,4},{4,2},{6,7},{7,6},{5,3},{3,5},{1,0},{8,9},{10,12},{12,... | collective-permute-start | bytes 638984 | tf_op jit(solution)/shard_map/ppermute | solution.py:376
  61.1 7.7 %collective-permute-start.17 = (bf16[32,1664]{1,0:T(8,128)(2,1)S(1)}, bf16[32,1664]{1,0:T(8,128)(2,1)S(1)}, u32[]{:S(2)}, u32[]{:S(2)}) collective-permute-start(bf16[32,1664]{1,0:T(8,128)(2,1)S(1)} %get-tuple-element.65), channel_id=1, source_target_pairs={{0,2},{2,0},{1,3},{3,1},{4,6},{6,4},{5,7},{7,5},{8,10},{10,8},{9,1... | collective-permute-start | bytes 319496 | tf_op jit(solution)/shard_map/ppermute | solution.py:377
  63.4 5.4 %collective-permute-start.18 = (bf16[32,1664]{1,0:T(8,128)(2,1)S(1)}, bf16[32,1664]{1,0:T(8,128)(2,1)S(1)}, u32[]{:S(2)}, u32[]{:S(2)}) collective-permute-start(bf16[32,1664]{1,0:T(8,128)(2,1)S(1)} %get-tuple-element.60.refs_0_), channel_id=1, source_target_pairs={{0,2},{2,0},{1,3},{3,1},{4,6},{6,4},{5,7},{7,5},{8,10},{10,8},{9,1... | collective-permute-start | bytes 319496 | tf_op jit(solution)/shard_map/ppermute | solution.py:377
  68.9 6.1 %collective-permute-start.19 = (bf16[16,1664]{1,0:T(8,128)(2,1)S(1)}, bf16[16,1664]{1,0:T(8,128)(2,1)S(1)}, u32[]{:S(2)}, u32[]{:S(2)}) collective-permute-start(bf16[16,1664]{1,0:T(8,128)(2,1)S(1)} %get-tuple-element.68), channel_id=1, source_target_pairs={{0,8},{8,0},{16,24},{24,16},{1,9},{9,1},{17,25},{25,17},{2,10},{10... | collective-permute-start | bytes 159752 | tf_op jit(solution)/shard_map/ppermute | solution.py:383
  69.0 6.0 %collective-permute-start.20 = (bf16[16,1664]{1,0:T(8,128)(2,1)S(1)}, bf16[16,1664]{1,0:T(8,128)(2,1)S(1)}, u32[]{:S(2)}, u32[]{:S(2)}) collective-permute-start(bf16[16,1664]{1,0:T(8,128)(2,1)S(1)} %get-tuple-element.69), channel_id=1, source_target_pairs={{0,16},{8,24},{16,0},{24,8},{1,17},{9,25},{17,1},{25,9},{2,18},{10... | collective-permute-start | bytes 159752 | tf_op jit(solution)/shard_map/ppermute | solution.py:383
  70.3 4.7 %collective-permute-start.21 = (bf16[16,1664]{1,0:T(8,128)(2,1)S(1)}, bf16[16,1664]{1,0:T(8,128)(2,1)S(1)}, u32[]{:S(2)}, u32[]{:S(2)}) collective-permute-start(bf16[16,1664]{1,0:T(8,128)(2,1)S(1)} %get-tuple-element.70), channel_id=1, source_target_pairs={{0,24},{8,16},{16,8},{24,0},{1,25},{9,17},{17,9},{25,1},{2,26},{10... | collective-permute-start | bytes 159752 | tf_op jit(solution)/shard_map/ppermute | solution.py:383
  70.8 4.2 %copy-start = (bf16[128,1664]{1,0:T(8,128)(2,1)S(1)}, bf16[128,1664]{1,0:T(8,128)(2,1)}, u32[]{:S(2)}) copy-start(bf16[128,1664]{1,0:T(8,128)(2,1)} %out_grad_ref.3) | copy-start | bytes 1277956
  70.8 4.2 %copy-start.1 = (s32[128,2]{0,1:T(2,128)S(1)}, s32[128,2]{0,1:T(2,128)}, u32[]{:S(2)}) copy-start(s32[128,2]{0,1:T(2,128)} %param.9) | copy-start | bytes 3076
  70.8 4.2 %copy-start.2 = (s32[128,2]{0,1:T(2,128)S(1)}, s32[128,2]{0,1:T(2,128)}, u32[]{:S(2)}) copy-start(s32[128,2]{0,1:T(2,128)} %param.10) | copy-start | bytes 3076
  70.8 4.2 %copy-start.3 = (s32[128,2]{0,1:T(2,128)S(1)}, s32[128,2]{0,1:T(2,128)}, u32[]{:S(2)}) copy-start(s32[128,2]{0,1:T(2,128)} %param.11) | copy-start | bytes 3076
  70.8 4.2 %copy-start.4 = (f32[128,2]{0,1:T(2,128)S(1)}, f32[128,2]{0,1:T(2,128)}, u32[]{:S(2)}) copy-start(f32[128,2]{0,1:T(2,128)} %param.12) | copy-start | bytes 3076

commit v4 on v3

--- a/solution.py
+++ b/solution.py
@@ -37,11 +37,12 @@
     )
 
 
-def order_matrix(expert, exp_local, count):
-    shape = (count // exp_local, count)
-    pick = lax.broadcasted_iota(jnp.int32, shape, 0)
-    row = lax.broadcasted_iota(jnp.int32, shape, 1)
-    wanted = (pick // CAP) * (CAP * exp_local) + expert * CAP + pick % CAP
+def order_matrix(exp_local, count):
+    pick = lax.broadcasted_iota(jnp.int32, (count, count), 0)
+    row = lax.broadcasted_iota(jnp.int32, (count, count), 1)
+    each = count // exp_local
+    expert, rest = pick // each, pick % each
+    wanted = (rest // CAP) * (CAP * exp_local) + expert * CAP + rest % CAP
     return (row == wanted).astype(jnp.bfloat16)
 
 
@@ -82,28 +83,33 @@
 def finish_kernel(
     ids_ref, slot_ref, dropped_ref, gates_ref, out_grad_ref, *refs, exp_local
 ):
-    parts, (mixed_ref, tok_grad_ref, gate_grad_ref) = refs[:-3], refs[-3:]
+    parts, outs, (made, sems) = refs[:-5], refs[-5:-2], refs[-2:]
+    mixed_ref, tok_grad_ref, gate_grad_ref = outs
     returned, returned_grad = [rows.astype(jnp.bfloat16) for rows in stack_halves(parts)]
     masks = slot_masks(ids_ref, slot_ref, dropped_ref, exp_local, returned.shape[0])
     select = sum(mask.astype(jnp.float32) for mask in masks).astype(jnp.bfloat16)
-    tok_grad_ref[...] = contract(select, returned_grad, 0, 0).astype(jnp.bfloat16)
+    made[0] = contract(select, returned_grad, 0, 0).astype(jnp.bfloat16)
+    copies = [pltpu.make_async_copy(made.at[0], tok_grad_ref, sems.at[0])]
+    copies[0].start()
     tokens = gates_ref.shape[1]
     gates = jnp.concatenate([gates_ref[...], jnp.zeros((6, tokens), jnp.float32)], axis=0).T
     wide = out_grad_ref[...].astype(jnp.float32)
-    mixed = jnp.zeros(wide.shape, jnp.float32)
-    grads = []
-    for k, mask in enumerate(masks):
-        picked = contract(mask.astype(jnp.bfloat16), returned, 0, 0)
-        mixed = mixed + gates[:, k : k + 1] * picked
-        grads.append(jnp.sum(picked * wide, axis=1, keepdims=True))
-    mixed_ref[...] = mixed.astype(jnp.bfloat16)
+    all_picked = [contract(mask.astype(jnp.bfloat16), returned, 0, 0) for mask in masks]
+    mixed = sum(gates[:, k : k + 1] * picked for k, picked in enumerate(all_picked))
+    made[1] = mixed.astype(jnp.bfloat16)
+    copies.append(pltpu.make_async_copy(made.at[1], mixed_ref, sems.at[1]))
+    copies[1].start()
+    grads = [jnp.sum(picked * wide, axis=1, keepdims=True) for picked in all_picked]
     grads.append(jnp.zeros((tokens, 6), jnp.float32))
     gate_grad_ref[...] = jnp.concatenate(grads, axis=1).T[:2]
-
-
-def split_kernel(after_ref, *refs):
+    for copy in copies:
+        copy.wait()
+
+
+def split_kernel(after_ref, *refs, exp_local):
     for out_ref, rows in zip(refs[-2:], stack_halves(refs[:-2])):
-        out_ref[...] = rows.astype(jnp.bfloat16)
+        order = order_matrix(exp_local, rows.shape[0])
+        out_ref[...] = contract(order, rows.astype(jnp.bfloat16), 1, 0).astype(jnp.bfloat16)
 
 
 def pair_kernel(*refs):
@@ -135,10 +141,11 @@
     other_ref[...] = total[half:]
 
 
-def join_kernel(*refs, groups):
+def join_kernel(*refs, groups, exp_local):
     first_a, first_b, second_a, second_b = refs[-groups - 4 : -groups]
-    first = add(first_a, first_b).astype(jnp.float32)
-    second = add(second_a, second_b).astype(jnp.float32)
+    order = order_matrix(exp_local, first_a.shape[0])
+    first = contract(order, add(first_a, first_b), 0, 0)
+    second = contract(order, add(second_a, second_b), 0, 0)
     half = first.shape[0] // groups
     for group, out_ref in enumerate(refs[-groups:]):
         part = slice(group * half, (group + 1) * half)
@@ -178,14 +185,14 @@
     pre_grad_ref, rows_ref = refs[skip : skip + 2]
     out_ref, done_ref, made, sems = refs[-4:]
     done_ref[...] = jnp.zeros(done_ref.shape, done_ref.dtype)
-    turned = rows_ref[expert].T
+    width, units = made.shape
     copies = []
-    for i, begin in enumerate(range(0, made.shape[1], chunk)):
-        here, there = pl.ds(begin, chunk), pl.ds(at + begin, chunk)
-        made[:, here] = contract(turned, pre_grad_ref[expert, :, there], 1, 0)
-        copies.append(
-            pltpu.make_async_copy(made.at[:, here], out_ref.at[expert, :, there], sems.at[i])
-        )
+    for i, begin in enumerate(range(0, width, chunk)):
+        here = pl.ds(begin, min(chunk, width - begin))
+        turned = rows_ref[expert, :, here].T
+        made[here] = contract(turned, pre_grad_ref[expert, :, at : at + units], 1, 0)
+        there = out_ref.at[expert, here, pl.ds(at, units)]
+        copies.append(pltpu.make_async_copy(made.at[here], there, sems.at[i]))
         copies[-1].start()
     for copy in copies:
         copy.wait()
@@ -209,12 +216,15 @@
 
 
 def finish(choices, gates, out_grad, parts, exp_local):
+    by_token = jax.ShapeDtypeStruct(out_grad.shape, jnp.bfloat16)
+    anywhere = pl.BlockSpec(memory_space=pl.ANY)
     return pl.pallas_call(
         functools.partial(finish_kernel, exp_local=exp_local),
-        out_shape=[
-            jax.ShapeDtypeStruct(out_grad.shape, jnp.bfloat16),
-            jax.ShapeDtypeStruct(out_grad.shape, jnp.bfloat16),
-            jax.ShapeDtypeStruct(gates.shape, jnp.float32),
+        out_specs=[anywhere, anywhere, pl.BlockSpec(memory_space=pltpu.VMEM)],
+        out_shape=[by_token, by_token, jax.ShapeDtypeStruct(gates.shape, jnp.float32)],
+        scratch_shapes=[
+            pltpu.VMEM((2,) + out_grad.shape, jnp.bfloat16),
+            pltpu.SemaphoreType.DMA((2,)),
         ],
         compiler_params=params(out_grad.shape[0]),
         name="finish",
@@ -254,8 +264,9 @@
     whole = pl.BlockSpec(memory_space=pltpu.VMEM)
     anywhere = pl.BlockSpec(memory_space=pl.ANY)
     width, units = rows.shape[2], hidden.shape[2] // parts
-    chunk = min(CHUNK // 2 if kernel is w_out_grad_kernel else CHUNK, units)
-    made = (units, width) if kernel is w_out_grad_kernel else (width, units)
+    made, chunk = (width, units), CHUNK
+    if kernel is w_out_grad_kernel:
+        made, chunk = (units, width), min(CHUNK // 2, units)
     operands = (*after, hidden, rows) + (() if base is None else (base,))
     return pl.pallas_call(
         functools.partial(kernel, skip=len(after), expert=expert, at=part * units, chunk=chunk),
@@ -265,7 +276,7 @@
         input_output_aliases={} if base is None else {len(operands) - 1: 0},
         scratch_shapes=[
             pltpu.VMEM(made, jnp.float32),
-            pltpu.SemaphoreType.DMA((units // chunk,)),
+            pltpu.SemaphoreType.DMA((-(-made[0] // chunk),)),
         ],
         compiler_params=pltpu.CompilerParams(vmem_limit_bytes=24 << 20),
         cost_estimate=pl.CostEstimate(
@@ -280,29 +291,40 @@
 def sort_kernel(after_ref, *refs, places):
     blocks, out_ref = refs[:-1], refs[-1]
     experts = out_ref.shape[0]
-    count = blocks[0].shape[0]
-    part = count // experts // 2
-    for expert in range(experts):
-        order = order_matrix(expert, experts, count)
-        for step, ref in enumerate(blocks):
-            rows = contract(order, ref[...], 1, 0).astype(jnp.bfloat16)
-            for i in range(2):
-                at = places[2 * step + i] * part
-                out_ref[expert, at : at + part] = rows[i * part : (i + 1) * part]
+    part = blocks[0].shape[0] // (2 * experts)
+    for i, place in enumerate(places):
+        for expert in range(experts):
+            at = ((i % 2) * experts + expert) * part
+            out_ref[expert, place * part : (place + 1) * part] = blocks[i // 2][at : at + part]
 
 
 def unsort_kernel(after_ref, in_ref, *blocks):
     experts = in_ref.shape[0]
-    count = blocks[0].shape[0]
-    part = count // experts
-    order = jnp.concatenate(
-        [order_matrix(expert, experts, count) for expert in range(experts)], axis=0
-    )
-    for step, ref in enumerate(blocks):
-        piece = jnp.concatenate(
-            [in_ref[expert, step * part : (step + 1) * part] for expert in range(experts)], axis=0
-        )
-        ref[...] = contract(order, piece, 0, 0).astype(jnp.bfloat16)
+    part = blocks[0].shape[0] // (2 * experts)
+    for i in range(2 * len(blocks)):
+        for expert in range(experts):
+            at = ((i % 2) * experts + expert) * part
+            blocks[i // 2][at : at + part] = in_ref[expert, i * part : (i + 1) * part]
+
+
+def backward_kernel(after_ref, *refs, places):
+    blocks, (slope_ref, w_in_ref, w_out_ref) = refs[:-7], refs[-7:-4]
+    rows_ref, pre_grad_ref, row_grad_ref, turned = refs[-4:]
+    experts, units, width = w_out_ref.shape
+    step = min(2 * CHUNK, units)
+    sort_kernel(after_ref, *blocks, rows_ref, places=places)
+    for expert in range(experts):
+        grads = rows_ref[expert].T
+        for at in range(0, units, step):
+            here = slice(at, at + step)
+            hidden_grad = contract(w_out_ref[expert, here], grads, 1, 0)
+            pre_grad = (hidden_grad * slope_ref[expert, :, here].T).astype(jnp.bfloat16)
+            turned[here] = pre_grad
+            pre_grad_ref[expert, :, here] = pre_grad.T
+        for at in range(0, width, CHUNK):
+            here = slice(at, min(at + CHUNK, width))
+            row_grad = contract(w_in_ref[expert, here], turned[...], 1, 0)
+            row_grad_ref[expert, :, here] = row_grad.T.astype(jnp.bfloat16)
 
 
 def order_cost(count, width):
@@ -323,6 +345,26 @@
         cost_estimate=order_cost(experts * rows, width),
         name="sort_rows",
     )(after, *blocks)
+
+
+def backward(blocks, slope, w_in, w_out, places, after):
+    experts, units, width = w_out.shape
+    rows = slope.shape[1]
+    by_row = jax.ShapeDtypeStruct((experts, rows, width), jnp.bfloat16)
+    return pl.pallas_call(
+        functools.partial(backward_kernel, places=places),
+        in_specs=[pl.BlockSpec(memory_space=pl.ANY)]
+        + [pl.BlockSpec(memory_space=pltpu.VMEM)] * (len(blocks) + 3),
+        out_shape=[by_row, jax.ShapeDtypeStruct(slope.shape, jnp.bfloat16), by_row],
+        scratch_shapes=[pltpu.VMEM((units, rows), jnp.bfloat16)],
+        compiler_params=pltpu.CompilerParams(vmem_limit_bytes=(10 << 20) + rows * (40 << 10)),
+        cost_estimate=pl.CostEstimate(
+            flops=4 * experts * rows * width * units,
+            bytes_accessed=4 * experts * rows * width,
+            transcendentals=0,
+        ),
+        name="backward",
+    )(after, *blocks, slope, w_in, w_out)
 
 
 def unsort_rows(rows, steps, after):
@@ -397,7 +439,9 @@
     send = prepare(choices, gates, tokens, out_grad, n_expert, exp_local)
     got = expert_swap(send)
     held_in, done_in = hold([], w_in)
-    own_rows, own_grads = small_call(split_kernel, "split", [done_in], got, [count] * 2)
+    own_rows, own_grads = small_call(
+        functools.partial(split_kernel, exp_local=exp_local), "split", [done_in], got, [count] * 2
+    )
 
     mate_rows, mate_grads = swap(own_rows, False), swap(own_grads, True)
     pairs = [own_rows, mate_rows]
@@ -416,31 +460,25 @@
     hidden = gelu_exact(pre).astype(jnp.bfloat16)
     output = jnp.einsum("xmf,xfd->xmd", hidden, held_out, preferred_element_type=jnp.float32)
     out_blocks = unsort_rows(output.astype(jnp.bfloat16), steps, done_out)
-    grad_rows = sort_rows(grad_blocks, exp_local, regroup(n_dp), out_blocks[-1])
-    hidden_grad = jnp.einsum(
-        "xmd,xfd->xmf", grad_rows, held_out, preferred_element_type=jnp.float32
-    )
-    pre_grad = (hidden_grad * gelu_slope(pre)).astype(jnp.bfloat16)
-    row_grad = jnp.einsum(
-        "xmf,xdf->xmd", pre_grad, held_in, preferred_element_type=jnp.float32
-    )
-
-    parts = 1
-    work = [
-        (kernel, left, right, shape, expert, part)
-        for kernel, left, right, shape in (
-            (w_out_grad_kernel, hidden, grad_rows, w_out.shape),
-            (w_in_grad_kernel, pre_grad, rows, w_in.shape),
-        )
-        for expert in range(exp_local)
-        for part in range(parts)
-    ]
+    grad_rows, pre_grad, row_grad = backward(
+        grad_blocks, gelu_slope(pre), held_in, held_out, regroup(n_dp), out_blocks[-1]
+    )
+
+    def out_piece(expert, part, parts):
+        return (w_out_grad_kernel, hidden, grad_rows, w_out.shape, expert, part, parts)
+
+    def in_piece(expert, part, parts):
+        return (w_in_grad_kernel, pre_grad, rows, w_in.shape, expert, part, parts)
+
+    others, final = range(exp_local - 1), exp_local - 1
+    work = [out_piece(x, 0, 1) for x in others] + [out_piece(final, part, 2) for part in (0, 1)]
+    work += [in_piece(x, 0, 1) for x in range(exp_local)]
     made = {}
 
     def next_piece(after):
         if len(work) == 0:
             return after
-        kernel, left, right, shape, expert, part = work.pop(0)
+        kernel, left, right, shape, expert, part, parts = work.pop(0)
         name = kernel.__name__
         made[name], ready = weight_gradient(
             kernel, left, right, shape, [after], name, expert, part, parts, made.get(name)
@@ -462,14 +500,16 @@
         out_sum = add_step(ready, out_blocks[step - 1], out_arrived, step)
         out_arrived = swap(out_sum[-1], step % 2 == 0)
         if step == last:
-            back_blocks = unsort_rows(row_grad.astype(jnp.bfloat16), steps, out_sum[0])
+            back_blocks = unsort_rows(row_grad, steps, out_sum[0])
             back_sum = back_blocks[last:]
             back_arrived = swap(back_sum[-1], step % 2 == 1)
             ready = [next_piece(back_sum[-1])]
+        elif step > 1:
+            ready = [next_piece(out_sum[-1])]
         back_sum = add_step(ready, back_blocks[step - 1], back_arrived, step)
     back_arrived = swap(back_sum[-1], False)
     joined = small_call(
-        functools.partial(join_kernel, groups=n_expert),
+        functools.partial(join_kernel, groups=n_expert, exp_local=exp_local),
         "join",
         [next_piece(back_sum[-1])],
         [out_sum[0], out_arrived, back_sum[0], back_arrived],

time: 76.7 us -> 76.1 us (level)
  matrix products: 7.26 us -> 2.75 us
  Pallas kernels: 25.7 us -> 29.6 us
  waiting for transfers between devices: 11.1 us -> 12.4 us
  starting transfers between devices: 31.5 us -> 30.3 us
    dot_general x2 -> x0, matrix products: 4.7 us -> none  [the longest x1 2.37 us: per_device(): jnp.einsum('xmd,xfd->xmf', grad_rows, held_out, preferred_element_type=jn...]
    pallas_call x0 -> x1, Pallas kernels: none -> 4.05 us  [backward(): pl.pallas_call(functools.partial(backward_kernel, places=places), in_spec...]
    ppermute x8, starting transfers between devices: 14.9 us -> 13.5 us  [swap(): return lax.ppermute(block, 'near', [(0, 1), (1, 0)])]
    ppermute x8, waiting for transfers between devices: 4.29 us -> 5.54 us  [swap(): return lax.ppermute(block, DP, odd_edges(lax.axis_size(DP)))]
    pallas_call x4 -> x5, Pallas kernels: 14 us -> 14.3 us  [weight_gradient(): pl.pallas_call(functools.partial(kernel, skip=len(after), expert=expert,...]
  transfers between devices with their start and end apart: 22 -> 22, of which waited for: 12 -> 13; matrix products, arithmetic and copies ran while one was open for 9% -> 4% of each run, Pallas kernels for 28% -> 33%
where the time goes in v4:
time: 76.1 us; the launch traced here: 76 us
  starting transfers between devices  30.3 us (40%)
  Pallas kernels  29.6 us (39%)
  waiting for transfers between devices  12.4 us (16%)
  matrix products  2.75 us (4%)
  between operations  0.91 us (1%)
    pallas_call x5, Pallas kernels, weight_gradient(): pl.pallas_call(functools.partial(kernel, skip=len(after), expert=expert,...  14.3 us
    ppermute x8, starting transfers between devices, swap(): return lax.ppermute(block, 'near', [(0, 1), (1, 0)])  13.5 us
    ppermute x8, starting transfers between devices, swap(): return lax.ppermute(block, DP, odd_edges(lax.axis_size(DP)))  11.8 us
    ppermute x8, waiting for transfers between devices, swap(): return lax.ppermute(block, 'near', [(0, 1), (1, 0)])  6.05 us
    pallas_call x2, Pallas kernels, hold(): pl.pallas_call(hold_kernel, in_specs=[pl.BlockSpec(memory_space=pl.ANY)]...  6.04 us
    ppermute x8, waiting for transfers between devices, swap(): return lax.ppermute(block, DP, odd_edges(lax.axis_size(DP)))  5.54 us
    ppermute x6, starting transfers between devices, expert_swap(): lax.ppermute(blocks[k], 'expert', [(i, i ^ k) for i in range(size)])  5.02 us
    pallas_call x1, Pallas kernels, backward(): pl.pallas_call(functools.partial(backward_kernel, places=places), in_spec...  4.05 us
  transfers between devices with their start and end apart: 22, of which 13 were waited for; matrix products, arithmetic and copies ran while one was open for 4% of the time, Pallas kernels for 33%

profile of v4, /device:TPU:0, one launch (start us, length us, event | category | flops | bytes accessed | tf_op | source)
XLA Modules:
  0.0 76.0 jit_solution(1502208325200529038)
XLA Ops:
  0.6 2.1 %prepare.1 = (bf16[16,1664]{1,0:T(8,128)(2,1)S(1)}, bf16[16,1664]{1,0:T(8,128)(2,1)}, bf16[16,1664]{1,0:T(8,128)(2,1)}, bf16[16,1664]{1,0:T(8,128)(2,1)}) custom-call(s32[2,128]{1,0:T(2,128)} %bitcast.9, s32[2,128]{1,0:T(2,128)} %bitcast.11, s32[2,128]{1,0:T(2,128)} %bitcast.13, f32[2,128]{1,0:T(2,128)} %bitcast.15, bf16[128,1664]{1,0:T(8,128)(2,1)} %tokens_ref.1, ...), custom_call_target="tpu_custom_call" | custom-call | tf_op jit(solution)/shard_map/prepare/pallas_call | solution.py:208
  2.8 0.4 collective-permute-start
  3.2 2.5 %collective-permute-start.1 = (bf16[16,1664]{1,0:T(8,128)(2,1)}, bf16[16,1664]{1,0:T(8,128)(2,1)S(1)}, u32[]{:S(2)}, u32[]{:S(2)}) collective-permute-start(bf16[16,1664]{1,0:T(8,128)(2,1)} %get-tuple-element.49), channel_id=1, source_target_pairs={{0,16},{8,24},{16,0},{24,8},{1,17},{9,25},{17,1},{25,9},{2,18},{10... | collective-permute-start | bytes 159752 | tf_op jit(solution)/shard_map/ppermute | solution.py:425
  5.7 0.1 collective-permute-start.2
  5.8 3.0 %hold.2 = (bf16[2,1664,1024]{2,1,0:T(8,128)(2,1)S(1)}, f32[8,128]{1,0:T(8,128)S(1)}) custom-call(bf16[2,1664,1024]{2,1,0:T(8,128)(2,1)} %refs_0_.1), custom_call_target="tpu_custom_call" | custom-call | bytes 13631488 | tf_op jit(solution)/shard_map/hold/pallas_call | solution.py:249
  8.9 0.8 %collective-permute-done.2.refs_3_ = bf16[16,1664]{1,0:T(8,128)(2,1)S(1)} collective-permute-done((bf16[16,1664]{1,0:T(8,128)(2,1)}, bf16[16,1664]{1,0:T(8,128)(2,1)S(1)}, u32[]{:S(2)}, u32[]{:S(2)}) %collective-permute-start.2) | collective-permute-done | bytes 53280 | tf_op jit(solution)/shard_map/ppermute | solution.py:425
  9.7 0.2 split.1
  9.9 1.6 %collective-permute-start.3 = (bf16[32,1664]{1,0:T(8,128)(2,1)S(1)}, bf16[32,1664]{1,0:T(8,128)(2,1)S(1)}, u32[]{:S(2)}, u32[]{:S(2)}) collective-permute-start(bf16[32,1664]{1,0:T(8,128)(2,1)S(1)} %get-tuple-element.51.refs_0_), channel_id=1, source_target_pairs={{0,1},{2,4},{4,2},{6,7},{7,6},{5,3},{3,5},{1,0},{8,9},{10,12},{12,... | collective-permute-start | bytes 319496 | tf_op jit(solution)/shard_map/ppermute | solution.py:418
  11.5 1.6 %collective-permute-start.4 = (bf16[32,1664]{1,0:T(8,128)(2,1)S(1)}, bf16[32,1664]{1,0:T(8,128)(2,1)S(1)}, u32[]{:S(2)}, u32[]{:S(2)}) collective-permute-start(bf16[32,1664]{1,0:T(8,128)(2,1)S(1)} %get-tuple-element.52.refs_1_), channel_id=1, source_target_pairs={{0,2},{2,0},{1,3},{3,1},{4,6},{6,4},{5,7},{7,5},{8,10},{10,8},{9,1... | collective-permute-start | bytes 319496 | tf_op jit(solution)/shard_map/ppermute | solution.py:419
  13.1 1.9 %collective-permute-done.3.refs_0_.refs_1_ = bf16[32,1664]{1,0:T(8,128)(2,1)S(1)} collective-permute-done((bf16[32,1664]{1,0:T(8,128)(2,1)S(1)}, bf16[32,1664]{1,0:T(8,128)(2,1)S(1)}, u32[]{:S(2)}, u32[]{:S(2)}) %collective-permute-start.3) | collective-permute-done | bytes 106528 | tf_op jit(solution)/shard_map/ppermute | solution.py:418
  15.0 1.2 %collective-permute-done.4.refs_2_ = bf16[32,1664]{1,0:T(8,128)(2,1)S(1)} collective-permute-done((bf16[32,1664]{1,0:T(8,128)(2,1)S(1)}, bf16[32,1664]{1,0:T(8,128)(2,1)S(1)}, u32[]{:S(2)}, u32[]{:S(2)}) %collective-permute-start.4) | collective-permute-done | bytes 106528 | tf_op jit(solution)/shard_map/ppermute | solution.py:419
  16.3 1.5 %collective-permute-start.5 = (bf16[64,1664]{1,0:T(8,128)(2,1)S(1)}, bf16[64,1664]{1,0:T(8,128)(2,1)S(1)}, u32[]{:S(2)}, u32[]{:S(2)}) collective-permute-start(bf16[64,1664]{1,0:T(8,128)(2,1)S(1)} %pair.2.refs_0_), channel_id=1, source_target_pairs={{0,1},{2,4},{4,2},{6,7},{7,6},{5,3},{3,5},{1,0},{8,9},{10,12},{12,... | collective-permute-start | bytes 638984 | tf_op jit(solution)/shard_map/ppermute | solution.py:418
  17.8 1.6 %collective-permute-start.10 = (bf16[64,1664]{1,0:T(8,128)(2,1)S(1)}, bf16[64,1664]{1,0:T(8,128)(2,1)S(1)}, u32[]{:S(2)}, u32[]{:S(2)}) collective-permute-start(bf16[64,1664]{1,0:T(8,128)(2,1)S(1)} %pair.3.refs_1_.refs_0_), channel_id=1, source_target_pairs={{0,2},{2,0},{1,3},{3,1},{4,6},{6,4},{5,7},{7,5},{8,10},{10,8},{9,1... | collective-permute-start | bytes 638984 | tf_op jit(solution)/shard_map/ppermute | solution.py:419
  19.4 3.0 %hold.3 = (bf16[2,1024,1664]{2,1,0:T(8,128)(2,1)S(1)}, f32[8,128]{1,0:T(8,128)S(1)}) custom-call(bf16[64,1664]{1,0:T(8,128)(2,1)S(1)} %pair.2.refs_0_, bf16[64,1664]{1,0:T(8,128)(2,1)S(1)} %pair.3.refs_1_.refs_0_, bf16[2,1024,1664]{2,1,0:T(8,128)(2,1)} %refs_2_.1), custom_call_target="tpu_custom_call" | custom-call | bytes 13631488 | tf_op jit(solution)/shard_map/hold/pallas_call | solution.py:249
  22.5 1.7 %collective-permute-start.6 = (bf16[64,1664]{1,0:T(8,128)(2,1)S(1)}, bf16[64,1664]{1,0:T(8,128)(2,1)S(1)}, u32[]{:S(2)}, u32[]{:S(2)}) collective-permute-start(bf16[64,1664]{1,0:T(8,128)(2,1)S(1)} %pass.1.refs_1_), channel_id=1, source_target_pairs={{0,2},{2,0},{1,3},{3,1},{4,6},{6,4},{5,7},{7,5},{8,10},{10,8},{9,1... | collective-permute-start | bytes 638984 | tf_op jit(solution)/shard_map/ppermute | solution.py:419
  24.2 1.5 %collective-permute-start.11 = (bf16[64,1664]{1,0:T(8,128)(2,1)S(1)}, bf16[64,1664]{1,0:T(8,128)(2,1)S(1)}, u32[]{:S(2)}, u32[]{:S(2)}) collective-permute-start(bf16[64,1664]{1,0:T(8,128)(2,1)S(1)} %collective-permute-done.10.refs_1_), channel_id=1, source_target_pairs={{0,1},{2,4},{4,2},{6,7},{7,6},{5,3},{3,5},{1,0},{8,9},{10,12},{12,... | collective-permute-start | bytes 638984 | tf_op jit(solution)/shard_map/ppermute | solution.py:418
  25.7 2.9 %collective-permute-done.6.refs_2_ = bf16[64,1664]{1,0:T(8,128)(2,1)S(1)} collective-permute-done((bf16[64,1664]{1,0:T(8,128)(2,1)S(1)}, bf16[64,1664]{1,0:T(8,128)(2,1)S(1)}, u32[]{:S(2)}, u32[]{:S(2)}) %collective-permute-start.6) | collective-permute-done | bytes 213024 | tf_op jit(solution)/shard_map/ppermute | solution.py:419
  28.6 1.6 %collective-permute-start.7 = (bf16[64,1664]{1,0:T(8,128)(2,1)S(1)}, bf16[64,1664]{1,0:T(8,128)(2,1)S(1)}, u32[]{:S(2)}, u32[]{:S(2)}) collective-permute-start(bf16[64,1664]{1,0:T(8,128)(2,1)S(1)} %collective-permute-done.6.refs_2_), channel_id=1, source_target_pairs={{0,1},{2,4},{4,2},{6,7},{7,6},{5,3},{3,5},{1,0},{8,9},{10,12},{12,... | collective-permute-start | bytes 638984 | tf_op jit(solution)/shard_map/ppermute | solution.py:418
  30.1 0.8 %collective-permute-done.11.refs_2_ = bf16[64,1664]{1,0:T(8,128)(2,1)S(1)} collective-permute-done((bf16[64,1664]{1,0:T(8,128)(2,1)S(1)}, bf16[64,1664]{1,0:T(8,128)(2,1)S(1)}, u32[]{:S(2)}, u32[]{:S(2)}) %collective-permute-start.11) | collective-permute-done | bytes 213024 | tf_op jit(solution)/shard_map/ppermute | solution.py:418
  30.9 2.6 %collective-permute-start.12 = (bf16[64,1664]{1,0:T(8,128)(2,1)S(1)}, bf16[64,1664]{1,0:T(8,128)(2,1)S(1)}, u32[]{:S(2)}, u32[]{:S(2)}) collective-permute-start(bf16[64,1664]{1,0:T(8,128)(2,1)S(1)} %collective-permute-done.11.refs_2_), channel_id=1, source_target_pairs={{0,2},{2,0},{1,3},{3,1},{4,6},{6,4},{5,7},{7,5},{8,10},{10,8},{9,1... | collective-permute-start | bytes 638984 | tf_op jit(solution)/shard_map/ppermute | solution.py:419
  33.6 1.0 %collective-permute-done.7.refs_3_ = bf16[64,1664]{1,0:T(8,128)(2,1)S(1)} collective-permute-done((bf16[64,1664]{1,0:T(8,128)(2,1)S(1)}, bf16[64,1664]{1,0:T(8,128)(2,1)S(1)}, u32[]{:S(2)}, u32[]{:S(2)}) %collective-permute-start.7) | collective-permute-done | bytes 213024 | tf_op jit(solution)/shard_map/ppermute | solution.py:418
  34.7 1.6 %fusion.3 = (f32[2,128,1024]{2,1,0:T(8,128)S(1)}, bf16[2,128,1024]{2,1,0:T(8,128)(2,1)S(1)}) fusion(bf16[2,128,1664]{2,1,0:T(8,128)(2,1)S(1)} %sort_rows.1.refs_2_, bf16[2,1664,1024]{2,1,0:T(8,128)(2,1)S(1)} %get-tuple-element.54.refs_5_), kind=kOutput, calls=%fused_computation.5 | convolution fusion | flops 875298816 | bytes 9240576 | tf_op jit(solution)/shard_map/xmd,xdf->xmf/dot_general | solution.py:459
  36.3 1.2 %convolution_convert_fusion.in_ref = bf16[2,128,1664]{2,1,0:T(8,128)(2,1)S(1)} fusion(bf16[2,128,1024]{2,1,0:T(8,128)(2,1)S(1)} %get-tuple-element.88.refs_1_, bf16[2,1024,1664]{2,1,0:T(8,128)(2,1)S(1)} %get-tuple-element.55.refs_6_), kind=kOutput, calls=%fused_computation | convolution fusion | flops 872841216 | bytes 8192000 | tf_op jit(solution)/shard_map/xmf,xfd->xmd/dot_general | solution.py:461
  37.5 1.6 %collective-permute-start.8 = (bf16[64,1664]{1,0:T(8,128)(2,1)S(1)}, bf16[64,1664]{1,0:T(8,128)(2,1)S(1)}, u32[]{:S(2)}, u32[]{:S(2)}) collective-permute-start(bf16[64,1664]{1,0:T(8,128)(2,1)S(1)} %get-tuple-element.58.after_ref), channel_id=1, source_target_pairs={{0,1},{2,4},{4,2},{6,7},{7,6},{5,3},{3,5},{1,0},{8,9},{10,12},{12,... | collective-permute-start | bytes 638984 | tf_op jit(solution)/shard_map/ppermute | solution.py:418
  39.1 4.0 %backward.1 = (bf16[2,128,1664]{2,1,0:T(8,128)(2,1)S(1)}, bf16[2,128,1024]{2,1,0:T(8,128)(2,1)S(1)}, bf16[2,128,1664]{2,1,0:T(8,128)(2,1)S(1)}) custom-call(bf16[64,1664]{1,0:T(8,128)(2,1)S(1)} %get-tuple-element.58.after_ref, bf16[64,1664]{1,0:T(8,128)(2,1)S(1)} %pair.3.refs_1_.refs_0_, bf16[64,1664]{1,0:T(8,128)(2,1)S(1)} %collective-permute-done.10.refs_1_, ...), custom_call_target="tpu_custom_call" | custom-call | flops 1744830464 | bytes 1703936 | tf_op jit(solution)/shard_map/backward/pallas_call | solution.py:354
  43.2 0.3 collective-permute-done.8.refs_1_
  43.6 2.0 %collective-permute-start.13 = (bf16[64,1664]{1,0:T(8,128)(2,1)S(1)}, bf16[64,1664]{1,0:T(8,128)(2,1)S(1)}, u32[]{:S(2)}, u32[]{:S(2)}) collective-permute-start(bf16[64,1664]{1,0:T(8,128)(2,1)S(1)} %get-tuple-element.61.refs_0_), channel_id=1, source_target_pairs={{0,1},{2,4},{4,2},{6,7},{7,6},{5,3},{3,5},{1,0},{8,9},{10,12},{12,... | collective-permute-start | bytes 638984 | tf_op jit(solution)/shard_map/ppermute | solution.py:418
  45.5 1.2 %collective-permute-start.9 = (bf16[64,1664]{1,0:T(8,128)(2,1)S(1)}, bf16[64,1664]{1,0:T(8,128)(2,1)S(1)}, u32[]{:S(2)}, u32[]{:S(2)}) collective-permute-start(bf16[64,1664]{1,0:T(8,128)(2,1)S(1)} %add.19.after_ref), channel_id=1, source_target_pairs={{0,2},{2,0},{1,3},{3,1},{4,6},{6,4},{5,7},{7,5},{8,10},{10,8},{9,1... | collective-permute-start | bytes 638984 | tf_op jit(solution)/shard_map/ppermute | solution.py:419
  46.7 3.2 %w_out_grad_kernel.3 = (f32[2,1024,1664]{2,1,0:T(8,128)}, f32[8,128]{1,0:T(8,128)S(1)}) custom-call(bf16[64,1664]{1,0:T(8,128)(2,1)S(1)} %get-tuple-element.61.refs_0_, bf16[2,128,1024]{2,1,0:T(8,128)(2,1)S(1)} %get-tuple-element.88.refs_1_, bf16[2,128,1664]{2,1,0:T(8,128)(2,1)S(1)} %get-tuple-element.59.refs_2_), custom_call_target="tpu_custom_call" | custom-call | flops 436207616 | bytes 6815744 | tf_op jit(solution)/shard_map/w_out_grad_kernel/pallas_call | solution.py:271
  50.0 1.8 %collective-permute-start.14 = (bf16[64,1664]{1,0:T(8,128)(2,1)S(1)}, bf16[64,1664]{1,0:T(8,128)(2,1)S(1)}, u32[]{:S(2)}, u32[]{:S(2)}) collective-permute-start(bf16[64,1664]{1,0:T(8,128)(2,1)S(1)} %add.21), channel_id=1, source_target_pairs={{0,2},{2,0},{1,3},{3,1},{4,6},{6,4},{5,7},{7,5},{8,10},{10,8},{9,1... | collective-permute-start | bytes 638984 | tf_op jit(solution)/shard_map/ppermute | solution.py:419
  51.8 1.6 %collective-permute-done.9.refs_1_ = bf16[64,1664]{1,0:T(8,128)(2,1)S(1)} collective-permute-done((bf16[64,1664]{1,0:T(8,128)(2,1)S(1)}, bf16[64,1664]{1,0:T(8,128)(2,1)S(1)}, u32[]{:S(2)}, u32[]{:S(2)}) %collective-permute-start.9) | collective-permute-done | bytes 213024 | tf_op jit(solution)/shard_map/ppermute | solution.py:419
  53.4 0.2 collective-permute-start.16
  53.6 2.1 %w_out_grad_kernel.4 = (f32[2,1024,1664]{2,1,0:T(8,128)}, f32[8,128]{1,0:T(8,128)S(1)}) custom-call(bf16[64,1664]{1,0:T(8,128)(2,1)S(1)} %add.20.refs_0_, bf16[2,128,1024]{2,1,0:T(8,128)(2,1)S(1)} %get-tuple-element.88.refs_1_, bf16[2,128,1664]{2,1,0:T(8,128)(2,1)S(1)} %get-tuple-element.59.refs_2_, ...), custom_call_target="tpu_custom_call", output_to_operand_aliasing={{0}: (3, {})} | custom-call | flops 218103808 | bytes 3407872 | tf_op jit(solution)/shard_map/w_out_grad_kernel/pallas_call | solution.py:271
  55.7 0.3 collective-permute-done.14.refs_2_
  56.0 1.9 %collective-permute-start.15 = (bf16[64,1664]{1,0:T(8,128)(2,1)S(1)}, bf16[64,1664]{1,0:T(8,128)(2,1)S(1)}, u32[]{:S(2)}, u32[]{:S(2)}) collective-permute-start(bf16[64,1664]{1,0:T(8,128)(2,1)S(1)} %add.22.refs_0_), channel_id=1, source_target_pairs={{0,1},{2,4},{4,2},{6,7},{7,6},{5,3},{3,5},{1,0},{8,9},{10,12},{12,... | collective-permute-start | bytes 638984 | tf_op jit(solution)/shard_map/ppermute | solution.py:418
  57.9 2.1 %w_out_grad_kernel.5 = (f32[2,1024,1664]{2,1,0:T(8,128)}, f32[8,128]{1,0:T(8,128)S(1)}) custom-call(bf16[64,1664]{1,0:T(8,128)(2,1)S(1)} %add.22.refs_0_, bf16[2,128,1024]{2,1,0:T(8,128)(2,1)S(1)} %get-tuple-element.88.refs_1_, bf16[2,128,1664]{2,1,0:T(8,128)(2,1)S(1)} %get-tuple-element.59.refs_2_, ...), custom_call_target="tpu_custom_call", output_to_operand_aliasing={{0}: (3, {})} | custom-call | flops 218103808 | bytes 3407872 | tf_op jit(solution)/shard_map/w_out_grad_kernel/pallas_call | solution.py:271
  60.0 0.8 %collective-permute-done.16.refs_2_ = bf16[64,1664]{1,0:T(8,128)(2,1)S(1)} collective-permute-done((bf16[64,1664]{1,0:T(8,128)(2,1)S(1)}, bf16[64,1664]{1,0:T(8,128)(2,1)S(1)}, u32[]{:S(2)}, u32[]{:S(2)}) %collective-permute-start.16) | collective-permute-done | bytes 213024 | tf_op jit(solution)/shard_map/ppermute | solution.py:418
  60.8 1.5 %collective-permute-start.17 = (bf16[32,1664]{1,0:T(8,128)(2,1)S(1)}, bf16[32,1664]{1,0:T(8,128)(2,1)S(1)}, u32[]{:S(2)}, u32[]{:S(2)}) collective-permute-start(bf16[32,1664]{1,0:T(8,128)(2,1)S(1)} %get-tuple-element.75), channel_id=1, source_target_pairs={{0,2},{2,0},{1,3},{3,1},{4,6},{6,4},{5,7},{7,5},{8,10},{10,8},{9,1... | collective-permute-start | bytes 319496 | tf_op jit(solution)/shard_map/ppermute | solution.py:419
  62.3 0.8 collective-permute-done.15.refs_2_
  63.1 1.5 %collective-permute-start.18 = (bf16[32,1664]{1,0:T(8,128)(2,1)S(1)}, bf16[32,1664]{1,0:T(8,128)(2,1)S(1)}, u32[]{:S(2)}, u32[]{:S(2)}) collective-permute-start(bf16[32,1664]{1,0:T(8,128)(2,1)S(1)} %get-tuple-element.70.refs_0_), channel_id=1, source_target_pairs={{0,2},{2,0},{1,3},{3,1},{4,6},{6,4},{5,7},{7,5},{8,10},{10,8},{9,1... | collective-permute-start | bytes 319496 | tf_op jit(solution)/shard_map/ppermute | solution.py:419
  64.6 3.2 %w_in_grad_kernel.2 = (f32[2,1664,1024]{2,1,0:T(8,128)}, f32[8,128]{1,0:T(8,128)S(1)}) custom-call(bf16[32,1664]{1,0:T(8,128)(2,1)S(1)} %get-tuple-element.70.refs_0_, bf16[2,128,1024]{2,1,0:T(8,128)(2,1)S(1)} %get-tuple-element.71.refs_1_, bf16[2,128,1664]{2,1,0:T(8,128)(2,1)S(1)} %sort_rows.1.refs_2_), custom_call_target="tpu_custom_call" | custom-call | flops 436207616 | bytes 6815744 | tf_op jit(solution)/shard_map/w_in_grad_kernel/pallas_call | solution.py:271
  67.8 0.1 collective-permute-done.18.refs_4_
  67.9 0.2 join.1
  68.1 0.1 collective-permute-start.19
  68.2 1.5 %collective-permute-start.20 = (bf16[16,1664]{1,0:T(8,128)(2,1)S(1)}, bf16[16,1664]{1,0:T(8,128)(2,1)S(1)}, u32[]{:S(2)}, u32[]{:S(2)}) collective-permute-start(bf16[16,1664]{1,0:T(8,128)(2,1)S(1)} %get-tuple-element.79), channel_id=1, source_target_pairs={{0,16},{8,24},{16,0},{24,8},{1,17},{9,25},{17,1},{25,9},{2,18},{10... | collective-permute-start | bytes 159752 | tf_op jit(solution)/shard_map/ppermute | solution.py:425
  69.7 0.4 collective-permute-start.21
  70.1 3.8 %w_in_grad_kernel.3 = (f32[2,1664,1024]{2,1,0:T(8,128)}, f32[8,128]{1,0:T(8,128)}) custom-call(bf16[16,1664]{1,0:T(8,128)(2,1)S(1)} %get-tuple-element.77.refs_0_, bf16[2,128,1024]{2,1,0:T(8,128)(2,1)S(1)} %get-tuple-element.71.refs_1_, bf16[2,128,1664]{2,1,0:T(8,128)(2,1)S(1)} %sort_rows.1.refs_2_, ...), custom_call_target="tpu_custom_call", output_to_operand_aliasing={{0}: (3, {})} | custom-call | flops 436207616 | bytes 6815744 | tf_op jit(solution)/shard_map/w_in_grad_kernel/pallas_call | solution.py:271
  74.0 2.0 %finish.1 = (bf16[128,1664]{1,0:T(8,128)(2,1)}, bf16[128,1664]{1,0:T(8,128)(2,1)}, f32[2,128]{1,0:T(2,128)}) custom-call(s32[2,128]{1,0:T(2,128)S(1)} %bitcast.10, s32[2,128]{1,0:T(2,128)S(1)} %bitcast.12, s32[2,128]{1,0:T(2,128)S(1)} %bitcast.14, f32[2,128]{1,0:T(2,128)S(1)} %bitcast.16, bf16[128,1664]{1,0:T(8,128)(2,1)S(1)} %copy-done, ...), custom_call_target="tpu_custom_call" | custom-call | tf_op jit(solution)/shard_map/finish/pallas_call | solution.py:221
  (32 shorter events, 0.7 us)
Async XLA Ops:
  2.8 6.1 %collective-permute-start = (bf16[16,1664]{1,0:T(8,128)(2,1)}, bf16[16,1664]{1,0:T(8,128)(2,1)S(1)}, u32[]{:S(2)}, u32[]{:S(2)}) collective-permute-start(bf16[16,1664]{1,0:T(8,128)(2,1)} %get-tuple-element.48), channel_id=1, source_target_pairs={{0,8},{8,0},{16,24},{24,16},{1,9},{9,1},{17,25},{25,17},{2,10},{10... | collective-permute-start | bytes 159752 | tf_op jit(solution)/shard_map/ppermute | solution.py:425
  3.2 5.7 %collective-permute-start.1 = (bf16[16,1664]{1,0:T(8,128)(2,1)}, bf16[16,1664]{1,0:T(8,128)(2,1)S(1)}, u32[]{:S(2)}, u32[]{:S(2)}) collective-permute-start(bf16[16,1664]{1,0:T(8,128)(2,1)} %get-tuple-element.49), channel_id=1, source_target_pairs={{0,16},{8,24},{16,0},{24,8},{1,17},{9,25},{17,1},{25,9},{2,18},{10... | collective-permute-start | bytes 159752 | tf_op jit(solution)/shard_map/ppermute | solution.py:425
  5.7 4.0 %collective-permute-start.2 = (bf16[16,1664]{1,0:T(8,128)(2,1)}, bf16[16,1664]{1,0:T(8,128)(2,1)S(1)}, u32[]{:S(2)}, u32[]{:S(2)}) collective-permute-start(bf16[16,1664]{1,0:T(8,128)(2,1)} %get-tuple-element.50), channel_id=1, source_target_pairs={{0,24},{8,16},{16,8},{24,0},{1,25},{9,17},{17,9},{25,1},{2,26},{10... | collective-permute-start | bytes 159752 | tf_op jit(solution)/shard_map/ppermute | solution.py:425
  9.9 5.1 %collective-permute-start.3 = (bf16[32,1664]{1,0:T(8,128)(2,1)S(1)}, bf16[32,1664]{1,0:T(8,128)(2,1)S(1)}, u32[]{:S(2)}, u32[]{:S(2)}) collective-permute-start(bf16[32,1664]{1,0:T(8,128)(2,1)S(1)} %get-tuple-element.51.refs_0_), channel_id=1, source_target_pairs={{0,1},{2,4},{4,2},{6,7},{7,6},{5,3},{3,5},{1,0},{8,9},{10,12},{12,... | collective-permute-start | bytes 319496 | tf_op jit(solution)/shard_map/ppermute | solution.py:418
  11.5 4.7 %collective-permute-start.4 = (bf16[32,1664]{1,0:T(8,128)(2,1)S(1)}, bf16[32,1664]{1,0:T(8,128)(2,1)S(1)}, u32[]{:S(2)}, u32[]{:S(2)}) collective-permute-start(bf16[32,1664]{1,0:T(8,128)(2,1)S(1)} %get-tuple-element.52.refs_1_), channel_id=1, source_target_pairs={{0,2},{2,0},{1,3},{3,1},{4,6},{6,4},{5,7},{7,5},{8,10},{10,8},{9,1... | collective-permute-start | bytes 319496 | tf_op jit(solution)/shard_map/ppermute | solution.py:419
  16.3 6.2 %collective-permute-start.5 = (bf16[64,1664]{1,0:T(8,128)(2,1)S(1)}, bf16[64,1664]{1,0:T(8,128)(2,1)S(1)}, u32[]{:S(2)}, u32[]{:S(2)}) collective-permute-start(bf16[64,1664]{1,0:T(8,128)(2,1)S(1)} %pair.2.refs_0_), channel_id=1, source_target_pairs={{0,1},{2,4},{4,2},{6,7},{7,6},{5,3},{3,5},{1,0},{8,9},{10,12},{12,... | collective-permute-start | bytes 638984 | tf_op jit(solution)/shard_map/ppermute | solution.py:418
  17.8 6.4 %collective-permute-start.10 = (bf16[64,1664]{1,0:T(8,128)(2,1)S(1)}, bf16[64,1664]{1,0:T(8,128)(2,1)S(1)}, u32[]{:S(2)}, u32[]{:S(2)}) collective-permute-start(bf16[64,1664]{1,0:T(8,128)(2,1)S(1)} %pair.3.refs_1_.refs_0_), channel_id=1, source_target_pairs={{0,2},{2,0},{1,3},{3,1},{4,6},{6,4},{5,7},{7,5},{8,10},{10,8},{9,1... | collective-permute-start | bytes 638984 | tf_op jit(solution)/shard_map/ppermute | solution.py:419
  22.5 6.1 %collective-permute-start.6 = (bf16[64,1664]{1,0:T(8,128)(2,1)S(1)}, bf16[64,1664]{1,0:T(8,128)(2,1)S(1)}, u32[]{:S(2)}, u32[]{:S(2)}) collective-permute-start(bf16[64,1664]{1,0:T(8,128)(2,1)S(1)} %pass.1.refs_1_), channel_id=1, source_target_pairs={{0,2},{2,0},{1,3},{3,1},{4,6},{6,4},{5,7},{7,5},{8,10},{10,8},{9,1... | collective-permute-start | bytes 638984 | tf_op jit(solution)/shard_map/ppermute | solution.py:419
  24.2 6.7 %collective-permute-start.11 = (bf16[64,1664]{1,0:T(8,128)(2,1)S(1)}, bf16[64,1664]{1,0:T(8,128)(2,1)S(1)}, u32[]{:S(2)}, u32[]{:S(2)}) collective-permute-start(bf16[64,1664]{1,0:T(8,128)(2,1)S(1)} %collective-permute-done.10.refs_1_), channel_id=1, source_target_pairs={{0,1},{2,4},{4,2},{6,7},{7,6},{5,3},{3,5},{1,0},{8,9},{10,12},{12,... | collective-permute-start | bytes 638984 | tf_op jit(solution)/shard_map/ppermute | solution.py:418
  28.6 6.0 %collective-permute-start.7 = (bf16[64,1664]{1,0:T(8,128)(2,1)S(1)}, bf16[64,1664]{1,0:T(8,128)(2,1)S(1)}, u32[]{:S(2)}, u32[]{:S(2)}) collective-permute-start(bf16[64,1664]{1,0:T(8,128)(2,1)S(1)} %collective-permute-done.6.refs_2_), channel_id=1, source_target_pairs={{0,1},{2,4},{4,2},{6,7},{7,6},{5,3},{3,5},{1,0},{8,9},{10,12},{12,... | collective-permute-start | bytes 638984 | tf_op jit(solution)/shard_map/ppermute | solution.py:418
  30.9 8.2 %collective-permute-start.12 = (bf16[64,1664]{1,0:T(8,128)(2,1)S(1)}, bf16[64,1664]{1,0:T(8,128)(2,1)S(1)}, u32[]{:S(2)}, u32[]{:S(2)}) collective-permute-start(bf16[64,1664]{1,0:T(8,128)(2,1)S(1)} %collective-permute-done.11.refs_2_), channel_id=1, source_target_pairs={{0,2},{2,0},{1,3},{3,1},{4,6},{6,4},{5,7},{7,5},{8,10},{10,8},{9,1... | collective-permute-start | bytes 638984 | tf_op jit(solution)/shard_map/ppermute | solution.py:419
  37.5 5.9 %collective-permute-start.8 = (bf16[64,1664]{1,0:T(8,128)(2,1)S(1)}, bf16[64,1664]{1,0:T(8,128)(2,1)S(1)}, u32[]{:S(2)}, u32[]{:S(2)}) collective-permute-start(bf16[64,1664]{1,0:T(8,128)(2,1)S(1)} %get-tuple-element.58.after_ref), channel_id=1, source_target_pairs={{0,1},{2,4},{4,2},{6,7},{7,6},{5,3},{3,5},{1,0},{8,9},{10,12},{12,... | collective-permute-start | bytes 638984 | tf_op jit(solution)/shard_map/ppermute | solution.py:418
  43.6 6.4 %collective-permute-start.13 = (bf16[64,1664]{1,0:T(8,128)(2,1)S(1)}, bf16[64,1664]{1,0:T(8,128)(2,1)S(1)}, u32[]{:S(2)}, u32[]{:S(2)}) collective-permute-start(bf16[64,1664]{1,0:T(8,128)(2,1)S(1)} %get-tuple-element.61.refs_0_), channel_id=1, source_target_pairs={{0,1},{2,4},{4,2},{6,7},{7,6},{5,3},{3,5},{1,0},{8,9},{10,12},{12,... | collective-permute-start | bytes 638984 | tf_op jit(solution)/shard_map/ppermute | solution.py:418
  45.5 7.8 %collective-permute-start.9 = (bf16[64,1664]{1,0:T(8,128)(2,1)S(1)}, bf16[64,1664]{1,0:T(8,128)(2,1)S(1)}, u32[]{:S(2)}, u32[]{:S(2)}) collective-permute-start(bf16[64,1664]{1,0:T(8,128)(2,1)S(1)} %add.19.after_ref), channel_id=1, source_target_pairs={{0,2},{2,0},{1,3},{3,1},{4,6},{6,4},{5,7},{7,5},{8,10},{10,8},{9,1... | collective-permute-start | bytes 638984 | tf_op jit(solution)/shard_map/ppermute | solution.py:419
  50.0 5.9 %collective-permute-start.14 = (bf16[64,1664]{1,0:T(8,128)(2,1)S(1)}, bf16[64,1664]{1,0:T(8,128)(2,1)S(1)}, u32[]{:S(2)}, u32[]{:S(2)}) collective-permute-start(bf16[64,1664]{1,0:T(8,128)(2,1)S(1)} %add.21), channel_id=1, source_target_pairs={{0,2},{2,0},{1,3},{3,1},{4,6},{6,4},{5,7},{7,5},{8,10},{10,8},{9,1... | collective-permute-start | bytes 638984 | tf_op jit(solution)/shard_map/ppermute | solution.py:419
  53.4 7.4 %collective-permute-start.16 = (bf16[64,1664]{1,0:T(8,128)(2,1)S(1)}, bf16[64,1664]{1,0:T(8,128)(2,1)S(1)}, u32[]{:S(2)}, u32[]{:S(2)}) collective-permute-start(bf16[64,1664]{1,0:T(8,128)(2,1)S(1)} %add.20.refs_0_), channel_id=1, source_target_pairs={{0,1},{2,4},{4,2},{6,7},{7,6},{5,3},{3,5},{1,0},{8,9},{10,12},{12,... | collective-permute-start | bytes 638984 | tf_op jit(solution)/shard_map/ppermute | solution.py:418
  56.0 7.0 %collective-permute-start.15 = (bf16[64,1664]{1,0:T(8,128)(2,1)S(1)}, bf16[64,1664]{1,0:T(8,128)(2,1)S(1)}, u32[]{:S(2)}, u32[]{:S(2)}) collective-permute-start(bf16[64,1664]{1,0:T(8,128)(2,1)S(1)} %add.22.refs_0_), channel_id=1, source_target_pairs={{0,1},{2,4},{4,2},{6,7},{7,6},{5,3},{3,5},{1,0},{8,9},{10,12},{12,... | collective-permute-start | bytes 638984 | tf_op jit(solution)/shard_map/ppermute | solution.py:418
  60.8 6.9 %collective-permute-start.17 = (bf16[32,1664]{1,0:T(8,128)(2,1)S(1)}, bf16[32,1664]{1,0:T(8,128)(2,1)S(1)}, u32[]{:S(2)}, u32[]{:S(2)}) collective-permute-start(bf16[32,1664]{1,0:T(8,128)(2,1)S(1)} %get-tuple-element.75), channel_id=1, source_target_pairs={{0,2},{2,0},{1,3},{3,1},{4,6},{6,4},{5,7},{7,5},{8,10},{10,8},{9,1... | collective-permute-start | bytes 319496 | tf_op jit(solution)/shard_map/ppermute | solution.py:419
  63.1 4.8 %collective-permute-start.18 = (bf16[32,1664]{1,0:T(8,128)(2,1)S(1)}, bf16[32,1664]{1,0:T(8,128)(2,1)S(1)}, u32[]{:S(2)}, u32[]{:S(2)}) collective-permute-start(bf16[32,1664]{1,0:T(8,128)(2,1)S(1)} %get-tuple-element.70.refs_0_), channel_id=1, source_target_pairs={{0,2},{2,0},{1,3},{3,1},{4,6},{6,4},{5,7},{7,5},{8,10},{10,8},{9,1... | collective-permute-start | bytes 319496 | tf_op jit(solution)/shard_map/ppermute | solution.py:419
  68.1 5.7 %collective-permute-start.19 = (bf16[16,1664]{1,0:T(8,128)(2,1)S(1)}, bf16[16,1664]{1,0:T(8,128)(2,1)S(1)}, u32[]{:S(2)}, u32[]{:S(2)}) collective-permute-start(bf16[16,1664]{1,0:T(8,128)(2,1)S(1)} %get-tuple-element.78), channel_id=1, source_target_pairs={{0,8},{8,0},{16,24},{24,16},{1,9},{9,1},{17,25},{25,17},{2,10},{10... | collective-permute-start | bytes 159752 | tf_op jit(solution)/shard_map/ppermute | solution.py:425
  68.2 5.7 %collective-permute-start.20 = (bf16[16,1664]{1,0:T(8,128)(2,1)S(1)}, bf16[16,1664]{1,0:T(8,128)(2,1)S(1)}, u32[]{:S(2)}, u32[]{:S(2)}) collective-permute-start(bf16[16,1664]{1,0:T(8,128)(2,1)S(1)} %get-tuple-element.79), channel_id=1, source_target_pairs={{0,16},{8,24},{16,0},{24,8},{1,17},{9,25},{17,1},{25,9},{2,18},{10... | collective-permute-start | bytes 159752 | tf_op jit(solution)/shard_map/ppermute | solution.py:425
  69.7 4.2 %collective-permute-start.21 = (bf16[16,1664]{1,0:T(8,128)(2,1)S(1)}, bf16[16,1664]{1,0:T(8,128)(2,1)S(1)}, u32[]{:S(2)}, u32[]{:S(2)}) collective-permute-start(bf16[16,1664]{1,0:T(8,128)(2,1)S(1)} %get-tuple-element.80), channel_id=1, source_target_pairs={{0,24},{8,16},{16,8},{24,0},{1,25},{9,17},{17,9},{25,1},{2,26},{10... | collective-permute-start | bytes 159752 | tf_op jit(solution)/shard_map/ppermute | solution.py:425
  70.1 3.8 %copy-start = (bf16[128,1664]{1,0:T(8,128)(2,1)S(1)}, bf16[128,1664]{1,0:T(8,128)(2,1)}, u32[]{:S(2)}) copy-start(bf16[128,1664]{1,0:T(8,128)(2,1)} %out_grad_ref.3) | copy-start | bytes 1277956
  70.1 3.8 %copy-start.1 = (s32[128,2]{0,1:T(2,128)S(1)}, s32[128,2]{0,1:T(2,128)}, u32[]{:S(2)}) copy-start(s32[128,2]{0,1:T(2,128)} %param.9) | copy-start | bytes 3076
  70.1 3.9 %copy-start.2 = (s32[128,2]{0,1:T(2,128)S(1)}, s32[128,2]{0,1:T(2,128)}, u32[]{:S(2)}) copy-start(s32[128,2]{0,1:T(2,128)} %param.10) | copy-start | bytes 3076
  70.1 3.9 %copy-start.3 = (s32[128,2]{0,1:T(2,128)S(1)}, s32[128,2]{0,1:T(2,128)}, u32[]{:S(2)}) copy-start(s32[128,2]{0,1:T(2,128)} %param.11) | copy-start | bytes 3076
  70.1 3.9 %copy-start.4 = (f32[128,2]{0,1:T(2,128)S(1)}, f32[128,2]{0,1:T(2,128)}, u32[]{:S(2)}) copy-start(f32[128,2]{0,1:T(2,128)} %param.12) | copy-start | bytes 3076

commit v5 on v4

--- a/solution.py
+++ b/solution.py
@@ -83,27 +83,23 @@
 def finish_kernel(
     ids_ref, slot_ref, dropped_ref, gates_ref, out_grad_ref, *refs, exp_local
 ):
-    parts, outs, (made, sems) = refs[:-5], refs[-5:-2], refs[-2:]
-    mixed_ref, tok_grad_ref, gate_grad_ref = outs
+    parts, (mixed_ref, tok_grad_ref, gate_grad_ref) = refs[:-3], refs[-3:]
     returned, returned_grad = [rows.astype(jnp.bfloat16) for rows in stack_halves(parts)]
     masks = slot_masks(ids_ref, slot_ref, dropped_ref, exp_local, returned.shape[0])
     select = sum(mask.astype(jnp.float32) for mask in masks).astype(jnp.bfloat16)
-    made[0] = contract(select, returned_grad, 0, 0).astype(jnp.bfloat16)
-    copies = [pltpu.make_async_copy(made.at[0], tok_grad_ref, sems.at[0])]
-    copies[0].start()
+    tok_grad_ref[...] = contract(select, returned_grad, 0, 0).astype(jnp.bfloat16)
     tokens = gates_ref.shape[1]
     gates = jnp.concatenate([gates_ref[...], jnp.zeros((6, tokens), jnp.float32)], axis=0).T
     wide = out_grad_ref[...].astype(jnp.float32)
-    all_picked = [contract(mask.astype(jnp.bfloat16), returned, 0, 0) for mask in masks]
-    mixed = sum(gates[:, k : k + 1] * picked for k, picked in enumerate(all_picked))
-    made[1] = mixed.astype(jnp.bfloat16)
-    copies.append(pltpu.make_async_copy(made.at[1], mixed_ref, sems.at[1]))
-    copies[1].start()
-    grads = [jnp.sum(picked * wide, axis=1, keepdims=True) for picked in all_picked]
+    mixed = jnp.zeros(wide.shape, jnp.float32)
+    grads = []
+    for k, mask in enumerate(masks):
+        picked = contract(mask.astype(jnp.bfloat16), returned, 0, 0)
+        mixed = mixed + gates[:, k : k + 1] * picked
+        grads.append(jnp.sum(picked * wide, axis=1, keepdims=True))
+    mixed_ref[...] = mixed.astype(jnp.bfloat16)
     grads.append(jnp.zeros((tokens, 6), jnp.float32))
     gate_grad_ref[...] = jnp.concatenate(grads, axis=1).T[:2]
-    for copy in copies:
-        copy.wait()
 
 
 def split_kernel(after_ref, *refs, exp_local):
@@ -216,15 +212,12 @@
 
 
 def finish(choices, gates, out_grad, parts, exp_local):
-    by_token = jax.ShapeDtypeStruct(out_grad.shape, jnp.bfloat16)
-    anywhere = pl.BlockSpec(memory_space=pl.ANY)
     return pl.pallas_call(
         functools.partial(finish_kernel, exp_local=exp_local),
-        out_specs=[anywhere, anywhere, pl.BlockSpec(memory_space=pltpu.VMEM)],
-        out_shape=[by_token, by_token, jax.ShapeDtypeStruct(gates.shape, jnp.float32)],
-        scratch_shapes=[
-            pltpu.VMEM((2,) + out_grad.shape, jnp.bfloat16),
-            pltpu.SemaphoreType.DMA((2,)),
+        out_shape=[
+            jax.ShapeDtypeStruct(out_grad.shape, jnp.bfloat16),
+            jax.ShapeDtypeStruct(out_grad.shape, jnp.bfloat16),
+            jax.ShapeDtypeStruct(gates.shape, jnp.float32),
         ],
         compiler_params=params(out_grad.shape[0]),
         name="finish",
@@ -307,26 +300,6 @@
             blocks[i // 2][at : at + part] = in_ref[expert, i * part : (i + 1) * part]
 
 
-def backward_kernel(after_ref, *refs, places):
-    blocks, (slope_ref, w_in_ref, w_out_ref) = refs[:-7], refs[-7:-4]
-    rows_ref, pre_grad_ref, row_grad_ref, turned = refs[-4:]
-    experts, units, width = w_out_ref.shape
-    step = min(2 * CHUNK, units)
-    sort_kernel(after_ref, *blocks, rows_ref, places=places)
-    for expert in range(experts):
-        grads = rows_ref[expert].T
-        for at in range(0, units, step):
-            here = slice(at, at + step)
-            hidden_grad = contract(w_out_ref[expert, here], grads, 1, 0)
-            pre_grad = (hidden_grad * slope_ref[expert, :, here].T).astype(jnp.bfloat16)
-            turned[here] = pre_grad
-            pre_grad_ref[expert, :, here] = pre_grad.T
-        for at in range(0, width, CHUNK):
-            here = slice(at, min(at + CHUNK, width))
-            row_grad = contract(w_in_ref[expert, here], turned[...], 1, 0)
-            row_grad_ref[expert, :, here] = row_grad.T.astype(jnp.bfloat16)
-
-
 def order_cost(count, width):
     return pl.CostEstimate(
         flops=2 * count * count * width, bytes_accessed=4 * count * width, transcendentals=0
@@ -345,26 +318,6 @@
         cost_estimate=order_cost(experts * rows, width),
         name="sort_rows",
     )(after, *blocks)
-
-
-def backward(blocks, slope, w_in, w_out, places, after):
-    experts, units, width = w_out.shape
-    rows = slope.shape[1]
-    by_row = jax.ShapeDtypeStruct((experts, rows, width), jnp.bfloat16)
-    return pl.pallas_call(
-        functools.partial(backward_kernel, places=places),
-        in_specs=[pl.BlockSpec(memory_space=pl.ANY)]
-        + [pl.BlockSpec(memory_space=pltpu.VMEM)] * (len(blocks) + 3),
-        out_shape=[by_row, jax.ShapeDtypeStruct(slope.shape, jnp.bfloat16), by_row],
-        scratch_shapes=[pltpu.VMEM((units, rows), jnp.bfloat16)],
-        compiler_params=pltpu.CompilerParams(vmem_limit_bytes=(10 << 20) + rows * (40 << 10)),
-        cost_estimate=pl.CostEstimate(
-            flops=4 * experts * rows * width * units,
-            bytes_accessed=4 * experts * rows * width,
-            transcendentals=0,
-        ),
-        name="backward",
-    )(after, *blocks, slope, w_in, w_out)
 
 
 def unsort_rows(rows, steps, after):
@@ -460,8 +413,13 @@
     hidden = gelu_exact(pre).astype(jnp.bfloat16)
     output = jnp.einsum("xmf,xfd->xmd", hidden, held_out, preferred_element_type=jnp.float32)
     out_blocks = unsort_rows(output.astype(jnp.bfloat16), steps, done_out)
-    grad_rows, pre_grad, row_grad = backward(
-        grad_blocks, gelu_slope(pre), held_in, held_out, regroup(n_dp), out_blocks[-1]
+    grad_rows = sort_rows(grad_blocks, exp_local, regroup(n_dp), out_blocks[-1])
+    hidden_grad = jnp.einsum(
+        "xmd,xfd->xmf", grad_rows, held_out, preferred_element_type=jnp.float32
+    )
+    pre_grad = (hidden_grad * gelu_slope(pre)).astype(jnp.bfloat16)
+    row_grad = jnp.einsum(
+        "xmf,xdf->xmd", pre_grad, held_in, preferred_element_type=jnp.float32
     )
 
     def out_piece(expert, part, parts):
@@ -471,8 +429,8 @@
         return (w_in_grad_kernel, pre_grad, rows, w_in.shape, expert, part, parts)
 
     others, final = range(exp_local - 1), exp_local - 1
-    work = [out_piece(x, 0, 1) for x in others] + [out_piece(final, part, 2) for part in (0, 1)]
-    work += [in_piece(x, 0, 1) for x in range(exp_local)]
+    work = [out_piece(x, 0, 1) for x in others] + [out_piece(final, 0, 2)]
+    work += [in_piece(x, 0, 1) for x in others] + [out_piece(final, 1, 2), in_piece(final, 0, 1)]
     made = {}
 
     def next_piece(after):
@@ -500,7 +458,7 @@
         out_sum = add_step(ready, out_blocks[step - 1], out_arrived, step)
         out_arrived = swap(out_sum[-1], step % 2 == 0)
         if step == last:
-            back_blocks = unsort_rows(row_grad, steps, out_sum[0])
+            back_blocks = unsort_rows(row_grad.astype(jnp.bfloat16), steps, out_sum[0])
             back_sum = back_blocks[last:]
             back_arrived = swap(back_sum[-1], step % 2 == 1)
             ready = [next_piece(back_sum[-1])]

time: 76.1 us -> 75 us (0.986)
  Pallas kernels: 29.6 us -> 25 us
  matrix products: 2.75 us -> 7.26 us
  waiting for transfers between devices: 12.4 us -> 10.7 us
    dot_general x0 -> x2, matrix products: none -> 4.7 us  [the longest x1 2.37 us: per_device(): jnp.einsum('xmd,xfd->xmf', grad_rows, held_out, preferred_element_type=jn...]
    pallas_call x1 -> x0, Pallas kernels: 4.05 us -> none  [backward(): pl.pallas_call(functools.partial(backward_kernel, places=places), in_spec...]
    ppermute x8, waiting for transfers between devices: 5.54 us -> 4.32 us  [swap(): return lax.ppermute(block, DP, odd_edges(lax.axis_size(DP)))]
  transfers between devices with their start and end apart: 22 -> 22, of which waited for: 13 -> 11; matrix products, arithmetic and copies ran while one was open for 4% -> 10% of each run, Pallas kernels for 33% -> 28%
where the time goes in v5:
time: 75 us; the launch traced here: 74.9 us
  starting transfers between devices  31 us (41%)
  Pallas kernels  25 us (33%)
  waiting for transfers between devices  10.7 us (14%)
  matrix products  7.26 us (10%)
  between operations  0.93 us (1%)
    pallas_call x5, Pallas kernels, weight_gradient(): pl.pallas_call(functools.partial(kernel, skip=len(after), expert=expert,...  14.3 us
    ppermute x8, starting transfers between devices, swap(): return lax.ppermute(block, 'near', [(0, 1), (1, 0)])  14.2 us
    ppermute x8, starting transfers between devices, swap(): return lax.ppermute(block, DP, odd_edges(lax.axis_size(DP)))  11.7 us
    pallas_call x2, Pallas kernels, hold(): pl.pallas_call(hold_kernel, in_specs=[pl.BlockSpec(memory_space=pl.ANY)]...  6.04 us
    ppermute x8, waiting for transfers between devices, swap(): return lax.ppermute(block, 'near', [(0, 1), (1, 0)])  5.53 us
    ppermute x6, starting transfers between devices, expert_swap(): lax.ppermute(blocks[k], 'expert', [(i, i ^ k) for i in range(size)])  5.02 us
    ppermute x8, waiting for transfers between devices, swap(): return lax.ppermute(block, DP, odd_edges(lax.axis_size(DP)))  4.32 us
    dot_general x1, matrix products, per_device(): jnp.einsum('xmd,xfd->xmf', grad_rows, held_out, preferred_element_type=jn...  2.37 us
  transfers between devices with their start and end apart: 22, of which 11 were waited for; matrix products, arithmetic and copies ran while one was open for 10% of the time, Pallas kernels for 28%

profile of v5, /device:TPU:0, one launch (start us, length us, event | category | flops | bytes accessed | tf_op | source)
XLA Modules:
  0.0 74.9 jit_solution(7891122313297040357)
XLA Ops:
  0.6 2.1 %prepare.1 = (bf16[16,1664]{1,0:T(8,128)(2,1)S(1)}, bf16[16,1664]{1,0:T(8,128)(2,1)}, bf16[16,1664]{1,0:T(8,128)(2,1)}, bf16[16,1664]{1,0:T(8,128)(2,1)}) custom-call(s32[2,128]{1,0:T(2,128)} %bitcast.13, s32[2,128]{1,0:T(2,128)} %bitcast.15, s32[2,128]{1,0:T(2,128)} %bitcast.17, f32[2,128]{1,0:T(2,128)} %bitcast.19, bf16[128,1664]{1,0:T(8,128)(2,1)} %tokens_ref.1, ...), custom_call_target="tpu_custom_call" | custom-call | tf_op jit(solution)/shard_map/prepare/pallas_call | solution.py:204
  2.8 0.4 collective-permute-start
  3.2 2.5 %collective-permute-start.1 = (bf16[16,1664]{1,0:T(8,128)(2,1)}, bf16[16,1664]{1,0:T(8,128)(2,1)S(1)}, u32[]{:S(2)}, u32[]{:S(2)}) collective-permute-start(bf16[16,1664]{1,0:T(8,128)(2,1)} %get-tuple-element.46), channel_id=1, source_target_pairs={{0,16},{8,24},{16,0},{24,8},{1,17},{9,25},{17,1},{25,9},{2,18},{10... | collective-permute-start | bytes 159752 | tf_op jit(solution)/shard_map/ppermute | solution.py:378
  5.7 0.1 collective-permute-start.2
  5.8 3.0 %hold.2 = (bf16[2,1664,1024]{2,1,0:T(8,128)(2,1)S(1)}, f32[8,128]{1,0:T(8,128)S(1)}) custom-call(bf16[2,1664,1024]{2,1,0:T(8,128)(2,1)} %refs_0_.1), custom_call_target="tpu_custom_call" | custom-call | bytes 13631488 | tf_op jit(solution)/shard_map/hold/pallas_call | solution.py:242
  8.9 0.8 %collective-permute-done.2.refs_3_ = bf16[16,1664]{1,0:T(8,128)(2,1)S(1)} collective-permute-done((bf16[16,1664]{1,0:T(8,128)(2,1)}, bf16[16,1664]{1,0:T(8,128)(2,1)S(1)}, u32[]{:S(2)}, u32[]{:S(2)}) %collective-permute-start.2) | collective-permute-done | bytes 53280 | tf_op jit(solution)/shard_map/ppermute | solution.py:378
  9.7 0.2 split.1
  9.9 1.6 %collective-permute-start.3 = (bf16[32,1664]{1,0:T(8,128)(2,1)S(1)}, bf16[32,1664]{1,0:T(8,128)(2,1)S(1)}, u32[]{:S(2)}, u32[]{:S(2)}) collective-permute-start(bf16[32,1664]{1,0:T(8,128)(2,1)S(1)} %get-tuple-element.48.refs_0_), channel_id=1, source_target_pairs={{0,1},{2,4},{4,2},{6,7},{7,6},{5,3},{3,5},{1,0},{8,9},{10,12},{12,... | collective-permute-start | bytes 319496 | tf_op jit(solution)/shard_map/ppermute | solution.py:371
  11.5 1.6 %collective-permute-start.4 = (bf16[32,1664]{1,0:T(8,128)(2,1)S(1)}, bf16[32,1664]{1,0:T(8,128)(2,1)S(1)}, u32[]{:S(2)}, u32[]{:S(2)}) collective-permute-start(bf16[32,1664]{1,0:T(8,128)(2,1)S(1)} %get-tuple-element.49.refs_1_), channel_id=1, source_target_pairs={{0,2},{2,0},{1,3},{3,1},{4,6},{6,4},{5,7},{7,5},{8,10},{10,8},{9,1... | collective-permute-start | bytes 319496 | tf_op jit(solution)/shard_map/ppermute | solution.py:372
  13.1 1.9 %collective-permute-done.3.refs_0_.refs_1_ = bf16[32,1664]{1,0:T(8,128)(2,1)S(1)} collective-permute-done((bf16[32,1664]{1,0:T(8,128)(2,1)S(1)}, bf16[32,1664]{1,0:T(8,128)(2,1)S(1)}, u32[]{:S(2)}, u32[]{:S(2)}) %collective-permute-start.3) | collective-permute-done | bytes 106528 | tf_op jit(solution)/shard_map/ppermute | solution.py:371
  15.0 1.2 %collective-permute-done.4.refs_2_ = bf16[32,1664]{1,0:T(8,128)(2,1)S(1)} collective-permute-done((bf16[32,1664]{1,0:T(8,128)(2,1)S(1)}, bf16[32,1664]{1,0:T(8,128)(2,1)S(1)}, u32[]{:S(2)}, u32[]{:S(2)}) %collective-permute-start.4) | collective-permute-done | bytes 106528 | tf_op jit(solution)/shard_map/ppermute | solution.py:372
  16.3 1.5 %collective-permute-start.5 = (bf16[64,1664]{1,0:T(8,128)(2,1)S(1)}, bf16[64,1664]{1,0:T(8,128)(2,1)S(1)}, u32[]{:S(2)}, u32[]{:S(2)}) collective-permute-start(bf16[64,1664]{1,0:T(8,128)(2,1)S(1)} %pair.2.refs_0_), channel_id=1, source_target_pairs={{0,1},{2,4},{4,2},{6,7},{7,6},{5,3},{3,5},{1,0},{8,9},{10,12},{12,... | collective-permute-start | bytes 638984 | tf_op jit(solution)/shard_map/ppermute | solution.py:371
  17.8 1.6 %collective-permute-start.10 = (bf16[64,1664]{1,0:T(8,128)(2,1)S(1)}, bf16[64,1664]{1,0:T(8,128)(2,1)S(1)}, u32[]{:S(2)}, u32[]{:S(2)}) collective-permute-start(bf16[64,1664]{1,0:T(8,128)(2,1)S(1)} %pair.3.refs_1_.refs_0_), channel_id=1, source_target_pairs={{0,2},{2,0},{1,3},{3,1},{4,6},{6,4},{5,7},{7,5},{8,10},{10,8},{9,1... | collective-permute-start | bytes 638984 | tf_op jit(solution)/shard_map/ppermute | solution.py:372
  19.4 3.0 %hold.3 = (bf16[2,1024,1664]{2,1,0:T(8,128)(2,1)S(1)}, f32[8,128]{1,0:T(8,128)S(1)}) custom-call(bf16[64,1664]{1,0:T(8,128)(2,1)S(1)} %pair.2.refs_0_, bf16[64,1664]{1,0:T(8,128)(2,1)S(1)} %pair.3.refs_1_.refs_0_, bf16[2,1024,1664]{2,1,0:T(8,128)(2,1)} %refs_2_.1), custom_call_target="tpu_custom_call" | custom-call | bytes 13631488 | tf_op jit(solution)/shard_map/hold/pallas_call | solution.py:242
  22.5 1.7 %collective-permute-start.6 = (bf16[64,1664]{1,0:T(8,128)(2,1)S(1)}, bf16[64,1664]{1,0:T(8,128)(2,1)S(1)}, u32[]{:S(2)}, u32[]{:S(2)}) collective-permute-start(bf16[64,1664]{1,0:T(8,128)(2,1)S(1)} %pass.1.refs_1_), channel_id=1, source_target_pairs={{0,2},{2,0},{1,3},{3,1},{4,6},{6,4},{5,7},{7,5},{8,10},{10,8},{9,1... | collective-permute-start | bytes 638984 | tf_op jit(solution)/shard_map/ppermute | solution.py:372
  24.2 1.5 %collective-permute-start.11 = (bf16[64,1664]{1,0:T(8,128)(2,1)S(1)}, bf16[64,1664]{1,0:T(8,128)(2,1)S(1)}, u32[]{:S(2)}, u32[]{:S(2)}) collective-permute-start(bf16[64,1664]{1,0:T(8,128)(2,1)S(1)} %collective-permute-done.10.refs_1_), channel_id=1, source_target_pairs={{0,1},{2,4},{4,2},{6,7},{7,6},{5,3},{3,5},{1,0},{8,9},{10,12},{12,... | collective-permute-start | bytes 638984 | tf_op jit(solution)/shard_map/ppermute | solution.py:371
  25.7 2.9 %collective-permute-done.6.refs_2_ = bf16[64,1664]{1,0:T(8,128)(2,1)S(1)} collective-permute-done((bf16[64,1664]{1,0:T(8,128)(2,1)S(1)}, bf16[64,1664]{1,0:T(8,128)(2,1)S(1)}, u32[]{:S(2)}, u32[]{:S(2)}) %collective-permute-start.6) | collective-permute-done | bytes 213024 | tf_op jit(solution)/shard_map/ppermute | solution.py:372
  28.6 1.6 %collective-permute-start.7 = (bf16[64,1664]{1,0:T(8,128)(2,1)S(1)}, bf16[64,1664]{1,0:T(8,128)(2,1)S(1)}, u32[]{:S(2)}, u32[]{:S(2)}) collective-permute-start(bf16[64,1664]{1,0:T(8,128)(2,1)S(1)} %collective-permute-done.6.refs_2_), channel_id=1, source_target_pairs={{0,1},{2,4},{4,2},{6,7},{7,6},{5,3},{3,5},{1,0},{8,9},{10,12},{12,... | collective-permute-start | bytes 638984 | tf_op jit(solution)/shard_map/ppermute | solution.py:371
  30.1 0.8 %collective-permute-done.11.refs_2_ = bf16[64,1664]{1,0:T(8,128)(2,1)S(1)} collective-permute-done((bf16[64,1664]{1,0:T(8,128)(2,1)S(1)}, bf16[64,1664]{1,0:T(8,128)(2,1)S(1)}, u32[]{:S(2)}, u32[]{:S(2)}) %collective-permute-start.11) | collective-permute-done | bytes 213024 | tf_op jit(solution)/shard_map/ppermute | solution.py:371
  30.9 2.6 %collective-permute-start.12 = (bf16[64,1664]{1,0:T(8,128)(2,1)S(1)}, bf16[64,1664]{1,0:T(8,128)(2,1)S(1)}, u32[]{:S(2)}, u32[]{:S(2)}) collective-permute-start(bf16[64,1664]{1,0:T(8,128)(2,1)S(1)} %collective-permute-done.11.refs_2_), channel_id=1, source_target_pairs={{0,2},{2,0},{1,3},{3,1},{4,6},{6,4},{5,7},{7,5},{8,10},{10,8},{9,1... | collective-permute-start | bytes 638984 | tf_op jit(solution)/shard_map/ppermute | solution.py:372
  33.6 1.0 %collective-permute-done.7.refs_3_ = bf16[64,1664]{1,0:T(8,128)(2,1)S(1)} collective-permute-done((bf16[64,1664]{1,0:T(8,128)(2,1)S(1)}, bf16[64,1664]{1,0:T(8,128)(2,1)S(1)}, u32[]{:S(2)}, u32[]{:S(2)}) %collective-permute-start.7) | collective-permute-done | bytes 213024 | tf_op jit(solution)/shard_map/ppermute | solution.py:371
  34.7 1.4 %multiply_convert_fusion = (bf16[2,128,1024]{2,1,0:T(8,128)(2,1)S(1)}, f32[2,128,1024]{2,1,0:T(8,128)S(1)}) fusion(bf16[2,128,1664]{2,1,0:T(8,128)(2,1)S(1)} %sort_rows.2.refs_2_, bf16[2,1664,1024]{2,1,0:T(8,128)(2,1)S(1)} %get-tuple-element.51), kind=kOutput, calls=%fused_computation.9 | convolution fusion | flops 873725952 | bytes 9240576 | tf_op jit(solution)/shard_map/xmd,xdf->xmf/dot_general | solution.py:412
  36.1 1.2 %convolution_convert_fusion.1.in_ref = bf16[2,128,1664]{2,1,0:T(8,128)(2,1)S(1)} fusion(bf16[2,128,1024]{2,1,0:T(8,128)(2,1)S(1)} %get-tuple-element.81.refs_1_, bf16[2,1024,1664]{2,1,0:T(8,128)(2,1)S(1)} %get-tuple-element.52), kind=kOutput, calls=%fused_computation.1 | convolution fusion | flops 872841216 | bytes 8192000 | tf_op jit(solution)/shard_map/xmf,xfd->xmd/dot_general | solution.py:414
  37.3 0.1 unsort_rows.2
  37.3 1.6 %collective-permute-start.8 = (bf16[64,1664]{1,0:T(8,128)(2,1)S(1)}, bf16[64,1664]{1,0:T(8,128)(2,1)S(1)}, u32[]{:S(2)}, u32[]{:S(2)}) collective-permute-start(bf16[64,1664]{1,0:T(8,128)(2,1)S(1)} %get-tuple-element.55.after_ref), channel_id=1, source_target_pairs={{0,1},{2,4},{4,2},{6,7},{7,6},{5,3},{3,5},{1,0},{8,9},{10,12},{12,... | collective-permute-start | bytes 638984 | tf_op jit(solution)/shard_map/ppermute | solution.py:371
  39.0 2.4 %fusion.refs_1_ = bf16[2,128,1024]{2,1,0:T(8,128)(2,1)S(1)} fusion(bf16[2,128,1664]{2,1,0:T(8,128)(2,1)S(1)} %sort_rows.3.refs_2_, bf16[2,1024,1664]{2,1,0:T(8,128)(2,1)S(1)} %get-tuple-element.52, f32[2,128,1024]{2,1,0:T(8,128)S(1)} %get-tuple-element.82), kind=kOutput, calls=%fused_computation.4 | convolution fusion | flops 875036672 | bytes 9240576 | tf_op jit(solution)/shard_map/xmd,xfd->xmf/dot_general | solution.py:417
  41.3 2.3 %convolution_convert_fusion.in_ref = bf16[2,128,1664]{2,1,0:T(8,128)(2,1)S(1)} fusion(bf16[2,128,1024]{2,1,0:T(8,128)(2,1)S(1)} %fusion.refs_1_, bf16[2,1664,1024]{2,1,0:T(8,128)(2,1)S(1)} %get-tuple-element.51), kind=kOutput, calls=%fused_computation | convolution fusion | flops 872841216 | bytes 8192000 | tf_op jit(solution)/shard_map/xmf,xdf->xmd/dot_general | solution.py:421
  43.8 1.1 %collective-permute-start.13 = (bf16[64,1664]{1,0:T(8,128)(2,1)S(1)}, bf16[64,1664]{1,0:T(8,128)(2,1)S(1)}, u32[]{:S(2)}, u32[]{:S(2)}) collective-permute-start(bf16[64,1664]{1,0:T(8,128)(2,1)S(1)} %get-tuple-element.56.refs_0_), channel_id=1, source_target_pairs={{0,1},{2,4},{4,2},{6,7},{7,6},{5,3},{3,5},{1,0},{8,9},{10,12},{12,... | collective-permute-start | bytes 638984 | tf_op jit(solution)/shard_map/ppermute | solution.py:371
  45.0 1.6 %collective-permute-start.9 = (bf16[64,1664]{1,0:T(8,128)(2,1)S(1)}, bf16[64,1664]{1,0:T(8,128)(2,1)S(1)}, u32[]{:S(2)}, u32[]{:S(2)}) collective-permute-start(bf16[64,1664]{1,0:T(8,128)(2,1)S(1)} %add.21.after_ref), channel_id=1, source_target_pairs={{0,2},{2,0},{1,3},{3,1},{4,6},{6,4},{5,7},{7,5},{8,10},{10,8},{9,1... | collective-permute-start | bytes 638984 | tf_op jit(solution)/shard_map/ppermute | solution.py:372
  46.5 3.2 %w_out_grad_kernel.3 = (f32[2,1024,1664]{2,1,0:T(8,128)}, f32[8,128]{1,0:T(8,128)S(1)}) custom-call(bf16[64,1664]{1,0:T(8,128)(2,1)S(1)} %get-tuple-element.56.refs_0_, bf16[2,128,1024]{2,1,0:T(8,128)(2,1)S(1)} %get-tuple-element.81.refs_1_, bf16[2,128,1664]{2,1,0:T(8,128)(2,1)S(1)} %sort_rows.3.refs_2_), custom_call_target="tpu_custom_call" | custom-call | flops 436207616 | bytes 6815744 | tf_op jit(solution)/shard_map/w_out_grad_kernel/pallas_call | solution.py:264
  49.8 1.6 %collective-permute-start.14 = (bf16[64,1664]{1,0:T(8,128)(2,1)S(1)}, bf16[64,1664]{1,0:T(8,128)(2,1)S(1)}, u32[]{:S(2)}, u32[]{:S(2)}) collective-permute-start(bf16[64,1664]{1,0:T(8,128)(2,1)S(1)} %add.23), channel_id=1, source_target_pairs={{0,2},{2,0},{1,3},{3,1},{4,6},{6,4},{5,7},{7,5},{8,10},{10,8},{9,1... | collective-permute-start | bytes 638984 | tf_op jit(solution)/shard_map/ppermute | solution.py:372
  51.4 0.4 collective-permute-done.9.refs_1_
  51.9 2.2 %collective-permute-start.16 = (bf16[64,1664]{1,0:T(8,128)(2,1)S(1)}, bf16[64,1664]{1,0:T(8,128)(2,1)S(1)}, u32[]{:S(2)}, u32[]{:S(2)}) collective-permute-start(bf16[64,1664]{1,0:T(8,128)(2,1)S(1)} %add.22.refs_0_), channel_id=1, source_target_pairs={{0,1},{2,4},{4,2},{6,7},{7,6},{5,3},{3,5},{1,0},{8,9},{10,12},{12,... | collective-permute-start | bytes 638984 | tf_op jit(solution)/shard_map/ppermute | solution.py:371
  54.1 2.1 %w_out_grad_kernel.4 = (f32[2,1024,1664]{2,1,0:T(8,128)}, f32[8,128]{1,0:T(8,128)S(1)}) custom-call(bf16[64,1664]{1,0:T(8,128)(2,1)S(1)} %add.22.refs_0_, bf16[2,128,1024]{2,1,0:T(8,128)(2,1)S(1)} %get-tuple-element.81.refs_1_, bf16[2,128,1664]{2,1,0:T(8,128)(2,1)S(1)} %sort_rows.3.refs_2_, ...), custom_call_target="tpu_custom_call", output_to_operand_aliasing={{0}: (3, {})} | custom-call | flops 218103808 | bytes 3407872 | tf_op jit(solution)/shard_map/w_out_grad_kernel/pallas_call | solution.py:264
  56.2 0.7 collective-permute-start.15
  56.9 3.2 %w_in_grad_kernel.2 = (f32[2,1664,1024]{2,1,0:T(8,128)}, f32[8,128]{1,0:T(8,128)S(1)}) custom-call(bf16[64,1664]{1,0:T(8,128)(2,1)S(1)} %add.24.refs_0_, bf16[2,128,1024]{2,1,0:T(8,128)(2,1)S(1)} %fusion.refs_1_, bf16[2,128,1664]{2,1,0:T(8,128)(2,1)S(1)} %sort_rows.2.refs_2_), custom_call_target="tpu_custom_call" | custom-call | flops 436207616 | bytes 6815744 | tf_op jit(solution)/shard_map/w_in_grad_kernel/pallas_call | solution.py:264
  60.1 0.1 collective-permute-done.16.refs_2_
  60.2 1.8 %collective-permute-start.17 = (bf16[32,1664]{1,0:T(8,128)(2,1)S(1)}, bf16[32,1664]{1,0:T(8,128)(2,1)S(1)}, u32[]{:S(2)}, u32[]{:S(2)}) collective-permute-start(bf16[32,1664]{1,0:T(8,128)(2,1)S(1)} %get-tuple-element.69), channel_id=1, source_target_pairs={{0,2},{2,0},{1,3},{3,1},{4,6},{6,4},{5,7},{7,5},{8,10},{10,8},{9,1... | collective-permute-start | bytes 319496 | tf_op jit(solution)/shard_map/ppermute | solution.py:372
  62.0 0.5 collective-permute-done.15.refs_2_
  62.5 1.6 %collective-permute-start.18 = (bf16[32,1664]{1,0:T(8,128)(2,1)S(1)}, bf16[32,1664]{1,0:T(8,128)(2,1)S(1)}, u32[]{:S(2)}, u32[]{:S(2)}) collective-permute-start(bf16[32,1664]{1,0:T(8,128)(2,1)S(1)} %get-tuple-element.64.refs_0_), channel_id=1, source_target_pairs={{0,2},{2,0},{1,3},{3,1},{4,6},{6,4},{5,7},{7,5},{8,10},{10,8},{9,1... | collective-permute-start | bytes 319496 | tf_op jit(solution)/shard_map/ppermute | solution.py:372
  64.2 2.1 %w_out_grad_kernel.5 = (f32[2,1024,1664]{2,1,0:T(8,128)}, f32[8,128]{1,0:T(8,128)S(1)}) custom-call(bf16[32,1664]{1,0:T(8,128)(2,1)S(1)} %get-tuple-element.64.refs_0_, bf16[2,128,1024]{2,1,0:T(8,128)(2,1)S(1)} %get-tuple-element.81.refs_1_, bf16[2,128,1664]{2,1,0:T(8,128)(2,1)S(1)} %sort_rows.3.refs_2_, ...), custom_call_target="tpu_custom_call", output_to_operand_aliasing={{0}: (3, {})} | custom-call | flops 218103808 | bytes 3407872 | tf_op jit(solution)/shard_map/w_out_grad_kernel/pallas_call | solution.py:264
  66.3 1.0 %collective-permute-done.18.refs_4_ = bf16[32,1664]{1,0:T(8,128)(2,1)S(1)} collective-permute-done((bf16[32,1664]{1,0:T(8,128)(2,1)S(1)}, bf16[32,1664]{1,0:T(8,128)(2,1)S(1)}, u32[]{:S(2)}, u32[]{:S(2)}) %collective-permute-start.18) | collective-permute-done | bytes 106528 | tf_op jit(solution)/shard_map/ppermute | solution.py:372
  67.3 0.2 join.1
  67.5 0.1 collective-permute-start.19
  67.6 1.4 %collective-permute-start.20 = (bf16[16,1664]{1,0:T(8,128)(2,1)S(1)}, bf16[16,1664]{1,0:T(8,128)(2,1)S(1)}, u32[]{:S(2)}, u32[]{:S(2)}) collective-permute-start(bf16[16,1664]{1,0:T(8,128)(2,1)S(1)} %get-tuple-element.73), channel_id=1, source_target_pairs={{0,16},{8,24},{16,0},{24,8},{1,17},{9,25},{17,1},{25,9},{2,18},{10... | collective-permute-start | bytes 159752 | tf_op jit(solution)/shard_map/ppermute | solution.py:378
  69.0 0.5 collective-permute-start.21
  69.5 3.8 %w_in_grad_kernel.3 = (f32[2,1664,1024]{2,1,0:T(8,128)}, f32[8,128]{1,0:T(8,128)}) custom-call(bf16[16,1664]{1,0:T(8,128)(2,1)S(1)} %get-tuple-element.71.refs_0_, bf16[2,128,1024]{2,1,0:T(8,128)(2,1)S(1)} %fusion.refs_1_, bf16[2,128,1664]{2,1,0:T(8,128)(2,1)S(1)} %sort_rows.2.refs_2_, ...), custom_call_target="tpu_custom_call", output_to_operand_aliasing={{0}: (3, {})} | custom-call | flops 436207616 | bytes 6815744 | tf_op jit(solution)/shard_map/w_in_grad_kernel/pallas_call | solution.py:264
  73.4 1.5 %finish.1 = (bf16[128,1664]{1,0:T(8,128)(2,1)}, bf16[128,1664]{1,0:T(8,128)(2,1)}, f32[2,128]{1,0:T(2,128)}) custom-call(s32[2,128]{1,0:T(2,128)S(1)} %bitcast.14, s32[2,128]{1,0:T(2,128)S(1)} %bitcast.16, s32[2,128]{1,0:T(2,128)S(1)} %bitcast.18, f32[2,128]{1,0:T(2,128)S(1)} %bitcast.20, bf16[128,1664]{1,0:T(8,128)(2,1)S(1)} %copy-done, ...), custom_call_target="tpu_custom_call" | custom-call | tf_op jit(solution)/shard_map/finish/pallas_call | solution.py:215
  (34 shorter events, 0.7 us)
Async XLA Ops:
  2.8 6.1 %collective-permute-start = (bf16[16,1664]{1,0:T(8,128)(2,1)}, bf16[16,1664]{1,0:T(8,128)(2,1)S(1)}, u32[]{:S(2)}, u32[]{:S(2)}) collective-permute-start(bf16[16,1664]{1,0:T(8,128)(2,1)} %get-tuple-element.45), channel_id=1, source_target_pairs={{0,8},{8,0},{16,24},{24,16},{1,9},{9,1},{17,25},{25,17},{2,10},{10... | collective-permute-start | bytes 159752 | tf_op jit(solution)/shard_map/ppermute | solution.py:378
  3.2 5.7 %collective-permute-start.1 = (bf16[16,1664]{1,0:T(8,128)(2,1)}, bf16[16,1664]{1,0:T(8,128)(2,1)S(1)}, u32[]{:S(2)}, u32[]{:S(2)}) collective-permute-start(bf16[16,1664]{1,0:T(8,128)(2,1)} %get-tuple-element.46), channel_id=1, source_target_pairs={{0,16},{8,24},{16,0},{24,8},{1,17},{9,25},{17,1},{25,9},{2,18},{10... | collective-permute-start | bytes 159752 | tf_op jit(solution)/shard_map/ppermute | solution.py:378
  5.7 4.0 %collective-permute-start.2 = (bf16[16,1664]{1,0:T(8,128)(2,1)}, bf16[16,1664]{1,0:T(8,128)(2,1)S(1)}, u32[]{:S(2)}, u32[]{:S(2)}) collective-permute-start(bf16[16,1664]{1,0:T(8,128)(2,1)} %get-tuple-element.47), channel_id=1, source_target_pairs={{0,24},{8,16},{16,8},{24,0},{1,25},{9,17},{17,9},{25,1},{2,26},{10... | collective-permute-start | bytes 159752 | tf_op jit(solution)/shard_map/ppermute | solution.py:378
  9.9 5.1 %collective-permute-start.3 = (bf16[32,1664]{1,0:T(8,128)(2,1)S(1)}, bf16[32,1664]{1,0:T(8,128)(2,1)S(1)}, u32[]{:S(2)}, u32[]{:S(2)}) collective-permute-start(bf16[32,1664]{1,0:T(8,128)(2,1)S(1)} %get-tuple-element.48.refs_0_), channel_id=1, source_target_pairs={{0,1},{2,4},{4,2},{6,7},{7,6},{5,3},{3,5},{1,0},{8,9},{10,12},{12,... | collective-permute-start | bytes 319496 | tf_op jit(solution)/shard_map/ppermute | solution.py:371
  11.5 4.7 %collective-permute-start.4 = (bf16[32,1664]{1,0:T(8,128)(2,1)S(1)}, bf16[32,1664]{1,0:T(8,128)(2,1)S(1)}, u32[]{:S(2)}, u32[]{:S(2)}) collective-permute-start(bf16[32,1664]{1,0:T(8,128)(2,1)S(1)} %get-tuple-element.49.refs_1_), channel_id=1, source_target_pairs={{0,2},{2,0},{1,3},{3,1},{4,6},{6,4},{5,7},{7,5},{8,10},{10,8},{9,1... | collective-permute-start | bytes 319496 | tf_op jit(solution)/shard_map/ppermute | solution.py:372
  16.3 6.2 %collective-permute-start.5 = (bf16[64,1664]{1,0:T(8,128)(2,1)S(1)}, bf16[64,1664]{1,0:T(8,128)(2,1)S(1)}, u32[]{:S(2)}, u32[]{:S(2)}) collective-permute-start(bf16[64,1664]{1,0:T(8,128)(2,1)S(1)} %pair.2.refs_0_), channel_id=1, source_target_pairs={{0,1},{2,4},{4,2},{6,7},{7,6},{5,3},{3,5},{1,0},{8,9},{10,12},{12,... | collective-permute-start | bytes 638984 | tf_op jit(solution)/shard_map/ppermute | solution.py:371
  17.8 6.4 %collective-permute-start.10 = (bf16[64,1664]{1,0:T(8,128)(2,1)S(1)}, bf16[64,1664]{1,0:T(8,128)(2,1)S(1)}, u32[]{:S(2)}, u32[]{:S(2)}) collective-permute-start(bf16[64,1664]{1,0:T(8,128)(2,1)S(1)} %pair.3.refs_1_.refs_0_), channel_id=1, source_target_pairs={{0,2},{2,0},{1,3},{3,1},{4,6},{6,4},{5,7},{7,5},{8,10},{10,8},{9,1... | collective-permute-start | bytes 638984 | tf_op jit(solution)/shard_map/ppermute | solution.py:372
  22.5 6.1 %collective-permute-start.6 = (bf16[64,1664]{1,0:T(8,128)(2,1)S(1)}, bf16[64,1664]{1,0:T(8,128)(2,1)S(1)}, u32[]{:S(2)}, u32[]{:S(2)}) collective-permute-start(bf16[64,1664]{1,0:T(8,128)(2,1)S(1)} %pass.1.refs_1_), channel_id=1, source_target_pairs={{0,2},{2,0},{1,3},{3,1},{4,6},{6,4},{5,7},{7,5},{8,10},{10,8},{9,1... | collective-permute-start | bytes 638984 | tf_op jit(solution)/shard_map/ppermute | solution.py:372
  24.2 6.7 %collective-permute-start.11 = (bf16[64,1664]{1,0:T(8,128)(2,1)S(1)}, bf16[64,1664]{1,0:T(8,128)(2,1)S(1)}, u32[]{:S(2)}, u32[]{:S(2)}) collective-permute-start(bf16[64,1664]{1,0:T(8,128)(2,1)S(1)} %collective-permute-done.10.refs_1_), channel_id=1, source_target_pairs={{0,1},{2,4},{4,2},{6,7},{7,6},{5,3},{3,5},{1,0},{8,9},{10,12},{12,... | collective-permute-start | bytes 638984 | tf_op jit(solution)/shard_map/ppermute | solution.py:371
  28.6 6.0 %collective-permute-start.7 = (bf16[64,1664]{1,0:T(8,128)(2,1)S(1)}, bf16[64,1664]{1,0:T(8,128)(2,1)S(1)}, u32[]{:S(2)}, u32[]{:S(2)}) collective-permute-start(bf16[64,1664]{1,0:T(8,128)(2,1)S(1)} %collective-permute-done.6.refs_2_), channel_id=1, source_target_pairs={{0,1},{2,4},{4,2},{6,7},{7,6},{5,3},{3,5},{1,0},{8,9},{10,12},{12,... | collective-permute-start | bytes 638984 | tf_op jit(solution)/shard_map/ppermute | solution.py:371
  30.9 8.0 %collective-permute-start.12 = (bf16[64,1664]{1,0:T(8,128)(2,1)S(1)}, bf16[64,1664]{1,0:T(8,128)(2,1)S(1)}, u32[]{:S(2)}, u32[]{:S(2)}) collective-permute-start(bf16[64,1664]{1,0:T(8,128)(2,1)S(1)} %collective-permute-done.11.refs_2_), channel_id=1, source_target_pairs={{0,2},{2,0},{1,3},{3,1},{4,6},{6,4},{5,7},{7,5},{8,10},{10,8},{9,1... | collective-permute-start | bytes 638984 | tf_op jit(solution)/shard_map/ppermute | solution.py:372
  37.3 6.4 %collective-permute-start.8 = (bf16[64,1664]{1,0:T(8,128)(2,1)S(1)}, bf16[64,1664]{1,0:T(8,128)(2,1)S(1)}, u32[]{:S(2)}, u32[]{:S(2)}) collective-permute-start(bf16[64,1664]{1,0:T(8,128)(2,1)S(1)} %get-tuple-element.55.after_ref), channel_id=1, source_target_pairs={{0,1},{2,4},{4,2},{6,7},{7,6},{5,3},{3,5},{1,0},{8,9},{10,12},{12,... | collective-permute-start | bytes 638984 | tf_op jit(solution)/shard_map/ppermute | solution.py:371
  43.8 5.9 %collective-permute-start.13 = (bf16[64,1664]{1,0:T(8,128)(2,1)S(1)}, bf16[64,1664]{1,0:T(8,128)(2,1)S(1)}, u32[]{:S(2)}, u32[]{:S(2)}) collective-permute-start(bf16[64,1664]{1,0:T(8,128)(2,1)S(1)} %get-tuple-element.56.refs_0_), channel_id=1, source_target_pairs={{0,1},{2,4},{4,2},{6,7},{7,6},{5,3},{3,5},{1,0},{8,9},{10,12},{12,... | collective-permute-start | bytes 638984 | tf_op jit(solution)/shard_map/ppermute | solution.py:371
  45.0 6.9 %collective-permute-start.9 = (bf16[64,1664]{1,0:T(8,128)(2,1)S(1)}, bf16[64,1664]{1,0:T(8,128)(2,1)S(1)}, u32[]{:S(2)}, u32[]{:S(2)}) collective-permute-start(bf16[64,1664]{1,0:T(8,128)(2,1)S(1)} %add.21.after_ref), channel_id=1, source_target_pairs={{0,2},{2,0},{1,3},{3,1},{4,6},{6,4},{5,7},{7,5},{8,10},{10,8},{9,1... | collective-permute-start | bytes 638984 | tf_op jit(solution)/shard_map/ppermute | solution.py:372
  49.8 6.4 %collective-permute-start.14 = (bf16[64,1664]{1,0:T(8,128)(2,1)S(1)}, bf16[64,1664]{1,0:T(8,128)(2,1)S(1)}, u32[]{:S(2)}, u32[]{:S(2)}) collective-permute-start(bf16[64,1664]{1,0:T(8,128)(2,1)S(1)} %add.23), channel_id=1, source_target_pairs={{0,2},{2,0},{1,3},{3,1},{4,6},{6,4},{5,7},{7,5},{8,10},{10,8},{9,1... | collective-permute-start | bytes 638984 | tf_op jit(solution)/shard_map/ppermute | solution.py:372
  51.9 8.3 %collective-permute-start.16 = (bf16[64,1664]{1,0:T(8,128)(2,1)S(1)}, bf16[64,1664]{1,0:T(8,128)(2,1)S(1)}, u32[]{:S(2)}, u32[]{:S(2)}) collective-permute-start(bf16[64,1664]{1,0:T(8,128)(2,1)S(1)} %add.22.refs_0_), channel_id=1, source_target_pairs={{0,1},{2,4},{4,2},{6,7},{7,6},{5,3},{3,5},{1,0},{8,9},{10,12},{12,... | collective-permute-start | bytes 638984 | tf_op jit(solution)/shard_map/ppermute | solution.py:371
  56.2 6.2 %collective-permute-start.15 = (bf16[64,1664]{1,0:T(8,128)(2,1)S(1)}, bf16[64,1664]{1,0:T(8,128)(2,1)S(1)}, u32[]{:S(2)}, u32[]{:S(2)}) collective-permute-start(bf16[64,1664]{1,0:T(8,128)(2,1)S(1)} %add.24.refs_0_), channel_id=1, source_target_pairs={{0,1},{2,4},{4,2},{6,7},{7,6},{5,3},{3,5},{1,0},{8,9},{10,12},{12,... | collective-permute-start | bytes 638984 | tf_op jit(solution)/shard_map/ppermute | solution.py:371
  60.2 6.0 %collective-permute-start.17 = (bf16[32,1664]{1,0:T(8,128)(2,1)S(1)}, bf16[32,1664]{1,0:T(8,128)(2,1)S(1)}, u32[]{:S(2)}, u32[]{:S(2)}) collective-permute-start(bf16[32,1664]{1,0:T(8,128)(2,1)S(1)} %get-tuple-element.69), channel_id=1, source_target_pairs={{0,2},{2,0},{1,3},{3,1},{4,6},{6,4},{5,7},{7,5},{8,10},{10,8},{9,1... | collective-permute-start | bytes 319496 | tf_op jit(solution)/shard_map/ppermute | solution.py:372
  62.5 4.8 %collective-permute-start.18 = (bf16[32,1664]{1,0:T(8,128)(2,1)S(1)}, bf16[32,1664]{1,0:T(8,128)(2,1)S(1)}, u32[]{:S(2)}, u32[]{:S(2)}) collective-permute-start(bf16[32,1664]{1,0:T(8,128)(2,1)S(1)} %get-tuple-element.64.refs_0_), channel_id=1, source_target_pairs={{0,2},{2,0},{1,3},{3,1},{4,6},{6,4},{5,7},{7,5},{8,10},{10,8},{9,1... | collective-permute-start | bytes 319496 | tf_op jit(solution)/shard_map/ppermute | solution.py:372
  67.5 5.7 %collective-permute-start.19 = (bf16[16,1664]{1,0:T(8,128)(2,1)S(1)}, bf16[16,1664]{1,0:T(8,128)(2,1)S(1)}, u32[]{:S(2)}, u32[]{:S(2)}) collective-permute-start(bf16[16,1664]{1,0:T(8,128)(2,1)S(1)} %get-tuple-element.72), channel_id=1, source_target_pairs={{0,8},{8,0},{16,24},{24,16},{1,9},{9,1},{17,25},{25,17},{2,10},{10... | collective-permute-start | bytes 159752 | tf_op jit(solution)/shard_map/ppermute | solution.py:378
  67.6 5.7 %collective-permute-start.20 = (bf16[16,1664]{1,0:T(8,128)(2,1)S(1)}, bf16[16,1664]{1,0:T(8,128)(2,1)S(1)}, u32[]{:S(2)}, u32[]{:S(2)}) collective-permute-start(bf16[16,1664]{1,0:T(8,128)(2,1)S(1)} %get-tuple-element.73), channel_id=1, source_target_pairs={{0,16},{8,24},{16,0},{24,8},{1,17},{9,25},{17,1},{25,9},{2,18},{10... | collective-permute-start | bytes 159752 | tf_op jit(solution)/shard_map/ppermute | solution.py:378
  69.0 4.3 %collective-permute-start.21 = (bf16[16,1664]{1,0:T(8,128)(2,1)S(1)}, bf16[16,1664]{1,0:T(8,128)(2,1)S(1)}, u32[]{:S(2)}, u32[]{:S(2)}) collective-permute-start(bf16[16,1664]{1,0:T(8,128)(2,1)S(1)} %get-tuple-element.74), channel_id=1, source_target_pairs={{0,24},{8,16},{16,8},{24,0},{1,25},{9,17},{17,9},{25,1},{2,26},{10... | collective-permute-start | bytes 159752 | tf_op jit(solution)/shard_map/ppermute | solution.py:378
  69.5 3.8 %copy-start = (bf16[128,1664]{1,0:T(8,128)(2,1)S(1)}, bf16[128,1664]{1,0:T(8,128)(2,1)}, u32[]{:S(2)}) copy-start(bf16[128,1664]{1,0:T(8,128)(2,1)} %out_grad_ref.3) | copy-start | bytes 1277956
  69.5 3.8 %copy-start.1 = (s32[128,2]{0,1:T(2,128)S(1)}, s32[128,2]{0,1:T(2,128)}, u32[]{:S(2)}) copy-start(s32[128,2]{0,1:T(2,128)} %param.9) | copy-start | bytes 3076
  69.5 3.9 %copy-start.2 = (s32[128,2]{0,1:T(2,128)S(1)}, s32[128,2]{0,1:T(2,128)}, u32[]{:S(2)}) copy-start(s32[128,2]{0,1:T(2,128)} %param.10) | copy-start | bytes 3076
  69.5 3.9 %copy-start.3 = (s32[128,2]{0,1:T(2,128)S(1)}, s32[128,2]{0,1:T(2,128)}, u32[]{:S(2)}) copy-start(s32[128,2]{0,1:T(2,128)} %param.11) | copy-start | bytes 3076
  69.5 3.9 %copy-start.4 = (f32[128,2]{0,1:T(2,128)S(1)}, f32[128,2]{0,1:T(2,128)}, u32[]{:S(2)}) copy-start(f32[128,2]{0,1:T(2,128)} %param.12) | copy-start | bytes 3076

commit v6 on v4

--- a/solution.py
+++ b/solution.py
@@ -83,27 +83,23 @@
 def finish_kernel(
     ids_ref, slot_ref, dropped_ref, gates_ref, out_grad_ref, *refs, exp_local
 ):
-    parts, outs, (made, sems) = refs[:-5], refs[-5:-2], refs[-2:]
-    mixed_ref, tok_grad_ref, gate_grad_ref = outs
+    parts, (mixed_ref, tok_grad_ref, gate_grad_ref) = refs[:-3], refs[-3:]
     returned, returned_grad = [rows.astype(jnp.bfloat16) for rows in stack_halves(parts)]
     masks = slot_masks(ids_ref, slot_ref, dropped_ref, exp_local, returned.shape[0])
     select = sum(mask.astype(jnp.float32) for mask in masks).astype(jnp.bfloat16)
-    made[0] = contract(select, returned_grad, 0, 0).astype(jnp.bfloat16)
-    copies = [pltpu.make_async_copy(made.at[0], tok_grad_ref, sems.at[0])]
-    copies[0].start()
+    tok_grad_ref[...] = contract(select, returned_grad, 0, 0).astype(jnp.bfloat16)
     tokens = gates_ref.shape[1]
     gates = jnp.concatenate([gates_ref[...], jnp.zeros((6, tokens), jnp.float32)], axis=0).T
     wide = out_grad_ref[...].astype(jnp.float32)
-    all_picked = [contract(mask.astype(jnp.bfloat16), returned, 0, 0) for mask in masks]
-    mixed = sum(gates[:, k : k + 1] * picked for k, picked in enumerate(all_picked))
-    made[1] = mixed.astype(jnp.bfloat16)
-    copies.append(pltpu.make_async_copy(made.at[1], mixed_ref, sems.at[1]))
-    copies[1].start()
-    grads = [jnp.sum(picked * wide, axis=1, keepdims=True) for picked in all_picked]
+    mixed = jnp.zeros(wide.shape, jnp.float32)
+    grads = []
+    for k, mask in enumerate(masks):
+        picked = contract(mask.astype(jnp.bfloat16), returned, 0, 0)
+        mixed = mixed + gates[:, k : k + 1] * picked
+        grads.append(jnp.sum(picked * wide, axis=1, keepdims=True))
+    mixed_ref[...] = mixed.astype(jnp.bfloat16)
     grads.append(jnp.zeros((tokens, 6), jnp.float32))
     gate_grad_ref[...] = jnp.concatenate(grads, axis=1).T[:2]
-    for copy in copies:
-        copy.wait()
 
 
 def split_kernel(after_ref, *refs, exp_local):
@@ -216,15 +212,12 @@
 
 
 def finish(choices, gates, out_grad, parts, exp_local):
-    by_token = jax.ShapeDtypeStruct(out_grad.shape, jnp.bfloat16)
-    anywhere = pl.BlockSpec(memory_space=pl.ANY)
     return pl.pallas_call(
         functools.partial(finish_kernel, exp_local=exp_local),
-        out_specs=[anywhere, anywhere, pl.BlockSpec(memory_space=pltpu.VMEM)],
-        out_shape=[by_token, by_token, jax.ShapeDtypeStruct(gates.shape, jnp.float32)],
-        scratch_shapes=[
-            pltpu.VMEM((2,) + out_grad.shape, jnp.bfloat16),
-            pltpu.SemaphoreType.DMA((2,)),
+        out_shape=[
+            jax.ShapeDtypeStruct(out_grad.shape, jnp.bfloat16),
+            jax.ShapeDtypeStruct(out_grad.shape, jnp.bfloat16),
+            jax.ShapeDtypeStruct(gates.shape, jnp.float32),
         ],
         compiler_params=params(out_grad.shape[0]),
         name="finish",
@@ -463,6 +456,7 @@
     grad_rows, pre_grad, row_grad = backward(
         grad_blocks, gelu_slope(pre), held_in, held_out, regroup(n_dp), out_blocks[-1]
     )
+    back_blocks = unsort_rows(row_grad, steps, done_out)
 
     def out_piece(expert, part, parts):
         return (w_out_grad_kernel, hidden, grad_rows, w_out.shape, expert, part, parts)
@@ -471,8 +465,8 @@
         return (w_in_grad_kernel, pre_grad, rows, w_in.shape, expert, part, parts)
 
     others, final = range(exp_local - 1), exp_local - 1
-    work = [out_piece(x, 0, 1) for x in others] + [out_piece(final, part, 2) for part in (0, 1)]
-    work += [in_piece(x, 0, 1) for x in range(exp_local)]
+    work = [out_piece(x, 0, 1) for x in others] + [out_piece(final, 0, 2)]
+    work += [in_piece(x, 0, 1) for x in others] + [out_piece(final, 1, 2), in_piece(final, 0, 1)]
     made = {}
 
     def next_piece(after):
@@ -500,7 +494,6 @@
         out_sum = add_step(ready, out_blocks[step - 1], out_arrived, step)
         out_arrived = swap(out_sum[-1], step % 2 == 0)
         if step == last:
-            back_blocks = unsort_rows(row_grad, steps, out_sum[0])
             back_sum = back_blocks[last:]
             back_arrived = swap(back_sum[-1], step % 2 == 1)
             ready = [next_piece(back_sum[-1])]

time: 76.1 us -> 74.8 us (0.983)
  waiting for transfers between devices: 12.4 us -> 11.3 us
  transfers between devices with their start and end apart: 22 -> 22, of which waited for: 13 -> 10; matrix products, arithmetic and copies ran while one was open for 4% -> 4% of each run, Pallas kernels for 33% -> 33%
where the time goes in v6:
time: 74.8 us; the launch traced here: 74.6 us
  starting transfers between devices  30.6 us (41%)
  Pallas kernels  29 us (39%)
  waiting for transfers between devices  11.3 us (15%)
  matrix products  2.75 us (4%)
  between operations  0.92 us (1%)
    pallas_call x5, Pallas kernels, weight_gradient(): pl.pallas_call(functools.partial(kernel, skip=len(after), expert=expert,...  14.3 us
    ppermute x8, starting transfers between devices, swap(): return lax.ppermute(block, 'near', [(0, 1), (1, 0)])  13.9 us
    ppermute x8, starting transfers between devices, swap(): return lax.ppermute(block, DP, odd_edges(lax.axis_size(DP)))  11.6 us
    pallas_call x2, Pallas kernels, hold(): pl.pallas_call(hold_kernel, in_specs=[pl.BlockSpec(memory_space=pl.ANY)]...  6.04 us
    ppermute x8, waiting for transfers between devices, swap(): return lax.ppermute(block, 'near', [(0, 1), (1, 0)])  5.5 us
    ppermute x6, starting transfers between devices, expert_swap(): lax.ppermute(blocks[k], 'expert', [(i, i ^ k) for i in range(size)])  5.02 us
    ppermute x8, waiting for transfers between devices, swap(): return lax.ppermute(block, DP, odd_edges(lax.axis_size(DP)))  4.97 us
    pallas_call x1, Pallas kernels, backward(): pl.pallas_call(functools.partial(backward_kernel, places=places), in_spec...  4.05 us
  transfers between devices with their start and end apart: 22, of which 10 were waited for; matrix products, arithmetic and copies ran while one was open for 4% of the time, Pallas kernels for 33%

profile of v6, /device:TPU:0, one launch (start us, length us, event | category | flops | bytes accessed | tf_op | source)
XLA Modules:
  0.0 74.6 jit_solution(10060336393571648512)
XLA Ops:
  0.6 2.1 %prepare.1 = (bf16[16,1664]{1,0:T(8,128)(2,1)S(1)}, bf16[16,1664]{1,0:T(8,128)(2,1)}, bf16[16,1664]{1,0:T(8,128)(2,1)}, bf16[16,1664]{1,0:T(8,128)(2,1)}) custom-call(s32[2,128]{1,0:T(2,128)} %bitcast.9, s32[2,128]{1,0:T(2,128)} %bitcast.11, s32[2,128]{1,0:T(2,128)} %bitcast.13, f32[2,128]{1,0:T(2,128)} %bitcast.15, bf16[128,1664]{1,0:T(8,128)(2,1)} %tokens_ref.1, ...), custom_call_target="tpu_custom_call" | custom-call | tf_op jit(solution)/shard_map/prepare/pallas_call | solution.py:204
  2.8 0.4 collective-permute-start
  3.2 2.5 %collective-permute-start.1 = (bf16[16,1664]{1,0:T(8,128)(2,1)}, bf16[16,1664]{1,0:T(8,128)(2,1)S(1)}, u32[]{:S(2)}, u32[]{:S(2)}) collective-permute-start(bf16[16,1664]{1,0:T(8,128)(2,1)} %get-tuple-element.49), channel_id=1, source_target_pairs={{0,16},{8,24},{16,0},{24,8},{1,17},{9,25},{17,1},{25,9},{2,18},{10... | collective-permute-start | bytes 159752 | tf_op jit(solution)/shard_map/ppermute | solution.py:418
  5.7 0.1 collective-permute-start.2
  5.8 3.0 %hold.2 = (bf16[2,1664,1024]{2,1,0:T(8,128)(2,1)S(1)}, f32[8,128]{1,0:T(8,128)S(1)}) custom-call(bf16[2,1664,1024]{2,1,0:T(8,128)(2,1)} %refs_0_.1), custom_call_target="tpu_custom_call" | custom-call | bytes 13631488 | tf_op jit(solution)/shard_map/hold/pallas_call | solution.py:242
  8.9 0.8 %collective-permute-done.2.refs_3_ = bf16[16,1664]{1,0:T(8,128)(2,1)S(1)} collective-permute-done((bf16[16,1664]{1,0:T(8,128)(2,1)}, bf16[16,1664]{1,0:T(8,128)(2,1)S(1)}, u32[]{:S(2)}, u32[]{:S(2)}) %collective-permute-start.2) | collective-permute-done | bytes 53280 | tf_op jit(solution)/shard_map/ppermute | solution.py:418
  9.7 0.2 split.1
  9.9 1.6 %collective-permute-start.3 = (bf16[32,1664]{1,0:T(8,128)(2,1)S(1)}, bf16[32,1664]{1,0:T(8,128)(2,1)S(1)}, u32[]{:S(2)}, u32[]{:S(2)}) collective-permute-start(bf16[32,1664]{1,0:T(8,128)(2,1)S(1)} %get-tuple-element.51.refs_0_), channel_id=1, source_target_pairs={{0,1},{2,4},{4,2},{6,7},{7,6},{5,3},{3,5},{1,0},{8,9},{10,12},{12,... | collective-permute-start | bytes 319496 | tf_op jit(solution)/shard_map/ppermute | solution.py:411
  11.5 1.6 %collective-permute-start.4 = (bf16[32,1664]{1,0:T(8,128)(2,1)S(1)}, bf16[32,1664]{1,0:T(8,128)(2,1)S(1)}, u32[]{:S(2)}, u32[]{:S(2)}) collective-permute-start(bf16[32,1664]{1,0:T(8,128)(2,1)S(1)} %get-tuple-element.52.refs_1_), channel_id=1, source_target_pairs={{0,2},{2,0},{1,3},{3,1},{4,6},{6,4},{5,7},{7,5},{8,10},{10,8},{9,1... | collective-permute-start | bytes 319496 | tf_op jit(solution)/shard_map/ppermute | solution.py:412
  13.1 1.9 %collective-permute-done.3.refs_0_.refs_1_ = bf16[32,1664]{1,0:T(8,128)(2,1)S(1)} collective-permute-done((bf16[32,1664]{1,0:T(8,128)(2,1)S(1)}, bf16[32,1664]{1,0:T(8,128)(2,1)S(1)}, u32[]{:S(2)}, u32[]{:S(2)}) %collective-permute-start.3) | collective-permute-done | bytes 106528 | tf_op jit(solution)/shard_map/ppermute | solution.py:411
  15.0 1.2 %collective-permute-done.4.refs_2_ = bf16[32,1664]{1,0:T(8,128)(2,1)S(1)} collective-permute-done((bf16[32,1664]{1,0:T(8,128)(2,1)S(1)}, bf16[32,1664]{1,0:T(8,128)(2,1)S(1)}, u32[]{:S(2)}, u32[]{:S(2)}) %collective-permute-start.4) | collective-permute-done | bytes 106528 | tf_op jit(solution)/shard_map/ppermute | solution.py:412
  16.3 1.5 %collective-permute-start.5 = (bf16[64,1664]{1,0:T(8,128)(2,1)S(1)}, bf16[64,1664]{1,0:T(8,128)(2,1)S(1)}, u32[]{:S(2)}, u32[]{:S(2)}) collective-permute-start(bf16[64,1664]{1,0:T(8,128)(2,1)S(1)} %pair.2.refs_0_), channel_id=1, source_target_pairs={{0,1},{2,4},{4,2},{6,7},{7,6},{5,3},{3,5},{1,0},{8,9},{10,12},{12,... | collective-permute-start | bytes 638984 | tf_op jit(solution)/shard_map/ppermute | solution.py:411
  17.8 1.6 %collective-permute-start.10 = (bf16[64,1664]{1,0:T(8,128)(2,1)S(1)}, bf16[64,1664]{1,0:T(8,128)(2,1)S(1)}, u32[]{:S(2)}, u32[]{:S(2)}) collective-permute-start(bf16[64,1664]{1,0:T(8,128)(2,1)S(1)} %pair.3.refs_1_.refs_0_), channel_id=1, source_target_pairs={{0,2},{2,0},{1,3},{3,1},{4,6},{6,4},{5,7},{7,5},{8,10},{10,8},{9,1... | collective-permute-start | bytes 638984 | tf_op jit(solution)/shard_map/ppermute | solution.py:412
  19.4 3.0 %hold.3 = (bf16[2,1024,1664]{2,1,0:T(8,128)(2,1)S(1)}, f32[8,128]{1,0:T(8,128)S(1)}) custom-call(bf16[64,1664]{1,0:T(8,128)(2,1)S(1)} %pair.2.refs_0_, bf16[64,1664]{1,0:T(8,128)(2,1)S(1)} %pair.3.refs_1_.refs_0_, bf16[2,1024,1664]{2,1,0:T(8,128)(2,1)} %refs_2_.1), custom_call_target="tpu_custom_call" | custom-call | bytes 13631488 | tf_op jit(solution)/shard_map/hold/pallas_call | solution.py:242
  22.5 1.7 %collective-permute-start.6 = (bf16[64,1664]{1,0:T(8,128)(2,1)S(1)}, bf16[64,1664]{1,0:T(8,128)(2,1)S(1)}, u32[]{:S(2)}, u32[]{:S(2)}) collective-permute-start(bf16[64,1664]{1,0:T(8,128)(2,1)S(1)} %pass.1.refs_1_), channel_id=1, source_target_pairs={{0,2},{2,0},{1,3},{3,1},{4,6},{6,4},{5,7},{7,5},{8,10},{10,8},{9,1... | collective-permute-start | bytes 638984 | tf_op jit(solution)/shard_map/ppermute | solution.py:412
  24.2 1.5 %collective-permute-start.11 = (bf16[64,1664]{1,0:T(8,128)(2,1)S(1)}, bf16[64,1664]{1,0:T(8,128)(2,1)S(1)}, u32[]{:S(2)}, u32[]{:S(2)}) collective-permute-start(bf16[64,1664]{1,0:T(8,128)(2,1)S(1)} %collective-permute-done.10.refs_1_), channel_id=1, source_target_pairs={{0,1},{2,4},{4,2},{6,7},{7,6},{5,3},{3,5},{1,0},{8,9},{10,12},{12,... | collective-permute-start | bytes 638984 | tf_op jit(solution)/shard_map/ppermute | solution.py:411
  25.7 2.9 %collective-permute-done.6.refs_2_ = bf16[64,1664]{1,0:T(8,128)(2,1)S(1)} collective-permute-done((bf16[64,1664]{1,0:T(8,128)(2,1)S(1)}, bf16[64,1664]{1,0:T(8,128)(2,1)S(1)}, u32[]{:S(2)}, u32[]{:S(2)}) %collective-permute-start.6) | collective-permute-done | bytes 213024 | tf_op jit(solution)/shard_map/ppermute | solution.py:412
  28.6 1.6 %collective-permute-start.7 = (bf16[64,1664]{1,0:T(8,128)(2,1)S(1)}, bf16[64,1664]{1,0:T(8,128)(2,1)S(1)}, u32[]{:S(2)}, u32[]{:S(2)}) collective-permute-start(bf16[64,1664]{1,0:T(8,128)(2,1)S(1)} %collective-permute-done.6.refs_2_), channel_id=1, source_target_pairs={{0,1},{2,4},{4,2},{6,7},{7,6},{5,3},{3,5},{1,0},{8,9},{10,12},{12,... | collective-permute-start | bytes 638984 | tf_op jit(solution)/shard_map/ppermute | solution.py:411
  30.1 0.8 %collective-permute-done.11.refs_2_ = bf16[64,1664]{1,0:T(8,128)(2,1)S(1)} collective-permute-done((bf16[64,1664]{1,0:T(8,128)(2,1)S(1)}, bf16[64,1664]{1,0:T(8,128)(2,1)S(1)}, u32[]{:S(2)}, u32[]{:S(2)}) %collective-permute-start.11) | collective-permute-done | bytes 213024 | tf_op jit(solution)/shard_map/ppermute | solution.py:411
  30.9 2.6 %collective-permute-start.12 = (bf16[64,1664]{1,0:T(8,128)(2,1)S(1)}, bf16[64,1664]{1,0:T(8,128)(2,1)S(1)}, u32[]{:S(2)}, u32[]{:S(2)}) collective-permute-start(bf16[64,1664]{1,0:T(8,128)(2,1)S(1)} %collective-permute-done.11.refs_2_), channel_id=1, source_target_pairs={{0,2},{2,0},{1,3},{3,1},{4,6},{6,4},{5,7},{7,5},{8,10},{10,8},{9,1... | collective-permute-start | bytes 638984 | tf_op jit(solution)/shard_map/ppermute | solution.py:412
  33.6 1.0 %collective-permute-done.7.refs_3_ = bf16[64,1664]{1,0:T(8,128)(2,1)S(1)} collective-permute-done((bf16[64,1664]{1,0:T(8,128)(2,1)S(1)}, bf16[64,1664]{1,0:T(8,128)(2,1)S(1)}, u32[]{:S(2)}, u32[]{:S(2)}) %collective-permute-start.7) | collective-permute-done | bytes 213024 | tf_op jit(solution)/shard_map/ppermute | solution.py:411
  34.6 0.1 sort_rows.1.refs_2_
  34.7 1.6 %fusion.3 = (f32[2,128,1024]{2,1,0:T(8,128)S(1)}, bf16[2,128,1024]{2,1,0:T(8,128)(2,1)S(1)}) fusion(bf16[2,128,1664]{2,1,0:T(8,128)(2,1)S(1)} %sort_rows.1.refs_2_, bf16[2,1664,1024]{2,1,0:T(8,128)(2,1)S(1)} %get-tuple-element.54.refs_5_), kind=kOutput, calls=%fused_computation.5 | convolution fusion | flops 875298816 | bytes 9240576 | tf_op jit(solution)/shard_map/xmd,xdf->xmf/dot_general | solution.py:452
  36.3 1.2 %convolution_convert_fusion.in_ref = bf16[2,128,1664]{2,1,0:T(8,128)(2,1)S(1)} fusion(bf16[2,128,1024]{2,1,0:T(8,128)(2,1)S(1)} %get-tuple-element.88.refs_1_, bf16[2,1024,1664]{2,1,0:T(8,128)(2,1)S(1)} %get-tuple-element.55.refs_6_), kind=kOutput, calls=%fused_computation | convolution fusion | flops 872841216 | bytes 8192000 | tf_op jit(solution)/shard_map/xmf,xfd->xmd/dot_general | solution.py:454
  37.4 0.1 unsort_rows.2
  37.5 1.6 %collective-permute-start.8 = (bf16[64,1664]{1,0:T(8,128)(2,1)S(1)}, bf16[64,1664]{1,0:T(8,128)(2,1)S(1)}, u32[]{:S(2)}, u32[]{:S(2)}) collective-permute-start(bf16[64,1664]{1,0:T(8,128)(2,1)S(1)} %get-tuple-element.58.after_ref), channel_id=1, source_target_pairs={{0,1},{2,4},{4,2},{6,7},{7,6},{5,3},{3,5},{1,0},{8,9},{10,12},{12,... | collective-permute-start | bytes 638984 | tf_op jit(solution)/shard_map/ppermute | solution.py:411
  39.1 4.0 %backward.1 = (bf16[2,128,1664]{2,1,0:T(8,128)(2,1)S(1)}, bf16[2,128,1024]{2,1,0:T(8,128)(2,1)S(1)}, bf16[2,128,1664]{2,1,0:T(8,128)(2,1)S(1)}) custom-call(bf16[64,1664]{1,0:T(8,128)(2,1)S(1)} %get-tuple-element.58.after_ref, bf16[64,1664]{1,0:T(8,128)(2,1)S(1)} %pair.3.refs_1_.refs_0_, bf16[64,1664]{1,0:T(8,128)(2,1)S(1)} %collective-permute-done.10.refs_1_, ...), custom_call_target="tpu_custom_call" | custom-call | flops 1744830464 | bytes 1703936 | tf_op jit(solution)/shard_map/backward/pallas_call | solution.py:347
  43.2 0.1 unsort_rows.3
  43.2 0.6 collective-permute-start.13
  43.9 2.1 %collective-permute-start.9 = (bf16[64,1664]{1,0:T(8,128)(2,1)S(1)}, bf16[64,1664]{1,0:T(8,128)(2,1)S(1)}, u32[]{:S(2)}, u32[]{:S(2)}) collective-permute-start(bf16[64,1664]{1,0:T(8,128)(2,1)S(1)} %add.19), channel_id=1, source_target_pairs={{0,2},{2,0},{1,3},{3,1},{4,6},{6,4},{5,7},{7,5},{8,10},{10,8},{9,1... | collective-permute-start | bytes 638984 | tf_op jit(solution)/shard_map/ppermute | solution.py:412
  46.0 3.2 %w_out_grad_kernel.3 = (f32[2,1024,1664]{2,1,0:T(8,128)}, f32[8,128]{1,0:T(8,128)S(1)}) custom-call(bf16[64,1664]{1,0:T(8,128)(2,1)S(1)} %get-tuple-element.61.refs_0_, bf16[2,128,1024]{2,1,0:T(8,128)(2,1)S(1)} %get-tuple-element.88.refs_1_, bf16[2,128,1664]{2,1,0:T(8,128)(2,1)S(1)} %get-tuple-element.59.refs_2_), custom_call_target="tpu_custom_call" | custom-call | flops 436207616 | bytes 6815744 | tf_op jit(solution)/shard_map/w_out_grad_kernel/pallas_call | solution.py:264
  49.2 1.6 %collective-permute-start.14 = (bf16[64,1664]{1,0:T(8,128)(2,1)S(1)}, bf16[64,1664]{1,0:T(8,128)(2,1)S(1)}, u32[]{:S(2)}, u32[]{:S(2)}) collective-permute-start(bf16[64,1664]{1,0:T(8,128)(2,1)S(1)} %add.21), channel_id=1, source_target_pairs={{0,2},{2,0},{1,3},{3,1},{4,6},{6,4},{5,7},{7,5},{8,10},{10,8},{9,1... | collective-permute-start | bytes 638984 | tf_op jit(solution)/shard_map/ppermute | solution.py:412
  50.9 2.9 %collective-permute-start.16 = (bf16[64,1664]{1,0:T(8,128)(2,1)S(1)}, bf16[64,1664]{1,0:T(8,128)(2,1)S(1)}, u32[]{:S(2)}, u32[]{:S(2)}) collective-permute-start(bf16[64,1664]{1,0:T(8,128)(2,1)S(1)} %add.20.refs_0_), channel_id=1, source_target_pairs={{0,1},{2,4},{4,2},{6,7},{7,6},{5,3},{3,5},{1,0},{8,9},{10,12},{12,... | collective-permute-start | bytes 638984 | tf_op jit(solution)/shard_map/ppermute | solution.py:411
  53.8 2.1 %w_out_grad_kernel.4 = (f32[2,1024,1664]{2,1,0:T(8,128)}, f32[8,128]{1,0:T(8,128)S(1)}) custom-call(bf16[64,1664]{1,0:T(8,128)(2,1)S(1)} %add.20.refs_0_, bf16[2,128,1024]{2,1,0:T(8,128)(2,1)S(1)} %get-tuple-element.88.refs_1_, bf16[2,128,1664]{2,1,0:T(8,128)(2,1)S(1)} %get-tuple-element.59.refs_2_, ...), custom_call_target="tpu_custom_call", output_to_operand_aliasing={{0}: (3, {})} | custom-call | flops 218103808 | bytes 3407872 | tf_op jit(solution)/shard_map/w_out_grad_kernel/pallas_call | solution.py:264
  56.0 0.4 collective-permute-start.15
  56.4 3.2 %w_in_grad_kernel.2 = (f32[2,1664,1024]{2,1,0:T(8,128)}, f32[8,128]{1,0:T(8,128)S(1)}) custom-call(bf16[64,1664]{1,0:T(8,128)(2,1)S(1)} %add.22.refs_0_, bf16[2,128,1024]{2,1,0:T(8,128)(2,1)S(1)} %get-tuple-element.67.refs_1_, bf16[2,128,1664]{2,1,0:T(8,128)(2,1)S(1)} %sort_rows.1.refs_2_), custom_call_target="tpu_custom_call" | custom-call | flops 436207616 | bytes 6815744 | tf_op jit(solution)/shard_map/w_in_grad_kernel/pallas_call | solution.py:264
  59.6 0.3 collective-permute-done.16.refs_2_
  60.0 1.3 %collective-permute-start.17 = (bf16[32,1664]{1,0:T(8,128)(2,1)S(1)}, bf16[32,1664]{1,0:T(8,128)(2,1)S(1)}, u32[]{:S(2)}, u32[]{:S(2)}) collective-permute-start(bf16[32,1664]{1,0:T(8,128)(2,1)S(1)} %get-tuple-element.75), channel_id=1, source_target_pairs={{0,2},{2,0},{1,3},{3,1},{4,6},{6,4},{5,7},{7,5},{8,10},{10,8},{9,1... | collective-permute-start | bytes 319496 | tf_op jit(solution)/shard_map/ppermute | solution.py:412
  61.3 0.9 %collective-permute-done.15.refs_2_ = bf16[64,1664]{1,0:T(8,128)(2,1)S(1)} collective-permute-done((bf16[64,1664]{1,0:T(8,128)(2,1)S(1)}, bf16[64,1664]{1,0:T(8,128)(2,1)S(1)}, u32[]{:S(2)}, u32[]{:S(2)}) %collective-permute-start.15) | collective-permute-done | bytes 213024 | tf_op jit(solution)/shard_map/ppermute | solution.py:411
  62.3 1.3 %collective-permute-start.18 = (bf16[32,1664]{1,0:T(8,128)(2,1)S(1)}, bf16[32,1664]{1,0:T(8,128)(2,1)S(1)}, u32[]{:S(2)}, u32[]{:S(2)}) collective-permute-start(bf16[32,1664]{1,0:T(8,128)(2,1)S(1)} %get-tuple-element.70.refs_0_), channel_id=1, source_target_pairs={{0,2},{2,0},{1,3},{3,1},{4,6},{6,4},{5,7},{7,5},{8,10},{10,8},{9,1... | collective-permute-start | bytes 319496 | tf_op jit(solution)/shard_map/ppermute | solution.py:412
  63.6 2.1 %w_out_grad_kernel.5 = (f32[2,1024,1664]{2,1,0:T(8,128)}, f32[8,128]{1,0:T(8,128)S(1)}) custom-call(bf16[32,1664]{1,0:T(8,128)(2,1)S(1)} %get-tuple-element.70.refs_0_, bf16[2,128,1024]{2,1,0:T(8,128)(2,1)S(1)} %get-tuple-element.88.refs_1_, bf16[2,128,1664]{2,1,0:T(8,128)(2,1)S(1)} %get-tuple-element.59.refs_2_, ...), custom_call_target="tpu_custom_call", output_to_operand_aliasing={{0}: (3, {})} | custom-call | flops 218103808 | bytes 3407872 | tf_op jit(solution)/shard_map/w_out_grad_kernel/pallas_call | solution.py:264
  65.7 1.4 %collective-permute-done.18.refs_4_ = bf16[32,1664]{1,0:T(8,128)(2,1)S(1)} collective-permute-done((bf16[32,1664]{1,0:T(8,128)(2,1)S(1)}, bf16[32,1664]{1,0:T(8,128)(2,1)S(1)}, u32[]{:S(2)}, u32[]{:S(2)}) %collective-permute-start.18) | collective-permute-done | bytes 106528 | tf_op jit(solution)/shard_map/ppermute | solution.py:412
  67.1 0.2 join.1
  67.3 0.1 collective-permute-start.19
  67.4 1.4 %collective-permute-start.20 = (bf16[16,1664]{1,0:T(8,128)(2,1)S(1)}, bf16[16,1664]{1,0:T(8,128)(2,1)S(1)}, u32[]{:S(2)}, u32[]{:S(2)}) collective-permute-start(bf16[16,1664]{1,0:T(8,128)(2,1)S(1)} %get-tuple-element.79), channel_id=1, source_target_pairs={{0,16},{8,24},{16,0},{24,8},{1,17},{9,25},{17,1},{25,9},{2,18},{10... | collective-permute-start | bytes 159752 | tf_op jit(solution)/shard_map/ppermute | solution.py:418
  68.8 0.5 collective-permute-start.21
  69.3 3.8 %w_in_grad_kernel.3 = (f32[2,1664,1024]{2,1,0:T(8,128)}, f32[8,128]{1,0:T(8,128)}) custom-call(bf16[16,1664]{1,0:T(8,128)(2,1)S(1)} %get-tuple-element.77.refs_0_, bf16[2,128,1024]{2,1,0:T(8,128)(2,1)S(1)} %get-tuple-element.67.refs_1_, bf16[2,128,1664]{2,1,0:T(8,128)(2,1)S(1)} %sort_rows.1.refs_2_, ...), custom_call_target="tpu_custom_call", output_to_operand_aliasing={{0}: (3, {})} | custom-call | flops 436207616 | bytes 6815744 | tf_op jit(solution)/shard_map/w_in_grad_kernel/pallas_call | solution.py:264
  73.1 1.5 %finish.1 = (bf16[128,1664]{1,0:T(8,128)(2,1)}, bf16[128,1664]{1,0:T(8,128)(2,1)}, f32[2,128]{1,0:T(2,128)}) custom-call(s32[2,128]{1,0:T(2,128)S(1)} %bitcast.10, s32[2,128]{1,0:T(2,128)S(1)} %bitcast.12, s32[2,128]{1,0:T(2,128)S(1)} %bitcast.14, f32[2,128]{1,0:T(2,128)S(1)} %bitcast.16, bf16[128,1664]{1,0:T(8,128)(2,1)S(1)} %copy-done, ...), custom_call_target="tpu_custom_call" | custom-call | tf_op jit(solution)/shard_map/finish/pallas_call | solution.py:215
  (32 shorter events, 0.5 us)
Async XLA Ops:
  2.8 6.1 %collective-permute-start = (bf16[16,1664]{1,0:T(8,128)(2,1)}, bf16[16,1664]{1,0:T(8,128)(2,1)S(1)}, u32[]{:S(2)}, u32[]{:S(2)}) collective-permute-start(bf16[16,1664]{1,0:T(8,128)(2,1)} %get-tuple-element.48), channel_id=1, source_target_pairs={{0,8},{8,0},{16,24},{24,16},{1,9},{9,1},{17,25},{25,17},{2,10},{10... | collective-permute-start | bytes 159752 | tf_op jit(solution)/shard_map/ppermute | solution.py:418
  3.2 5.7 %collective-permute-start.1 = (bf16[16,1664]{1,0:T(8,128)(2,1)}, bf16[16,1664]{1,0:T(8,128)(2,1)S(1)}, u32[]{:S(2)}, u32[]{:S(2)}) collective-permute-start(bf16[16,1664]{1,0:T(8,128)(2,1)} %get-tuple-element.49), channel_id=1, source_target_pairs={{0,16},{8,24},{16,0},{24,8},{1,17},{9,25},{17,1},{25,9},{2,18},{10... | collective-permute-start | bytes 159752 | tf_op jit(solution)/shard_map/ppermute | solution.py:418
  5.7 4.0 %collective-permute-start.2 = (bf16[16,1664]{1,0:T(8,128)(2,1)}, bf16[16,1664]{1,0:T(8,128)(2,1)S(1)}, u32[]{:S(2)}, u32[]{:S(2)}) collective-permute-start(bf16[16,1664]{1,0:T(8,128)(2,1)} %get-tuple-element.50), channel_id=1, source_target_pairs={{0,24},{8,16},{16,8},{24,0},{1,25},{9,17},{17,9},{25,1},{2,26},{10... | collective-permute-start | bytes 159752 | tf_op jit(solution)/shard_map/ppermute | solution.py:418
  9.9 5.1 %collective-permute-start.3 = (bf16[32,1664]{1,0:T(8,128)(2,1)S(1)}, bf16[32,1664]{1,0:T(8,128)(2,1)S(1)}, u32[]{:S(2)}, u32[]{:S(2)}) collective-permute-start(bf16[32,1664]{1,0:T(8,128)(2,1)S(1)} %get-tuple-element.51.refs_0_), channel_id=1, source_target_pairs={{0,1},{2,4},{4,2},{6,7},{7,6},{5,3},{3,5},{1,0},{8,9},{10,12},{12,... | collective-permute-start | bytes 319496 | tf_op jit(solution)/shard_map/ppermute | solution.py:411
  11.5 4.7 %collective-permute-start.4 = (bf16[32,1664]{1,0:T(8,128)(2,1)S(1)}, bf16[32,1664]{1,0:T(8,128)(2,1)S(1)}, u32[]{:S(2)}, u32[]{:S(2)}) collective-permute-start(bf16[32,1664]{1,0:T(8,128)(2,1)S(1)} %get-tuple-element.52.refs_1_), channel_id=1, source_target_pairs={{0,2},{2,0},{1,3},{3,1},{4,6},{6,4},{5,7},{7,5},{8,10},{10,8},{9,1... | collective-permute-start | bytes 319496 | tf_op jit(solution)/shard_map/ppermute | solution.py:412
  16.3 6.2 %collective-permute-start.5 = (bf16[64,1664]{1,0:T(8,128)(2,1)S(1)}, bf16[64,1664]{1,0:T(8,128)(2,1)S(1)}, u32[]{:S(2)}, u32[]{:S(2)}) collective-permute-start(bf16[64,1664]{1,0:T(8,128)(2,1)S(1)} %pair.2.refs_0_), channel_id=1, source_target_pairs={{0,1},{2,4},{4,2},{6,7},{7,6},{5,3},{3,5},{1,0},{8,9},{10,12},{12,... | collective-permute-start | bytes 638984 | tf_op jit(solution)/shard_map/ppermute | solution.py:411
  17.8 6.4 %collective-permute-start.10 = (bf16[64,1664]{1,0:T(8,128)(2,1)S(1)}, bf16[64,1664]{1,0:T(8,128)(2,1)S(1)}, u32[]{:S(2)}, u32[]{:S(2)}) collective-permute-start(bf16[64,1664]{1,0:T(8,128)(2,1)S(1)} %pair.3.refs_1_.refs_0_), channel_id=1, source_target_pairs={{0,2},{2,0},{1,3},{3,1},{4,6},{6,4},{5,7},{7,5},{8,10},{10,8},{9,1... | collective-permute-start | bytes 638984 | tf_op jit(solution)/shard_map/ppermute | solution.py:412
  22.5 6.1 %collective-permute-start.6 = (bf16[64,1664]{1,0:T(8,128)(2,1)S(1)}, bf16[64,1664]{1,0:T(8,128)(2,1)S(1)}, u32[]{:S(2)}, u32[]{:S(2)}) collective-permute-start(bf16[64,1664]{1,0:T(8,128)(2,1)S(1)} %pass.1.refs_1_), channel_id=1, source_target_pairs={{0,2},{2,0},{1,3},{3,1},{4,6},{6,4},{5,7},{7,5},{8,10},{10,8},{9,1... | collective-permute-start | bytes 638984 | tf_op jit(solution)/shard_map/ppermute | solution.py:412
  24.2 6.7 %collective-permute-start.11 = (bf16[64,1664]{1,0:T(8,128)(2,1)S(1)}, bf16[64,1664]{1,0:T(8,128)(2,1)S(1)}, u32[]{:S(2)}, u32[]{:S(2)}) collective-permute-start(bf16[64,1664]{1,0:T(8,128)(2,1)S(1)} %collective-permute-done.10.refs_1_), channel_id=1, source_target_pairs={{0,1},{2,4},{4,2},{6,7},{7,6},{5,3},{3,5},{1,0},{8,9},{10,12},{12,... | collective-permute-start | bytes 638984 | tf_op jit(solution)/shard_map/ppermute | solution.py:411
  28.6 6.0 %collective-permute-start.7 = (bf16[64,1664]{1,0:T(8,128)(2,1)S(1)}, bf16[64,1664]{1,0:T(8,128)(2,1)S(1)}, u32[]{:S(2)}, u32[]{:S(2)}) collective-permute-start(bf16[64,1664]{1,0:T(8,128)(2,1)S(1)} %collective-permute-done.6.refs_2_), channel_id=1, source_target_pairs={{0,1},{2,4},{4,2},{6,7},{7,6},{5,3},{3,5},{1,0},{8,9},{10,12},{12,... | collective-permute-start | bytes 638984 | tf_op jit(solution)/shard_map/ppermute | solution.py:411
  30.9 8.2 %collective-permute-start.12 = (bf16[64,1664]{1,0:T(8,128)(2,1)S(1)}, bf16[64,1664]{1,0:T(8,128)(2,1)S(1)}, u32[]{:S(2)}, u32[]{:S(2)}) collective-permute-start(bf16[64,1664]{1,0:T(8,128)(2,1)S(1)} %collective-permute-done.11.refs_2_), channel_id=1, source_target_pairs={{0,2},{2,0},{1,3},{3,1},{4,6},{6,4},{5,7},{7,5},{8,10},{10,8},{9,1... | collective-permute-start | bytes 638984 | tf_op jit(solution)/shard_map/ppermute | solution.py:412
  37.5 6.3 %collective-permute-start.8 = (bf16[64,1664]{1,0:T(8,128)(2,1)S(1)}, bf16[64,1664]{1,0:T(8,128)(2,1)S(1)}, u32[]{:S(2)}, u32[]{:S(2)}) collective-permute-start(bf16[64,1664]{1,0:T(8,128)(2,1)S(1)} %get-tuple-element.58.after_ref), channel_id=1, source_target_pairs={{0,1},{2,4},{4,2},{6,7},{7,6},{5,3},{3,5},{1,0},{8,9},{10,12},{12,... | collective-permute-start | bytes 638984 | tf_op jit(solution)/shard_map/ppermute | solution.py:411
  43.2 5.9 %collective-permute-start.13 = (bf16[64,1664]{1,0:T(8,128)(2,1)S(1)}, bf16[64,1664]{1,0:T(8,128)(2,1)S(1)}, u32[]{:S(2)}, u32[]{:S(2)}) collective-permute-start(bf16[64,1664]{1,0:T(8,128)(2,1)S(1)} %get-tuple-element.61.refs_0_), channel_id=1, source_target_pairs={{0,1},{2,4},{4,2},{6,7},{7,6},{5,3},{3,5},{1,0},{8,9},{10,12},{12,... | collective-permute-start | bytes 638984 | tf_op jit(solution)/shard_map/ppermute | solution.py:411
  43.9 7.0 %collective-permute-start.9 = (bf16[64,1664]{1,0:T(8,128)(2,1)S(1)}, bf16[64,1664]{1,0:T(8,128)(2,1)S(1)}, u32[]{:S(2)}, u32[]{:S(2)}) collective-permute-start(bf16[64,1664]{1,0:T(8,128)(2,1)S(1)} %add.19), channel_id=1, source_target_pairs={{0,2},{2,0},{1,3},{3,1},{4,6},{6,4},{5,7},{7,5},{8,10},{10,8},{9,1... | collective-permute-start | bytes 638984 | tf_op jit(solution)/shard_map/ppermute | solution.py:412
  49.2 6.7 %collective-permute-start.14 = (bf16[64,1664]{1,0:T(8,128)(2,1)S(1)}, bf16[64,1664]{1,0:T(8,128)(2,1)S(1)}, u32[]{:S(2)}, u32[]{:S(2)}) collective-permute-start(bf16[64,1664]{1,0:T(8,128)(2,1)S(1)} %add.21), channel_id=1, source_target_pairs={{0,2},{2,0},{1,3},{3,1},{4,6},{6,4},{5,7},{7,5},{8,10},{10,8},{9,1... | collective-permute-start | bytes 638984 | tf_op jit(solution)/shard_map/ppermute | solution.py:412
  50.9 9.0 %collective-permute-start.16 = (bf16[64,1664]{1,0:T(8,128)(2,1)S(1)}, bf16[64,1664]{1,0:T(8,128)(2,1)S(1)}, u32[]{:S(2)}, u32[]{:S(2)}) collective-permute-start(bf16[64,1664]{1,0:T(8,128)(2,1)S(1)} %add.20.refs_0_), channel_id=1, source_target_pairs={{0,1},{2,4},{4,2},{6,7},{7,6},{5,3},{3,5},{1,0},{8,9},{10,12},{12,... | collective-permute-start | bytes 638984 | tf_op jit(solution)/shard_map/ppermute | solution.py:411
  56.0 6.2 %collective-permute-start.15 = (bf16[64,1664]{1,0:T(8,128)(2,1)S(1)}, bf16[64,1664]{1,0:T(8,128)(2,1)S(1)}, u32[]{:S(2)}, u32[]{:S(2)}) collective-permute-start(bf16[64,1664]{1,0:T(8,128)(2,1)S(1)} %add.22.refs_0_), channel_id=1, source_target_pairs={{0,1},{2,4},{4,2},{6,7},{7,6},{5,3},{3,5},{1,0},{8,9},{10,12},{12,... | collective-permute-start | bytes 638984 | tf_op jit(solution)/shard_map/ppermute | solution.py:411
  60.0 5.7 %collective-permute-start.17 = (bf16[32,1664]{1,0:T(8,128)(2,1)S(1)}, bf16[32,1664]{1,0:T(8,128)(2,1)S(1)}, u32[]{:S(2)}, u32[]{:S(2)}) collective-permute-start(bf16[32,1664]{1,0:T(8,128)(2,1)S(1)} %get-tuple-element.75), channel_id=1, source_target_pairs={{0,2},{2,0},{1,3},{3,1},{4,6},{6,4},{5,7},{7,5},{8,10},{10,8},{9,1... | collective-permute-start | bytes 319496 | tf_op jit(solution)/shard_map/ppermute | solution.py:412
  62.3 4.8 %collective-permute-start.18 = (bf16[32,1664]{1,0:T(8,128)(2,1)S(1)}, bf16[32,1664]{1,0:T(8,128)(2,1)S(1)}, u32[]{:S(2)}, u32[]{:S(2)}) collective-permute-start(bf16[32,1664]{1,0:T(8,128)(2,1)S(1)} %get-tuple-element.70.refs_0_), channel_id=1, source_target_pairs={{0,2},{2,0},{1,3},{3,1},{4,6},{6,4},{5,7},{7,5},{8,10},{10,8},{9,1... | collective-permute-start | bytes 319496 | tf_op jit(solution)/shard_map/ppermute | solution.py:412
  67.3 5.7 %collective-permute-start.19 = (bf16[16,1664]{1,0:T(8,128)(2,1)S(1)}, bf16[16,1664]{1,0:T(8,128)(2,1)S(1)}, u32[]{:S(2)}, u32[]{:S(2)}) collective-permute-start(bf16[16,1664]{1,0:T(8,128)(2,1)S(1)} %get-tuple-element.78), channel_id=1, source_target_pairs={{0,8},{8,0},{16,24},{24,16},{1,9},{9,1},{17,25},{25,17},{2,10},{10... | collective-permute-start | bytes 159752 | tf_op jit(solution)/shard_map/ppermute | solution.py:418
  67.4 5.7 %collective-permute-start.20 = (bf16[16,1664]{1,0:T(8,128)(2,1)S(1)}, bf16[16,1664]{1,0:T(8,128)(2,1)S(1)}, u32[]{:S(2)}, u32[]{:S(2)}) collective-permute-start(bf16[16,1664]{1,0:T(8,128)(2,1)S(1)} %get-tuple-element.79), channel_id=1, source_target_pairs={{0,16},{8,24},{16,0},{24,8},{1,17},{9,25},{17,1},{25,9},{2,18},{10... | collective-permute-start | bytes 159752 | tf_op jit(solution)/shard_map/ppermute | solution.py:418
  68.8 4.3 %collective-permute-start.21 = (bf16[16,1664]{1,0:T(8,128)(2,1)S(1)}, bf16[16,1664]{1,0:T(8,128)(2,1)S(1)}, u32[]{:S(2)}, u32[]{:S(2)}) collective-permute-start(bf16[16,1664]{1,0:T(8,128)(2,1)S(1)} %get-tuple-element.80), channel_id=1, source_target_pairs={{0,24},{8,16},{16,8},{24,0},{1,25},{9,17},{17,9},{25,1},{2,26},{10... | collective-permute-start | bytes 159752 | tf_op jit(solution)/shard_map/ppermute | solution.py:418
  69.3 3.8 %copy-start = (bf16[128,1664]{1,0:T(8,128)(2,1)S(1)}, bf16[128,1664]{1,0:T(8,128)(2,1)}, u32[]{:S(2)}) copy-start(bf16[128,1664]{1,0:T(8,128)(2,1)} %out_grad_ref.3) | copy-start | bytes 1277956
  69.3 3.8 %copy-start.1 = (s32[128,2]{0,1:T(2,128)S(1)}, s32[128,2]{0,1:T(2,128)}, u32[]{:S(2)}) copy-start(s32[128,2]{0,1:T(2,128)} %param.9) | copy-start | bytes 3076
  69.3 3.9 %copy-start.2 = (s32[128,2]{0,1:T(2,128)S(1)}, s32[128,2]{0,1:T(2,128)}, u32[]{:S(2)}) copy-start(s32[128,2]{0,1:T(2,128)} %param.10) | copy-start | bytes 3076
  69.3 3.9 %copy-start.3 = (s32[128,2]{0,1:T(2,128)S(1)}, s32[128,2]{0,1:T(2,128)}, u32[]{:S(2)}) copy-start(s32[128,2]{0,1:T(2,128)} %param.11) | copy-start | bytes 3076
  69.3 3.9 %copy-start.4 = (f32[128,2]{0,1:T(2,128)S(1)}, f32[128,2]{0,1:T(2,128)}, u32[]{:S(2)}) copy-start(f32[128,2]{0,1:T(2,128)} %param.12) | copy-start | bytes 3076

commit v7 on v6

--- a/solution.py
+++ b/solution.py
@@ -464,18 +464,18 @@
     def in_piece(expert, part, parts):
         return (w_in_grad_kernel, pre_grad, rows, w_in.shape, expert, part, parts)
 
-    others, final = range(exp_local - 1), exp_local - 1
-    work = [out_piece(x, 0, 1) for x in others] + [out_piece(final, 0, 2)]
-    work += [in_piece(x, 0, 1) for x in others] + [out_piece(final, 1, 2), in_piece(final, 0, 1)]
+    work = []
+    for expert in range(exp_local):
+        work += [out_piece(expert, 0, 1), in_piece(expert, 0, 1)]
     made = {}
 
-    def next_piece(after):
+    def next_piece(*after):
         if len(work) == 0:
-            return after
+            return after[0]
         kernel, left, right, shape, expert, part, parts = work.pop(0)
         name = kernel.__name__
         made[name], ready = weight_gradient(
-            kernel, left, right, shape, [after], name, expert, part, parts, made.get(name)
+            kernel, left, right, shape, after, name, expert, part, parts, made.get(name)
         )
         return ready
 
@@ -496,9 +496,7 @@
         if step == last:
             back_sum = back_blocks[last:]
             back_arrived = swap(back_sum[-1], step % 2 == 1)
-            ready = [next_piece(back_sum[-1])]
-        elif step > 1:
-            ready = [next_piece(out_sum[-1])]
+            ready = [next_piece(back_sum[-1], out_sum[-1])]
         back_sum = add_step(ready, back_blocks[step - 1], back_arrived, step)
     back_arrived = swap(back_sum[-1], False)
     joined = small_call(

time: 74.8 us -> 74.8 us (level)
  Pallas kernels: 29 us -> 28 us
  starting transfers between devices: 30.6 us -> 31.4 us
    pallas_call x5 -> x4, Pallas kernels: 14.3 us -> 13.4 us  [weight_gradient(): pl.pallas_call(functools.partial(kernel, skip=len(after), expert=expert,...]
    ppermute x8, starting transfers between devices: 11.6 us -> 12.4 us  [swap(): return lax.ppermute(block, DP, odd_edges(lax.axis_size(DP)))]
  transfers between devices with their start and end apart: 22 -> 22, of which waited for: 10 -> 12; matrix products, arithmetic and copies ran while one was open for 4% -> 4% of each run, Pallas kernels for 33% -> 32%
where the time goes in v7:
time: 74.8 us; the launch traced here: 74.6 us
  starting transfers between devices  31.4 us (42%)
  Pallas kernels  28 us (37%)
  waiting for transfers between devices  11.5 us (15%)
  matrix products  2.75 us (4%)
  between operations  0.9 us (1%)
    ppermute x8, starting transfers between devices, swap(): return lax.ppermute(block, 'near', [(0, 1), (1, 0)])  14 us
    pallas_call x4, Pallas kernels, weight_gradient(): pl.pallas_call(functools.partial(kernel, skip=len(after), expert=expert,...  13.4 us
    ppermute x8, starting transfers between devices, swap(): return lax.ppermute(block, DP, odd_edges(lax.axis_size(DP)))  12.4 us
    pallas_call x2, Pallas kernels, hold(): pl.pallas_call(hold_kernel, in_specs=[pl.BlockSpec(memory_space=pl.ANY)]...  6.04 us
    ppermute x8, waiting for transfers between devices, swap(): return lax.ppermute(block, 'near', [(0, 1), (1, 0)])  5.71 us
    ppermute x6, starting transfers between devices, expert_swap(): lax.ppermute(blocks[k], 'expert', [(i, i ^ k) for i in range(size)])  5.02 us
    ppermute x8, waiting for transfers between devices, swap(): return lax.ppermute(block, DP, odd_edges(lax.axis_size(DP)))  4.96 us
    pallas_call x1, Pallas kernels, backward(): pl.pallas_call(functools.partial(backward_kernel, places=places), in_spec...  4.05 us
  transfers between devices with their start and end apart: 22, of which 12 were waited for; matrix products, arithmetic and copies ran while one was open for 4% of the time, Pallas kernels for 32%

profile of v7, /device:TPU:0, one launch (start us, length us, event | category | flops | bytes accessed | tf_op | source)
XLA Modules:
  0.0 74.6 jit_solution(11614259768285324893)
XLA Ops:
  0.6 2.1 %prepare.1 = (bf16[16,1664]{1,0:T(8,128)(2,1)S(1)}, bf16[16,1664]{1,0:T(8,128)(2,1)}, bf16[16,1664]{1,0:T(8,128)(2,1)}, bf16[16,1664]{1,0:T(8,128)(2,1)}) custom-call(s32[2,128]{1,0:T(2,128)} %bitcast.9, s32[2,128]{1,0:T(2,128)} %bitcast.11, s32[2,128]{1,0:T(2,128)} %bitcast.13, f32[2,128]{1,0:T(2,128)} %bitcast.15, bf16[128,1664]{1,0:T(8,128)(2,1)} %tokens_ref.1, ...), custom_call_target="tpu_custom_call" | custom-call | tf_op jit(solution)/shard_map/prepare/pallas_call | solution.py:204
  2.8 0.4 collective-permute-start
  3.2 2.5 %collective-permute-start.1 = (bf16[16,1664]{1,0:T(8,128)(2,1)}, bf16[16,1664]{1,0:T(8,128)(2,1)S(1)}, u32[]{:S(2)}, u32[]{:S(2)}) collective-permute-start(bf16[16,1664]{1,0:T(8,128)(2,1)} %get-tuple-element.47), channel_id=1, source_target_pairs={{0,16},{8,24},{16,0},{24,8},{1,17},{9,25},{17,1},{25,9},{2,18},{10... | collective-permute-start | bytes 159752 | tf_op jit(solution)/shard_map/ppermute | solution.py:418
  5.7 0.1 collective-permute-start.2
  5.8 3.0 %hold.2 = (bf16[2,1664,1024]{2,1,0:T(8,128)(2,1)S(1)}, f32[8,128]{1,0:T(8,128)S(1)}) custom-call(bf16[2,1664,1024]{2,1,0:T(8,128)(2,1)} %refs_0_.1), custom_call_target="tpu_custom_call" | custom-call | bytes 13631488 | tf_op jit(solution)/shard_map/hold/pallas_call | solution.py:242
  8.9 0.8 %collective-permute-done.2.refs_3_ = bf16[16,1664]{1,0:T(8,128)(2,1)S(1)} collective-permute-done((bf16[16,1664]{1,0:T(8,128)(2,1)}, bf16[16,1664]{1,0:T(8,128)(2,1)S(1)}, u32[]{:S(2)}, u32[]{:S(2)}) %collective-permute-start.2) | collective-permute-done | bytes 53280 | tf_op jit(solution)/shard_map/ppermute | solution.py:418
  9.7 0.2 split.1
  9.9 1.6 %collective-permute-start.3 = (bf16[32,1664]{1,0:T(8,128)(2,1)S(1)}, bf16[32,1664]{1,0:T(8,128)(2,1)S(1)}, u32[]{:S(2)}, u32[]{:S(2)}) collective-permute-start(bf16[32,1664]{1,0:T(8,128)(2,1)S(1)} %get-tuple-element.49.refs_0_), channel_id=1, source_target_pairs={{0,1},{2,4},{4,2},{6,7},{7,6},{5,3},{3,5},{1,0},{8,9},{10,12},{12,... | collective-permute-start | bytes 319496 | tf_op jit(solution)/shard_map/ppermute | solution.py:411
  11.5 1.6 %collective-permute-start.4 = (bf16[32,1664]{1,0:T(8,128)(2,1)S(1)}, bf16[32,1664]{1,0:T(8,128)(2,1)S(1)}, u32[]{:S(2)}, u32[]{:S(2)}) collective-permute-start(bf16[32,1664]{1,0:T(8,128)(2,1)S(1)} %get-tuple-element.50.refs_1_), channel_id=1, source_target_pairs={{0,2},{2,0},{1,3},{3,1},{4,6},{6,4},{5,7},{7,5},{8,10},{10,8},{9,1... | collective-permute-start | bytes 319496 | tf_op jit(solution)/shard_map/ppermute | solution.py:412
  13.1 1.9 %collective-permute-done.3.refs_0_.refs_1_ = bf16[32,1664]{1,0:T(8,128)(2,1)S(1)} collective-permute-done((bf16[32,1664]{1,0:T(8,128)(2,1)S(1)}, bf16[32,1664]{1,0:T(8,128)(2,1)S(1)}, u32[]{:S(2)}, u32[]{:S(2)}) %collective-permute-start.3) | collective-permute-done | bytes 106528 | tf_op jit(solution)/shard_map/ppermute | solution.py:411
  15.0 1.2 %collective-permute-done.4.refs_2_ = bf16[32,1664]{1,0:T(8,128)(2,1)S(1)} collective-permute-done((bf16[32,1664]{1,0:T(8,128)(2,1)S(1)}, bf16[32,1664]{1,0:T(8,128)(2,1)S(1)}, u32[]{:S(2)}, u32[]{:S(2)}) %collective-permute-start.4) | collective-permute-done | bytes 106528 | tf_op jit(solution)/shard_map/ppermute | solution.py:412
  16.3 1.5 %collective-permute-start.5 = (bf16[64,1664]{1,0:T(8,128)(2,1)S(1)}, bf16[64,1664]{1,0:T(8,128)(2,1)S(1)}, u32[]{:S(2)}, u32[]{:S(2)}) collective-permute-start(bf16[64,1664]{1,0:T(8,128)(2,1)S(1)} %pair.2.refs_0_), channel_id=1, source_target_pairs={{0,1},{2,4},{4,2},{6,7},{7,6},{5,3},{3,5},{1,0},{8,9},{10,12},{12,... | collective-permute-start | bytes 638984 | tf_op jit(solution)/shard_map/ppermute | solution.py:411
  17.8 1.6 %collective-permute-start.8 = (bf16[64,1664]{1,0:T(8,128)(2,1)S(1)}, bf16[64,1664]{1,0:T(8,128)(2,1)S(1)}, u32[]{:S(2)}, u32[]{:S(2)}) collective-permute-start(bf16[64,1664]{1,0:T(8,128)(2,1)S(1)} %pair.3.refs_1_.refs_0_), channel_id=1, source_target_pairs={{0,2},{2,0},{1,3},{3,1},{4,6},{6,4},{5,7},{7,5},{8,10},{10,8},{9,1... | collective-permute-start | bytes 638984 | tf_op jit(solution)/shard_map/ppermute | solution.py:412
  19.4 3.0 %hold.3 = (bf16[2,1024,1664]{2,1,0:T(8,128)(2,1)S(1)}, f32[8,128]{1,0:T(8,128)S(1)}) custom-call(bf16[64,1664]{1,0:T(8,128)(2,1)S(1)} %pair.2.refs_0_, bf16[64,1664]{1,0:T(8,128)(2,1)S(1)} %pair.3.refs_1_.refs_0_, bf16[2,1024,1664]{2,1,0:T(8,128)(2,1)} %refs_2_.1), custom_call_target="tpu_custom_call" | custom-call | bytes 13631488 | tf_op jit(solution)/shard_map/hold/pallas_call | solution.py:242
  22.5 1.7 %collective-permute-start.6 = (bf16[64,1664]{1,0:T(8,128)(2,1)S(1)}, bf16[64,1664]{1,0:T(8,128)(2,1)S(1)}, u32[]{:S(2)}, u32[]{:S(2)}) collective-permute-start(bf16[64,1664]{1,0:T(8,128)(2,1)S(1)} %pass.1.refs_1_), channel_id=1, source_target_pairs={{0,2},{2,0},{1,3},{3,1},{4,6},{6,4},{5,7},{7,5},{8,10},{10,8},{9,1... | collective-permute-start | bytes 638984 | tf_op jit(solution)/shard_map/ppermute | solution.py:412
  24.2 1.5 %collective-permute-start.9 = (bf16[64,1664]{1,0:T(8,128)(2,1)S(1)}, bf16[64,1664]{1,0:T(8,128)(2,1)S(1)}, u32[]{:S(2)}, u32[]{:S(2)}) collective-permute-start(bf16[64,1664]{1,0:T(8,128)(2,1)S(1)} %collective-permute-done.8.refs_1_), channel_id=1, source_target_pairs={{0,1},{2,4},{4,2},{6,7},{7,6},{5,3},{3,5},{1,0},{8,9},{10,12},{12,... | collective-permute-start | bytes 638984 | tf_op jit(solution)/shard_map/ppermute | solution.py:411
  25.7 2.9 %collective-permute-done.6.refs_2_ = bf16[64,1664]{1,0:T(8,128)(2,1)S(1)} collective-permute-done((bf16[64,1664]{1,0:T(8,128)(2,1)S(1)}, bf16[64,1664]{1,0:T(8,128)(2,1)S(1)}, u32[]{:S(2)}, u32[]{:S(2)}) %collective-permute-start.6) | collective-permute-done | bytes 213024 | tf_op jit(solution)/shard_map/ppermute | solution.py:412
  28.6 1.6 %collective-permute-start.7 = (bf16[64,1664]{1,0:T(8,128)(2,1)S(1)}, bf16[64,1664]{1,0:T(8,128)(2,1)S(1)}, u32[]{:S(2)}, u32[]{:S(2)}) collective-permute-start(bf16[64,1664]{1,0:T(8,128)(2,1)S(1)} %collective-permute-done.6.refs_2_), channel_id=1, source_target_pairs={{0,1},{2,4},{4,2},{6,7},{7,6},{5,3},{3,5},{1,0},{8,9},{10,12},{12,... | collective-permute-start | bytes 638984 | tf_op jit(solution)/shard_map/ppermute | solution.py:411
  30.1 0.8 %collective-permute-done.9.refs_2_ = bf16[64,1664]{1,0:T(8,128)(2,1)S(1)} collective-permute-done((bf16[64,1664]{1,0:T(8,128)(2,1)S(1)}, bf16[64,1664]{1,0:T(8,128)(2,1)S(1)}, u32[]{:S(2)}, u32[]{:S(2)}) %collective-permute-start.9) | collective-permute-done | bytes 213024 | tf_op jit(solution)/shard_map/ppermute | solution.py:411
  30.9 2.6 %collective-permute-start.10 = (bf16[64,1664]{1,0:T(8,128)(2,1)S(1)}, bf16[64,1664]{1,0:T(8,128)(2,1)S(1)}, u32[]{:S(2)}, u32[]{:S(2)}) collective-permute-start(bf16[64,1664]{1,0:T(8,128)(2,1)S(1)} %collective-permute-done.9.refs_2_), channel_id=1, source_target_pairs={{0,2},{2,0},{1,3},{3,1},{4,6},{6,4},{5,7},{7,5},{8,10},{10,8},{9,1... | collective-permute-start | bytes 638984 | tf_op jit(solution)/shard_map/ppermute | solution.py:412
  33.6 1.0 %collective-permute-done.7.refs_3_ = bf16[64,1664]{1,0:T(8,128)(2,1)S(1)} collective-permute-done((bf16[64,1664]{1,0:T(8,128)(2,1)S(1)}, bf16[64,1664]{1,0:T(8,128)(2,1)S(1)}, u32[]{:S(2)}, u32[]{:S(2)}) %collective-permute-start.7) | collective-permute-done | bytes 213024 | tf_op jit(solution)/shard_map/ppermute | solution.py:411
  34.6 0.1 sort_rows.1.refs_2_
  34.7 1.6 %fusion.3 = (f32[2,128,1024]{2,1,0:T(8,128)S(1)}, bf16[2,128,1024]{2,1,0:T(8,128)(2,1)S(1)}) fusion(bf16[2,128,1664]{2,1,0:T(8,128)(2,1)S(1)} %sort_rows.1.refs_2_, bf16[2,1664,1024]{2,1,0:T(8,128)(2,1)S(1)} %get-tuple-element.52.refs_5_), kind=kOutput, calls=%fused_computation.5 | convolution fusion | flops 875298816 | bytes 9240576 | tf_op jit(solution)/shard_map/xmd,xdf->xmf/dot_general | solution.py:452
  36.3 1.2 %convolution_convert_fusion.in_ref = bf16[2,128,1664]{2,1,0:T(8,128)(2,1)S(1)} fusion(bf16[2,128,1024]{2,1,0:T(8,128)(2,1)S(1)} %get-tuple-element.84.refs_2_.refs_1_, bf16[2,1024,1664]{2,1,0:T(8,128)(2,1)S(1)} %get-tuple-element.53.refs_6_), kind=kOutput, calls=%fused_computation | convolution fusion | flops 872841216 | bytes 8192000 | tf_op jit(solution)/shard_map/xmf,xfd->xmd/dot_general | solution.py:454
  37.4 0.1 unsort_rows.2
  37.5 1.6 %collective-permute-start.11 = (bf16[64,1664]{1,0:T(8,128)(2,1)S(1)}, bf16[64,1664]{1,0:T(8,128)(2,1)S(1)}, u32[]{:S(2)}, u32[]{:S(2)}) collective-permute-start(bf16[64,1664]{1,0:T(8,128)(2,1)S(1)} %get-tuple-element.54.after_ref), channel_id=1, source_target_pairs={{0,1},{2,4},{4,2},{6,7},{7,6},{5,3},{3,5},{1,0},{8,9},{10,12},{12,... | collective-permute-start | bytes 638984 | tf_op jit(solution)/shard_map/ppermute | solution.py:411
  39.1 4.0 %backward.1 = (bf16[2,128,1664]{2,1,0:T(8,128)(2,1)S(1)}, bf16[2,128,1024]{2,1,0:T(8,128)(2,1)S(1)}, bf16[2,128,1664]{2,1,0:T(8,128)(2,1)S(1)}) custom-call(bf16[64,1664]{1,0:T(8,128)(2,1)S(1)} %get-tuple-element.54.after_ref, bf16[64,1664]{1,0:T(8,128)(2,1)S(1)} %pair.3.refs_1_.refs_0_, bf16[64,1664]{1,0:T(8,128)(2,1)S(1)} %collective-permute-done.8.refs_1_, ...), custom_call_target="tpu_custom_call" | custom-call | flops 1744830464 | bytes 1703936 | tf_op jit(solution)/shard_map/backward/pallas_call | solution.py:347
  43.2 0.1 unsort_rows.3
  43.2 0.6 collective-permute-start.12
  43.9 2.1 %collective-permute-start.15 = (bf16[64,1664]{1,0:T(8,128)(2,1)S(1)}, bf16[64,1664]{1,0:T(8,128)(2,1)S(1)}, u32[]{:S(2)}, u32[]{:S(2)}) collective-permute-start(bf16[64,1664]{1,0:T(8,128)(2,1)S(1)} %add.19.refs_1_), channel_id=1, source_target_pairs={{0,2},{2,0},{1,3},{3,1},{4,6},{6,4},{5,7},{7,5},{8,10},{10,8},{9,1... | collective-permute-start | bytes 638984 | tf_op jit(solution)/shard_map/ppermute | solution.py:412
  46.0 3.2 %w_out_grad_kernel.2 = (f32[2,1024,1664]{2,1,0:T(8,128)}, f32[8,128]{1,0:T(8,128)S(1)}) custom-call(bf16[64,1664]{1,0:T(8,128)(2,1)S(1)} %get-tuple-element.57.refs_0_, bf16[64,1664]{1,0:T(8,128)(2,1)S(1)} %add.19.refs_1_, bf16[2,128,1024]{2,1,0:T(8,128)(2,1)S(1)} %get-tuple-element.84.refs_2_.refs_1_, ...), custom_call_target="tpu_custom_call" | custom-call | flops 436207616 | bytes 6815744 | tf_op jit(solution)/shard_map/w_out_grad_kernel/pallas_call | solution.py:264
  49.2 1.6 %collective-permute-start.13 = (bf16[64,1664]{1,0:T(8,128)(2,1)S(1)}, bf16[64,1664]{1,0:T(8,128)(2,1)S(1)}, u32[]{:S(2)}, u32[]{:S(2)}) collective-permute-start(bf16[64,1664]{1,0:T(8,128)(2,1)S(1)} %add.20), channel_id=1, source_target_pairs={{0,2},{2,0},{1,3},{3,1},{4,6},{6,4},{5,7},{7,5},{8,10},{10,8},{9,1... | collective-permute-start | bytes 638984 | tf_op jit(solution)/shard_map/ppermute | solution.py:412
  50.9 2.9 %collective-permute-start.16 = (bf16[64,1664]{1,0:T(8,128)(2,1)S(1)}, bf16[64,1664]{1,0:T(8,128)(2,1)S(1)}, u32[]{:S(2)}, u32[]{:S(2)}) collective-permute-start(bf16[64,1664]{1,0:T(8,128)(2,1)S(1)} %add.22), channel_id=1, source_target_pairs={{0,1},{2,4},{4,2},{6,7},{7,6},{5,3},{3,5},{1,0},{8,9},{10,12},{12,... | collective-permute-start | bytes 638984 | tf_op jit(solution)/shard_map/ppermute | solution.py:411
  53.8 1.3 %collective-permute-done.13.refs_1_ = bf16[64,1664]{1,0:T(8,128)(2,1)S(1)} collective-permute-done((bf16[64,1664]{1,0:T(8,128)(2,1)S(1)}, bf16[64,1664]{1,0:T(8,128)(2,1)S(1)}, u32[]{:S(2)}, u32[]{:S(2)}) %collective-permute-start.13) | collective-permute-done | bytes 213024 | tf_op jit(solution)/shard_map/ppermute | solution.py:412
  55.2 1.2 %collective-permute-start.14 = (bf16[64,1664]{1,0:T(8,128)(2,1)S(1)}, bf16[64,1664]{1,0:T(8,128)(2,1)S(1)}, u32[]{:S(2)}, u32[]{:S(2)}) collective-permute-start(bf16[64,1664]{1,0:T(8,128)(2,1)S(1)} %add.21.refs_0_), channel_id=1, source_target_pairs={{0,1},{2,4},{4,2},{6,7},{7,6},{5,3},{3,5},{1,0},{8,9},{10,12},{12,... | collective-permute-start | bytes 638984 | tf_op jit(solution)/shard_map/ppermute | solution.py:411
  56.4 3.2 %w_in_grad_kernel.2 = (f32[2,1664,1024]{2,1,0:T(8,128)}, f32[8,128]{1,0:T(8,128)S(1)}) custom-call(bf16[64,1664]{1,0:T(8,128)(2,1)S(1)} %add.21.refs_0_, bf16[2,128,1024]{2,1,0:T(8,128)(2,1)S(1)} %get-tuple-element.62.refs_1_, bf16[2,128,1664]{2,1,0:T(8,128)(2,1)S(1)} %sort_rows.1.refs_2_), custom_call_target="tpu_custom_call" | custom-call | flops 436207616 | bytes 6815744 | tf_op jit(solution)/shard_map/w_in_grad_kernel/pallas_call | solution.py:264
  59.6 0.3 collective-permute-done.16.refs_2_
  60.0 1.3 %collective-permute-start.17 = (bf16[32,1664]{1,0:T(8,128)(2,1)S(1)}, bf16[32,1664]{1,0:T(8,128)(2,1)S(1)}, u32[]{:S(2)}, u32[]{:S(2)}) collective-permute-start(bf16[32,1664]{1,0:T(8,128)(2,1)S(1)} %get-tuple-element.71), channel_id=1, source_target_pairs={{0,2},{2,0},{1,3},{3,1},{4,6},{6,4},{5,7},{7,5},{8,10},{10,8},{9,1... | collective-permute-start | bytes 319496 | tf_op jit(solution)/shard_map/ppermute | solution.py:412
  61.3 0.9 %collective-permute-done.14.refs_2_ = bf16[64,1664]{1,0:T(8,128)(2,1)S(1)} collective-permute-done((bf16[64,1664]{1,0:T(8,128)(2,1)S(1)}, bf16[64,1664]{1,0:T(8,128)(2,1)S(1)}, u32[]{:S(2)}, u32[]{:S(2)}) %collective-permute-start.14) | collective-permute-done | bytes 213024 | tf_op jit(solution)/shard_map/ppermute | solution.py:411
  62.3 1.3 %collective-permute-start.18 = (bf16[32,1664]{1,0:T(8,128)(2,1)S(1)}, bf16[32,1664]{1,0:T(8,128)(2,1)S(1)}, u32[]{:S(2)}, u32[]{:S(2)}) collective-permute-start(bf16[32,1664]{1,0:T(8,128)(2,1)S(1)} %get-tuple-element.65.refs_0_), channel_id=1, source_target_pairs={{0,2},{2,0},{1,3},{3,1},{4,6},{6,4},{5,7},{7,5},{8,10},{10,8},{9,1... | collective-permute-start | bytes 319496 | tf_op jit(solution)/shard_map/ppermute | solution.py:412
  63.6 3.2 %w_out_grad_kernel.3 = (f32[2,1024,1664]{2,1,0:T(8,128)}, f32[8,128]{1,0:T(8,128)S(1)}) custom-call(bf16[32,1664]{1,0:T(8,128)(2,1)S(1)} %get-tuple-element.65.refs_0_, bf16[2,128,1024]{2,1,0:T(8,128)(2,1)S(1)} %get-tuple-element.84.refs_2_.refs_1_, bf16[2,128,1664]{2,1,0:T(8,128)(2,1)S(1)} %get-tuple-element.59.refs_3_.refs_2_, ...), custom_call_target="tpu_custom_call", output_to_operand_aliasing={{0}: (3, {})} | custom-call | flops 436207616 | bytes 6815744 | tf_op jit(solution)/shard_map/w_out_grad_kernel/pallas_call | solution.py:264
  66.8 0.2 collective-permute-done.18.refs_4_
  67.1 0.2 join.1
  67.3 0.1 collective-permute-start.19
  67.4 1.4 %collective-permute-start.20 = (bf16[16,1664]{1,0:T(8,128)(2,1)S(1)}, bf16[16,1664]{1,0:T(8,128)(2,1)S(1)}, u32[]{:S(2)}, u32[]{:S(2)}) collective-permute-start(bf16[16,1664]{1,0:T(8,128)(2,1)S(1)} %get-tuple-element.75), channel_id=1, source_target_pairs={{0,16},{8,24},{16,0},{24,8},{1,17},{9,25},{17,1},{25,9},{2,18},{10... | collective-permute-start | bytes 159752 | tf_op jit(solution)/shard_map/ppermute | solution.py:418
  68.8 0.4 collective-permute-start.21
  69.3 3.8 %w_in_grad_kernel.3 = (f32[2,1664,1024]{2,1,0:T(8,128)}, f32[8,128]{1,0:T(8,128)}) custom-call(bf16[16,1664]{1,0:T(8,128)(2,1)S(1)} %get-tuple-element.73.refs_0_, bf16[2,128,1024]{2,1,0:T(8,128)(2,1)S(1)} %get-tuple-element.62.refs_1_, bf16[2,128,1664]{2,1,0:T(8,128)(2,1)S(1)} %sort_rows.1.refs_2_, ...), custom_call_target="tpu_custom_call", output_to_operand_aliasing={{0}: (3, {})} | custom-call | flops 436207616 | bytes 6815744 | tf_op jit(solution)/shard_map/w_in_grad_kernel/pallas_call | solution.py:264
  73.1 1.5 %finish.1 = (bf16[128,1664]{1,0:T(8,128)(2,1)}, bf16[128,1664]{1,0:T(8,128)(2,1)}, f32[2,128]{1,0:T(2,128)}) custom-call(s32[2,128]{1,0:T(2,128)S(1)} %bitcast.10, s32[2,128]{1,0:T(2,128)S(1)} %bitcast.12, s32[2,128]{1,0:T(2,128)S(1)} %bitcast.14, f32[2,128]{1,0:T(2,128)S(1)} %bitcast.16, bf16[128,1664]{1,0:T(8,128)(2,1)S(1)} %copy-done, ...), custom_call_target="tpu_custom_call" | custom-call | tf_op jit(solution)/shard_map/finish/pallas_call | solution.py:215
  (31 shorter events, 0.5 us)
Async XLA Ops:
  2.8 6.1 %collective-permute-start = (bf16[16,1664]{1,0:T(8,128)(2,1)}, bf16[16,1664]{1,0:T(8,128)(2,1)S(1)}, u32[]{:S(2)}, u32[]{:S(2)}) collective-permute-start(bf16[16,1664]{1,0:T(8,128)(2,1)} %get-tuple-element.46), channel_id=1, source_target_pairs={{0,8},{8,0},{16,24},{24,16},{1,9},{9,1},{17,25},{25,17},{2,10},{10... | collective-permute-start | bytes 159752 | tf_op jit(solution)/shard_map/ppermute | solution.py:418
  3.2 5.7 %collective-permute-start.1 = (bf16[16,1664]{1,0:T(8,128)(2,1)}, bf16[16,1664]{1,0:T(8,128)(2,1)S(1)}, u32[]{:S(2)}, u32[]{:S(2)}) collective-permute-start(bf16[16,1664]{1,0:T(8,128)(2,1)} %get-tuple-element.47), channel_id=1, source_target_pairs={{0,16},{8,24},{16,0},{24,8},{1,17},{9,25},{17,1},{25,9},{2,18},{10... | collective-permute-start | bytes 159752 | tf_op jit(solution)/shard_map/ppermute | solution.py:418
  5.7 4.0 %collective-permute-start.2 = (bf16[16,1664]{1,0:T(8,128)(2,1)}, bf16[16,1664]{1,0:T(8,128)(2,1)S(1)}, u32[]{:S(2)}, u32[]{:S(2)}) collective-permute-start(bf16[16,1664]{1,0:T(8,128)(2,1)} %get-tuple-element.48), channel_id=1, source_target_pairs={{0,24},{8,16},{16,8},{24,0},{1,25},{9,17},{17,9},{25,1},{2,26},{10... | collective-permute-start | bytes 159752 | tf_op jit(solution)/shard_map/ppermute | solution.py:418
  9.9 5.1 %collective-permute-start.3 = (bf16[32,1664]{1,0:T(8,128)(2,1)S(1)}, bf16[32,1664]{1,0:T(8,128)(2,1)S(1)}, u32[]{:S(2)}, u32[]{:S(2)}) collective-permute-start(bf16[32,1664]{1,0:T(8,128)(2,1)S(1)} %get-tuple-element.49.refs_0_), channel_id=1, source_target_pairs={{0,1},{2,4},{4,2},{6,7},{7,6},{5,3},{3,5},{1,0},{8,9},{10,12},{12,... | collective-permute-start | bytes 319496 | tf_op jit(solution)/shard_map/ppermute | solution.py:411
  11.5 4.7 %collective-permute-start.4 = (bf16[32,1664]{1,0:T(8,128)(2,1)S(1)}, bf16[32,1664]{1,0:T(8,128)(2,1)S(1)}, u32[]{:S(2)}, u32[]{:S(2)}) collective-permute-start(bf16[32,1664]{1,0:T(8,128)(2,1)S(1)} %get-tuple-element.50.refs_1_), channel_id=1, source_target_pairs={{0,2},{2,0},{1,3},{3,1},{4,6},{6,4},{5,7},{7,5},{8,10},{10,8},{9,1... | collective-permute-start | bytes 319496 | tf_op jit(solution)/shard_map/ppermute | solution.py:412
  16.3 6.2 %collective-permute-start.5 = (bf16[64,1664]{1,0:T(8,128)(2,1)S(1)}, bf16[64,1664]{1,0:T(8,128)(2,1)S(1)}, u32[]{:S(2)}, u32[]{:S(2)}) collective-permute-start(bf16[64,1664]{1,0:T(8,128)(2,1)S(1)} %pair.2.refs_0_), channel_id=1, source_target_pairs={{0,1},{2,4},{4,2},{6,7},{7,6},{5,3},{3,5},{1,0},{8,9},{10,12},{12,... | collective-permute-start | bytes 638984 | tf_op jit(solution)/shard_map/ppermute | solution.py:411
  17.8 6.4 %collective-permute-start.8 = (bf16[64,1664]{1,0:T(8,128)(2,1)S(1)}, bf16[64,1664]{1,0:T(8,128)(2,1)S(1)}, u32[]{:S(2)}, u32[]{:S(2)}) collective-permute-start(bf16[64,1664]{1,0:T(8,128)(2,1)S(1)} %pair.3.refs_1_.refs_0_), channel_id=1, source_target_pairs={{0,2},{2,0},{1,3},{3,1},{4,6},{6,4},{5,7},{7,5},{8,10},{10,8},{9,1... | collective-permute-start | bytes 638984 | tf_op jit(solution)/shard_map/ppermute | solution.py:412
  22.5 6.1 %collective-permute-start.6 = (bf16[64,1664]{1,0:T(8,128)(2,1)S(1)}, bf16[64,1664]{1,0:T(8,128)(2,1)S(1)}, u32[]{:S(2)}, u32[]{:S(2)}) collective-permute-start(bf16[64,1664]{1,0:T(8,128)(2,1)S(1)} %pass.1.refs_1_), channel_id=1, source_target_pairs={{0,2},{2,0},{1,3},{3,1},{4,6},{6,4},{5,7},{7,5},{8,10},{10,8},{9,1... | collective-permute-start | bytes 638984 | tf_op jit(solution)/shard_map/ppermute | solution.py:412
  24.2 6.7 %collective-permute-start.9 = (bf16[64,1664]{1,0:T(8,128)(2,1)S(1)}, bf16[64,1664]{1,0:T(8,128)(2,1)S(1)}, u32[]{:S(2)}, u32[]{:S(2)}) collective-permute-start(bf16[64,1664]{1,0:T(8,128)(2,1)S(1)} %collective-permute-done.8.refs_1_), channel_id=1, source_target_pairs={{0,1},{2,4},{4,2},{6,7},{7,6},{5,3},{3,5},{1,0},{8,9},{10,12},{12,... | collective-permute-start | bytes 638984 | tf_op jit(solution)/shard_map/ppermute | solution.py:411
  28.6 6.0 %collective-permute-start.7 = (bf16[64,1664]{1,0:T(8,128)(2,1)S(1)}, bf16[64,1664]{1,0:T(8,128)(2,1)S(1)}, u32[]{:S(2)}, u32[]{:S(2)}) collective-permute-start(bf16[64,1664]{1,0:T(8,128)(2,1)S(1)} %collective-permute-done.6.refs_2_), channel_id=1, source_target_pairs={{0,1},{2,4},{4,2},{6,7},{7,6},{5,3},{3,5},{1,0},{8,9},{10,12},{12,... | collective-permute-start | bytes 638984 | tf_op jit(solution)/shard_map/ppermute | solution.py:411
  30.9 8.2 %collective-permute-start.10 = (bf16[64,1664]{1,0:T(8,128)(2,1)S(1)}, bf16[64,1664]{1,0:T(8,128)(2,1)S(1)}, u32[]{:S(2)}, u32[]{:S(2)}) collective-permute-start(bf16[64,1664]{1,0:T(8,128)(2,1)S(1)} %collective-permute-done.9.refs_2_), channel_id=1, source_target_pairs={{0,2},{2,0},{1,3},{3,1},{4,6},{6,4},{5,7},{7,5},{8,10},{10,8},{9,1... | collective-permute-start | bytes 638984 | tf_op jit(solution)/shard_map/ppermute | solution.py:412
  37.5 6.3 %collective-permute-start.11 = (bf16[64,1664]{1,0:T(8,128)(2,1)S(1)}, bf16[64,1664]{1,0:T(8,128)(2,1)S(1)}, u32[]{:S(2)}, u32[]{:S(2)}) collective-permute-start(bf16[64,1664]{1,0:T(8,128)(2,1)S(1)} %get-tuple-element.54.after_ref), channel_id=1, source_target_pairs={{0,1},{2,4},{4,2},{6,7},{7,6},{5,3},{3,5},{1,0},{8,9},{10,12},{12,... | collective-permute-start | bytes 638984 | tf_op jit(solution)/shard_map/ppermute | solution.py:411
  43.2 6.0 %collective-permute-start.12 = (bf16[64,1664]{1,0:T(8,128)(2,1)S(1)}, bf16[64,1664]{1,0:T(8,128)(2,1)S(1)}, u32[]{:S(2)}, u32[]{:S(2)}) collective-permute-start(bf16[64,1664]{1,0:T(8,128)(2,1)S(1)} %get-tuple-element.57.refs_0_), channel_id=1, source_target_pairs={{0,1},{2,4},{4,2},{6,7},{7,6},{5,3},{3,5},{1,0},{8,9},{10,12},{12,... | collective-permute-start | bytes 638984 | tf_op jit(solution)/shard_map/ppermute | solution.py:411
  43.9 7.0 %collective-permute-start.15 = (bf16[64,1664]{1,0:T(8,128)(2,1)S(1)}, bf16[64,1664]{1,0:T(8,128)(2,1)S(1)}, u32[]{:S(2)}, u32[]{:S(2)}) collective-permute-start(bf16[64,1664]{1,0:T(8,128)(2,1)S(1)} %add.19.refs_1_), channel_id=1, source_target_pairs={{0,2},{2,0},{1,3},{3,1},{4,6},{6,4},{5,7},{7,5},{8,10},{10,8},{9,1... | collective-permute-start | bytes 638984 | tf_op jit(solution)/shard_map/ppermute | solution.py:412
  49.2 5.9 %collective-permute-start.13 = (bf16[64,1664]{1,0:T(8,128)(2,1)S(1)}, bf16[64,1664]{1,0:T(8,128)(2,1)S(1)}, u32[]{:S(2)}, u32[]{:S(2)}) collective-permute-start(bf16[64,1664]{1,0:T(8,128)(2,1)S(1)} %add.20), channel_id=1, source_target_pairs={{0,2},{2,0},{1,3},{3,1},{4,6},{6,4},{5,7},{7,5},{8,10},{10,8},{9,1... | collective-permute-start | bytes 638984 | tf_op jit(solution)/shard_map/ppermute | solution.py:412
  50.9 9.0 %collective-permute-start.16 = (bf16[64,1664]{1,0:T(8,128)(2,1)S(1)}, bf16[64,1664]{1,0:T(8,128)(2,1)S(1)}, u32[]{:S(2)}, u32[]{:S(2)}) collective-permute-start(bf16[64,1664]{1,0:T(8,128)(2,1)S(1)} %add.22), channel_id=1, source_target_pairs={{0,1},{2,4},{4,2},{6,7},{7,6},{5,3},{3,5},{1,0},{8,9},{10,12},{12,... | collective-permute-start | bytes 638984 | tf_op jit(solution)/shard_map/ppermute | solution.py:411
  55.2 7.0 %collective-permute-start.14 = (bf16[64,1664]{1,0:T(8,128)(2,1)S(1)}, bf16[64,1664]{1,0:T(8,128)(2,1)S(1)}, u32[]{:S(2)}, u32[]{:S(2)}) collective-permute-start(bf16[64,1664]{1,0:T(8,128)(2,1)S(1)} %add.21.refs_0_), channel_id=1, source_target_pairs={{0,1},{2,4},{4,2},{6,7},{7,6},{5,3},{3,5},{1,0},{8,9},{10,12},{12,... | collective-permute-start | bytes 638984 | tf_op jit(solution)/shard_map/ppermute | solution.py:411
  60.0 6.8 %collective-permute-start.17 = (bf16[32,1664]{1,0:T(8,128)(2,1)S(1)}, bf16[32,1664]{1,0:T(8,128)(2,1)S(1)}, u32[]{:S(2)}, u32[]{:S(2)}) collective-permute-start(bf16[32,1664]{1,0:T(8,128)(2,1)S(1)} %get-tuple-element.71), channel_id=1, source_target_pairs={{0,2},{2,0},{1,3},{3,1},{4,6},{6,4},{5,7},{7,5},{8,10},{10,8},{9,1... | collective-permute-start | bytes 319496 | tf_op jit(solution)/shard_map/ppermute | solution.py:412
  62.3 4.8 %collective-permute-start.18 = (bf16[32,1664]{1,0:T(8,128)(2,1)S(1)}, bf16[32,1664]{1,0:T(8,128)(2,1)S(1)}, u32[]{:S(2)}, u32[]{:S(2)}) collective-permute-start(bf16[32,1664]{1,0:T(8,128)(2,1)S(1)} %get-tuple-element.65.refs_0_), channel_id=1, source_target_pairs={{0,2},{2,0},{1,3},{3,1},{4,6},{6,4},{5,7},{7,5},{8,10},{10,8},{9,1... | collective-permute-start | bytes 319496 | tf_op jit(solution)/shard_map/ppermute | solution.py:412
  67.3 5.8 %collective-permute-start.19 = (bf16[16,1664]{1,0:T(8,128)(2,1)S(1)}, bf16[16,1664]{1,0:T(8,128)(2,1)S(1)}, u32[]{:S(2)}, u32[]{:S(2)}) collective-permute-start(bf16[16,1664]{1,0:T(8,128)(2,1)S(1)} %get-tuple-element.74), channel_id=1, source_target_pairs={{0,8},{8,0},{16,24},{24,16},{1,9},{9,1},{17,25},{25,17},{2,10},{10... | collective-permute-start | bytes 159752 | tf_op jit(solution)/shard_map/ppermute | solution.py:418
  67.4 5.7 %collective-permute-start.20 = (bf16[16,1664]{1,0:T(8,128)(2,1)S(1)}, bf16[16,1664]{1,0:T(8,128)(2,1)S(1)}, u32[]{:S(2)}, u32[]{:S(2)}) collective-permute-start(bf16[16,1664]{1,0:T(8,128)(2,1)S(1)} %get-tuple-element.75), channel_id=1, source_target_pairs={{0,16},{8,24},{16,0},{24,8},{1,17},{9,25},{17,1},{25,9},{2,18},{10... | collective-permute-start | bytes 159752 | tf_op jit(solution)/shard_map/ppermute | solution.py:418
  68.8 4.3 %collective-permute-start.21 = (bf16[16,1664]{1,0:T(8,128)(2,1)S(1)}, bf16[16,1664]{1,0:T(8,128)(2,1)S(1)}, u32[]{:S(2)}, u32[]{:S(2)}) collective-permute-start(bf16[16,1664]{1,0:T(8,128)(2,1)S(1)} %get-tuple-element.76), channel_id=1, source_target_pairs={{0,24},{8,16},{16,8},{24,0},{1,25},{9,17},{17,9},{25,1},{2,26},{10... | collective-permute-start | bytes 159752 | tf_op jit(solution)/shard_map/ppermute | solution.py:418
  69.3 3.8 %copy-start = (bf16[128,1664]{1,0:T(8,128)(2,1)S(1)}, bf16[128,1664]{1,0:T(8,128)(2,1)}, u32[]{:S(2)}) copy-start(bf16[128,1664]{1,0:T(8,128)(2,1)} %out_grad_ref.3) | copy-start | bytes 1277956
  69.3 3.9 %copy-start.1 = (s32[128,2]{0,1:T(2,128)S(1)}, s32[128,2]{0,1:T(2,128)}, u32[]{:S(2)}) copy-start(s32[128,2]{0,1:T(2,128)} %param.9) | copy-start | bytes 3076
  69.3 3.9 %copy-start.2 = (s32[128,2]{0,1:T(2,128)S(1)}, s32[128,2]{0,1:T(2,128)}, u32[]{:S(2)}) copy-start(s32[128,2]{0,1:T(2,128)} %param.10) | copy-start | bytes 3076
  69.3 3.9 %copy-start.3 = (s32[128,2]{0,1:T(2,128)S(1)}, s32[128,2]{0,1:T(2,128)}, u32[]{:S(2)}) copy-start(s32[128,2]{0,1:T(2,128)} %param.11) | copy-start | bytes 3076
  69.3 3.9 %copy-start.4 = (f32[128,2]{0,1:T(2,128)S(1)}, f32[128,2]{0,1:T(2,128)}, u32[]{:S(2)}) copy-start(f32[128,2]{0,1:T(2,128)} %param.12) | copy-start | bytes 3076
